TPU v7x, 128 devices: a whole 4x4x4 slice. The times are simulated.
128 devices in a mesh: dp: 8 (over z_hi, y), seq: 16 (over z_lo, x, core).
Axes of the slice: x: 4, y: 4, z: 4 (z_hi: 2, z_lo: 2; z = z_hi * 2 + z_lo), core: 2. Of those that a mesh axis runs over, the one named last changes fastest.
Arguments:
- queries: bfloat16 [8, 2048, 2048], P('dp', 'seq'), may hold values from -10 to 10
- keys: bfloat16 [8, 2048, 2048], P('dp', 'seq'), may hold values from -10 to 10
- values: bfloat16 [8, 2048, 2048], P('dp', 'seq'), may hold values from -6 to 6
- out_weight: bfloat16 [2048, 2048], replicated, may hold values from -0.125 to 0.125
- out_grad: bfloat16 [8, 2048, 2048], P('dp', 'seq'), may hold values from -6 to 6
Outputs:
- layer_out: bfloat16 [8, 2048, 2048], P('dp', 'seq')
- grad_queries: bfloat16 [8, 2048, 2048], P('dp', 'seq')
- grad_keys: bfloat16 [8, 2048, 2048], P('dp', 'seq')
- grad_values: bfloat16 [8, 2048, 2048], P('dp', 'seq')
- grad_weight: float32 [2048, 2048], P('seq')
All inputs are finite; a program needn't handle non-finite values.
Results may differ from a plain program's by a relative error of at most 0.035.
Values may be sent and summed in bfloat16 or wider, within the bound.
No kernel may reach another device: no remote copies, remote signals or barrier semaphores. Data moves between devices by JAX's collectives and lax.ppermute only.
A program may use at most 192 MiB of HBM per device.

v0:
```python
import jax
import jax.numpy as jnp
from jax import lax
from jax.sharding import PartitionSpec as P

HEAD_DIM = 128


def probabilities(query_block, key_prefix, first_row, factor):
    scores = (
        jnp.einsum("qhd,khd->hqk", query_block, key_prefix, preferred_element_type=jnp.float32)
        * factor
    )
    row_ids = first_row + lax.broadcasted_iota(jnp.int32, scores.shape, 1)
    col_ids = lax.broadcasted_iota(jnp.int32, scores.shape, 2)
    visible = row_ids >= col_ids
    scores = jnp.where(visible, scores, -1e30)
    peak = jnp.max(scores, axis=2, keepdims=True)
    weights = jnp.where(visible, jnp.exp(scores - peak), 0.0)
    return weights / jnp.sum(weights, axis=2, keepdims=True)


def product_first(left, right):
    return lax.dot_general(
        left, right, (((0,), (0,)), ((), ())), preferred_element_type=jnp.float32
    )


def product_last(left, right):
    return lax.dot_general(
        left, right, (((1,), (1,)), ((), ())), preferred_element_type=jnp.float32
    )


def on_device(queries, keys, values, out_weight, out_grad):
    parts_seq = lax.axis_size("seq")
    tokens_dev = queries.shape[1]
    width_all = queries.shape[2]
    factor = HEAD_DIM ** (-0.5)
    q_heads, k_heads, v_heads = (
        lax.all_to_all(
            queries.reshape(tokens_dev, width_all), "seq", split_axis=1, concat_axis=0, tiled=True
        ),
        lax.all_to_all(
            keys.reshape(tokens_dev, width_all), "seq", split_axis=1, concat_axis=0, tiled=True
        ),
        lax.all_to_all(
            values.reshape(tokens_dev, width_all), "seq", split_axis=1, concat_axis=0, tiled=True
        ),
    )
    seq_length = q_heads.shape[0]
    local_width = q_heads.shape[1]
    head_count = local_width // HEAD_DIM
    shape_three = (seq_length, head_count, HEAD_DIM)
    q_three = q_heads.reshape(shape_three)
    k_three = k_heads.reshape(shape_three)
    v_three = v_heads.reshape(shape_three)
    block_count = max(1, min(8, seq_length // 512))
    block_rows = seq_length // block_count
    outputs = []
    for number in range(block_count):
        start_row = number * block_rows
        end_row = start_row + block_rows
        weights = probabilities(q_three[start_row:end_row], k_three[:end_row], start_row, factor)
        outputs.append(
            jnp.einsum(
                "hqk,khd->qhd",
                weights.astype(jnp.bfloat16),
                v_three[:end_row],
                preferred_element_type=jnp.float32,
            ).astype(jnp.bfloat16)
        )
    o_three = jnp.concatenate(outputs, 0)
    o_heads = o_three.reshape(seq_length, local_width)
    o_tokens = lax.all_to_all(o_heads, "seq", split_axis=0, concat_axis=1, tiled=True)
    layer_out = jnp.dot(o_tokens, out_weight, preferred_element_type=jnp.float32).astype(
        jnp.bfloat16
    )
    grad_tokens = out_grad.reshape(tokens_dev, width_all)
    row_count = width_all // parts_seq
    row_start = lax.axis_index("seq") * row_count
    d_tokens = product_last(grad_tokens, out_weight).astype(jnp.bfloat16)
    d_heads = lax.all_to_all(d_tokens, "seq", split_axis=1, concat_axis=0, tiled=True)
    summed = lax.psum(product_first(o_tokens, grad_tokens), ("dp", "seq"))
    grad_rows = lax.dynamic_slice_in_dim(summed, row_start, row_count, 0)
    d_three = d_heads.reshape(shape_three)
    dk_total = jnp.zeros(shape_three, jnp.float32)
    dv_total = jnp.zeros(shape_three, jnp.float32)
    dq_blocks = []
    for number in range(block_count):
        start_row = number * block_rows
        end_row = start_row + block_rows
        query_block = q_three[start_row:end_row]
        d_block = d_three[start_row:end_row]
        probs_f = probabilities(query_block, k_three[:end_row], start_row, factor)
        probs = probs_f.astype(jnp.bfloat16)
        delta = jnp.sum(
            d_block.astype(jnp.float32) * o_three[start_row:end_row].astype(jnp.float32), axis=2
        )
        d_probs = jnp.einsum(
            "qhd,khd->hqk", d_block, v_three[:end_row], preferred_element_type=jnp.float32
        )
        d_scores = (probs_f * (d_probs - delta.T[:, :, None])).astype(jnp.bfloat16)
        dq_blocks.append(
            (
                jnp.einsum(
                    "hqk,khd->qhd", d_scores, k_three[:end_row], preferred_element_type=jnp.float32
                )
                * factor
            ).astype(jnp.bfloat16)
        )
        dk_total = dk_total.at[:end_row].add(
            jnp.einsum("hqk,qhd->khd", d_scores, query_block, preferred_element_type=jnp.float32)
        )
        dv_total = dv_total.at[:end_row].add(
            jnp.einsum("hqk,qhd->khd", probs, d_block, preferred_element_type=jnp.float32)
        )
    dq_heads = jnp.concatenate(dq_blocks, 0).reshape(seq_length, local_width)
    dk_heads = (dk_total * factor).astype(jnp.bfloat16).reshape(seq_length, local_width)
    dv_heads = dv_total.astype(jnp.bfloat16).reshape(seq_length, local_width)
    grad_q, grad_k, grad_v = (
        lax.all_to_all(dq_heads, "seq", split_axis=0, concat_axis=1, tiled=True),
        lax.all_to_all(dk_heads, "seq", split_axis=0, concat_axis=1, tiled=True),
        lax.all_to_all(dv_heads, "seq", split_axis=0, concat_axis=1, tiled=True),
    )
    return (
        layer_out.reshape(1, tokens_dev, width_all),
        grad_q.reshape(1, tokens_dev, width_all),
        grad_k.reshape(1, tokens_dev, width_all),
        grad_v.reshape(1, tokens_dev, width_all),
        grad_rows,
    )


def solution(mesh):
    return jax.shard_map(
        on_device,
        mesh=mesh,
        in_specs=(
            P("dp", "seq", None),
            P("dp", "seq", None),
            P("dp", "seq", None),
            P(),
            P("dp", "seq", None),
        ),
        out_specs=(
            P("dp", "seq", None),
            P("dp", "seq", None),
            P("dp", "seq", None),
            P("dp", "seq", None),
            P("seq", None),
        ),
        check_vma=False,
    )
```

profile of v0, /device:TPU:2, one launch (start us, length us, event | category | flops | bytes accessed | tf_op | source)
XLA Modules:
  0.0 363.1 jit_solution(924163174271841733)
XLA Ops:
  7.2 1.0 copy-done
  8.2 6.3 %fusion.23 = bf16[16,16,8,128]{3,2,1,0:T(8,128)(2,1)S(1)} fusion(bf16[2048,2048]{1,0:T(8,128)(2,1)} %param.28, bf16[1,128,2048]{2,1,0:T(8,128)(2,1)S(1)} %copy-done), kind=kOutput, calls=%fused_computation.43 | convolution fusion | flops 1074003968 | bytes 9437184 | tf_op jit(solution)/shard_map/dot_general | solution.py:30
  14.5 0.9 copy.68
  15.4 6.2 %all-to-all-start.4 = ((bf16[128,16,128]{2,0,1:T(8,128)(2,1)}), bf16[128,16,128]{2,0,1:T(8,128)(2,1)S(1)}, u32[]{:S(2)}, u32[]{:S(2)}) async-start(bf16[128,16,128]{2,0,1:T(8,128)(2,1)} %bitcast.223), calls=%async_computation.4 | async-start | bytes 1048576 | tf_op jit(solution)/shard_map/all_to_all | solution.py:83
  21.7 1.0 copy.46
  22.7 6.7 %all-to-all-done.4 = bf16[128,16,128]{2,0,1:T(8,128)(2,1)S(1)} async-done(((bf16[128,16,128]{2,0,1:T(8,128)(2,1)}), bf16[128,16,128]{2,0,1:T(8,128)(2,1)S(1)}, u32[]{:S(2)}, u32[]{:S(2)}) %all-to-all-start.4) | async-done | bytes 524320 | tf_op jit(solution)/shard_map/all_to_all | solution.py:83
  29.4 6.6 %all-to-all-start.2 = ((bf16[128,16,128]{0,2,1:T(8,128)(2,1)}), bf16[128,16,128]{0,2,1:T(8,128)(2,1)S(1)}, u32[]{:S(2)}, u32[]{:S(2)}) async-start(bf16[128,16,128]{0,2,1:T(8,128)(2,1)} %bitcast.6), calls=%async_computation.2 | async-start | bytes 1048576 | tf_op jit(solution)/shard_map/all_to_all | solution.py:47
  36.0 1.0 copy.44
  37.0 6.7 %all-to-all-done.2 = bf16[128,16,128]{0,2,1:T(8,128)(2,1)S(1)} async-done(((bf16[128,16,128]{0,2,1:T(8,128)(2,1)}), bf16[128,16,128]{0,2,1:T(8,128)(2,1)S(1)}, u32[]{:S(2)}, u32[]{:S(2)}) %all-to-all-start.2) | async-done | bytes 524320 | tf_op jit(solution)/shard_map/all_to_all | solution.py:47
  43.7 6.7 %all-to-all-start.1 = ((bf16[128,16,128]{0,2,1:T(8,128)(2,1)}), bf16[128,16,128]{0,2,1:T(8,128)(2,1)S(1)}, u32[]{:S(2)}, u32[]{:S(2)}) async-start(bf16[128,16,128]{0,2,1:T(8,128)(2,1)} %bitcast.3), calls=%async_computation.1 | async-start | bytes 1048576 | tf_op jit(solution)/shard_map/all_to_all | solution.py:44
  50.4 1.0 copy.42
  51.4 6.7 %all-to-all-done.1 = bf16[128,16,128]{0,2,1:T(8,128)(2,1)S(1)} async-done(((bf16[128,16,128]{0,2,1:T(8,128)(2,1)}), bf16[128,16,128]{0,2,1:T(8,128)(2,1)S(1)}, u32[]{:S(2)}, u32[]{:S(2)}) %all-to-all-start.1) | async-done | bytes 524320 | tf_op jit(solution)/shard_map/all_to_all | solution.py:44
  58.1 6.7 %all-to-all-start = ((bf16[128,16,128]{0,2,1:T(8,128)(2,1)}), bf16[128,16,128]{0,2,1:T(8,128)(2,1)S(1)}, u32[]{:S(2)}, u32[]{:S(2)}) async-start(bf16[128,16,128]{0,2,1:T(8,128)(2,1)} %bitcast), calls=%async_computation | async-start | bytes 1048576 | tf_op jit(solution)/shard_map/all_to_all | solution.py:41
  65.2 0.8 slice.271
  66.0 1.0 copy.55
  67.0 0.8 slice.270
  67.8 0.7 slice.268
  68.5 0.7 slice.267
  70.5 0.8 fusion.61
  71.3 1.2 all-to-all-done
  73.4 2.0 fusion
  75.4 1.4 fusion.9
  76.8 3.6 fusion.8
  81.0 0.8 fusion.63
  81.8 0.8 fusion.16
  82.6 2.5 fusion.15
  85.1 0.9 copy.50
  87.0 0.7 fusion.25
  87.7 0.8 fusion.24
  88.6 1.7 copy.47
  90.2 1.7 copy.43
  91.9 1.6 copy.45
  93.5 1.3 fusion.64
  95.0 3.5 fusion.53
  100.0 1.0 fusion.56
  101.1 1.0 copy.57
  102.1 14.4 %all_to_all.131 = bf16[16,128,128]{1,2,0:T(8,128)(2,1)S(1)} all-to-all(bf16[16,128,128]{1,2,0:T(8,128)(2,1)} %copy.57), channel_id=1, replica_groups=mesh['dp'=8,'seq'=16] {'seq'}, dimensions={0} | all-to-all | bytes 1048576 | tf_op jit(solution)/shard_map/all_to_all | solution.py:75
  116.5 8.1 %fusion.48 = f32[2048,2048]{1,0:T(8,128)} fusion(bf16[128,2048]{0,1:T(8,128)(2,1)S(1)} %bitcast.224, bf16[1,128,2048]{2,1,0:T(8,128)(2,1)S(1)} %copy-done), kind=kOutput, calls=%fused_computation.85 | convolution fusion | flops 1073741824 | bytes 17825792 | tf_op jit(solution)/shard_map/dot_general | solution.py:24
  124.6 1.7 fusion.21
  130.3 1.0 copy-done.2
  131.5 0.7 multiply_convert_fusion
  132.3 1.3 copy-done.6
  133.6 0.7 fusion.36
  134.3 0.8 pad_maximum_fusion.1
  135.1 7.3 %all-to-all-start.5 = ((bf16[16,128,128]{2,1,0:T(8,128)(2,1)}), bf16[16,128,128]{2,1,0:T(8,128)(2,1)}, u32[]{:S(2)}, u32[]{:S(2)}) async-start(bf16[16,128,128]{2,1,0:T(8,128)(2,1)} %bitcast.242), calls=%async_computation.5 | async-start | bytes 1048576 | tf_op jit(solution)/shard_map/all_to_all | solution.py:122
  142.9 1.7 convolution_bitcast_fusion.6
  145.3 0.7 fusion.5
  146.4 1.0 copy-done.10
  147.3 1.6 fusion.14
  148.9 3.4 all-to-all-done.5
  152.3 6.2 %all-to-all-start.6 = ((bf16[16,128,128]{2,1,0:T(8,128)(2,1)}), bf16[16,128,128]{2,1,0:T(8,128)(2,1)S(1)}, u32[]{:S(2)}, u32[]{:S(2)}) async-start(bf16[16,128,128]{2,1,0:T(8,128)(2,1)} %bitcast.78), calls=%async_computation.6 | async-start | bytes 1048576 | tf_op jit(solution)/shard_map/all_to_all | solution.py:123
  158.5 3.7 %fusion.7 = f32[2048,1,128]{0,2,1:T(8,128)} fusion(f32[2048,1,128]{0,2,1:T(8,128)} %copy-done.10, bf16[512,128]{1,0:T(8,128)(2,1)S(1)} %bitcast.250, f32[512,1536]{1,0:T(8,128)} %fusion.15), kind=kOutput, calls=%fused_computation.19 | convolution fusion | flops 202309632 | bytes 4849664 | tf_op jit(solution)/shard_map/hqk,qhd->khd/dot_general | solution.py:116
  162.2 1.7 fusion.22
  164.0 0.9 copy.62
  164.9 3.8 %all-to-all-done.6 = bf16[16,128,128]{2,1,0:T(8,128)(2,1)S(1)} async-done(((bf16[16,128,128]{2,1,0:T(8,128)(2,1)}), bf16[16,128,128]{2,1,0:T(8,128)(2,1)S(1)}, u32[]{:S(2)}, u32[]{:S(2)}) %all-to-all-start.6) | async-done | bytes 524320 | tf_op jit(solution)/shard_map/all_to_all | solution.py:123
  168.7 6.3 %all-to-all-start.7 = ((bf16[16,128,128]{1,2,0:T(8,128)(2,1)}), bf16[16,128,128]{1,2,0:T(8,128)(2,1)S(1)}, u32[]{:S(2)}, u32[]{:S(2)}) async-start(bf16[16,128,128]{1,2,0:T(8,128)(2,1)} %copy.62), calls=%async_computation.7 | async-start | bytes 1048576 | tf_op jit(solution)/shard_map/all_to_all | solution.py:124
  175.0 1.4 copy.60
  176.4 1.0 reshape.697
  177.8 1.0 reshape.701
  178.8 6.1 %all-to-all-done.7 = bf16[16,128,128]{1,2,0:T(8,128)(2,1)S(1)} async-done(((bf16[16,128,128]{1,2,0:T(8,128)(2,1)}), bf16[16,128,128]{1,2,0:T(8,128)(2,1)S(1)}, u32[]{:S(2)}, u32[]{:S(2)}) %all-to-all-start.7) | async-done | bytes 524320 | tf_op jit(solution)/shard_map/all_to_all | solution.py:124
  184.9 1.0 copy.63
  185.9 5.7 %fusion.17 = bf16[1,128,2048]{2,1,0:T(8,128)(2,1)} fusion(bf16[128,2048]{0,1:T(8,128)(2,1)S(1)} %bitcast.225, bf16[2048,2048]{1,0:T(8,128)(2,1)} %param.28), kind=kOutput, calls=%fused_computation.31 | convolution fusion | flops 1074003968 | bytes 9437184 | tf_op jit(solution)/shard_map/dot_general | solution.py:76
  191.7 162.3 %all-reduce.4.cloned.1.call-done = f32[2048,2048]{1,0:T(8,128)} async-done(((f32[2048,2048]{1,0:T(8,128)}), f32[2048,2048]{1,0:T(8,128)}) %all-reduce.4.cloned.1.call-update) | async-done | bytes 16777232 | tf_op jit(solution)/shard_map/psum | solution.py:84
  354.0 2.3 constant_dynamic-slice_fusion
  (134 shorter events, 11.7 us)
Async XLA Ops:
  7.2 1.1 copy-start
  7.2 14.5 %copy-start.42 = (bf16[1,128,2048]{2,1,0:T(8,128)(2,1)S(1)}, bf16[1,128,2048]{2,1,0:T(8,128)(2,1)}, u32[]{:S(2)}) copy-start(bf16[1,128,2048]{2,1,0:T(8,128)(2,1)} %param.27) | copy-start | bytes 1572868
  14.5 21.5 %copy-start.43 = (bf16[1,128,2048]{2,1,0:T(8,128)(2,1)S(1)}, bf16[1,128,2048]{2,1,0:T(8,128)(2,1)}, u32[]{:S(2)}) copy-start(bf16[1,128,2048]{2,1,0:T(8,128)(2,1)} %param.26) | copy-start | bytes 1572868
  14.5 35.9 %copy-start.44 = (bf16[1,128,2048]{2,1,0:T(8,128)(2,1)S(1)}, bf16[1,128,2048]{2,1,0:T(8,128)(2,1)}, u32[]{:S(2)}) copy-start(bf16[1,128,2048]{2,1,0:T(8,128)(2,1)} %param.25) | copy-start | bytes 1572868
  15.4 13.9 %all-to-all-start.4 = ((bf16[128,16,128]{2,0,1:T(8,128)(2,1)}), bf16[128,16,128]{2,0,1:T(8,128)(2,1)S(1)}, u32[]{:S(2)}, u32[]{:S(2)}) async-start(bf16[128,16,128]{2,0,1:T(8,128)(2,1)} %bitcast.223), calls=%async_computation.4 | async-start | bytes 1048576 | tf_op jit(solution)/shard_map/all_to_all | solution.py:83
  29.4 14.4 %all-to-all-start.2 = ((bf16[128,16,128]{0,2,1:T(8,128)(2,1)}), bf16[128,16,128]{0,2,1:T(8,128)(2,1)S(1)}, u32[]{:S(2)}, u32[]{:S(2)}) async-start(bf16[128,16,128]{0,2,1:T(8,128)(2,1)} %bitcast.6), calls=%async_computation.2 | async-start | bytes 1048576 | tf_op jit(solution)/shard_map/all_to_all | solution.py:47
  43.7 14.4 %all-to-all-start.1 = ((bf16[128,16,128]{0,2,1:T(8,128)(2,1)}), bf16[128,16,128]{0,2,1:T(8,128)(2,1)S(1)}, u32[]{:S(2)}, u32[]{:S(2)}) async-start(bf16[128,16,128]{0,2,1:T(8,128)(2,1)} %bitcast.3), calls=%async_computation.1 | async-start | bytes 1048576 | tf_op jit(solution)/shard_map/all_to_all | solution.py:44
  58.1 14.4 %all-to-all-start = ((bf16[128,16,128]{0,2,1:T(8,128)(2,1)}), bf16[128,16,128]{0,2,1:T(8,128)(2,1)S(1)}, u32[]{:S(2)}, u32[]{:S(2)}) async-start(bf16[128,16,128]{0,2,1:T(8,128)(2,1)} %bitcast), calls=%async_computation | async-start | bytes 1048576 | tf_op jit(solution)/shard_map/all_to_all | solution.py:41
  64.8 289.2 %all-reduce.4.cloned.1.call-start = ((), (), s32[]{:S(2)}) async-start(), calls=%async_computation.8 | async-start | bytes 33554432 | tf_op jit(solution)/shard_map/psum | solution.py:84
  65.1 29.9 %copy-start.13 = (bf16[16,128,128]{2,1,0:T(8,128)(2,1)}, bf16[16,128,128]{2,1,0:T(8,128)(2,1)S(1)}, u32[]{:S(2)}) copy-start(bf16[16,128,128]{2,1,0:T(8,128)(2,1)S(1)} %copy.56) | copy-start | bytes 1572868
  73.4 3.4 copy-start.46
  76.8 3.6 copy-start.31
  76.8 3.9 %copy-start.30 = (bf16[12,128,128]{1,2,0:T(8,128)(2,1)S(1)}, bf16[12,128,128]{1,2,0:T(8,128)(2,1)}, u32[]{:S(2)}) copy-start(bf16[12,128,128]{1,2,0:T(8,128)(2,1)} %slice.270) | copy-start | bytes 1179652
  80.7 1.0 copy-start.37
  81.0 1.6 copy-start.28
  82.6 2.5 copy-start.34
  82.6 3.5 copy-start.33
  86.1 0.8 copy-start.39
  86.3 0.7 copy-start.35
  94.8 5.2 %copy-start.32 = (f32[512,512]{0,1:T(8,128)}, f32[512,512]{0,1:T(8,128)S(1)}, u32[]{:S(2)}) copy-start(f32[512,512]{0,1:T(8,128)S(1)} %get-tuple-element.137) | copy-start | bytes 3145732
  94.8 3.7 %copy-start.4 = (f32[512,1536]{1,0:T(8,128)S(1)}, f32[512,1536]{1,0:T(8,128)}, u32[]{:S(2)}) copy-start(f32[512,1536]{1,0:T(8,128)} %fusion.15) | copy-start | bytes 9437188
  94.8 3.7 %copy-start.21 = (bf16[4,128,128]{2,1,0:T(8,128)(2,1)S(1)}, bf16[4,128,128]{2,1,0:T(8,128)(2,1)}, u32[]{:S(2)}) copy-start(bf16[4,128,128]{2,1,0:T(8,128)(2,1)} %get-tuple-element.124) | copy-start | bytes 393220
  95.0 5.0 %copy-start.51 = (f32[512]{0:T(512)}, f32[512]{0:T(512)S(1)}, u32[]{:S(2)}) copy-start(f32[512]{0:T(512)S(1)} %fusion.45) | copy-start | bytes 6148
  98.5 1.0 copy-start.15
  98.5 1.0 copy-start.24
  98.5 1.5 copy-start.48
  98.5 1.5 copy-start.49
  124.6 1.8 copy-start.45
  124.6 2.6 copy-start.16
  124.6 2.6 copy-start.25
  126.4 0.8 copy-start.17
  126.4 1.2 copy-start.36
  126.4 2.2 copy-start.5
  126.4 2.2 copy-start.22
  127.6 1.0 copy-start.11
  127.6 1.6 copy-start.29
  128.6 2.8 copy-start.2
  128.6 2.9 copy-start.14
  128.6 2.9 copy-start.19
  129.2 1.1 copy-start.8
  131.5 2.1 copy-start.27
  132.3 1.3 copy-start.6
  133.6 8.8 %copy-start.18 = (bf16[512,512]{0,1:T(8,128)(2,1)S(1)}, bf16[512,512]{0,1:T(8,128)(2,1)}, u32[]{:S(2)}) copy-start(bf16[512,512]{0,1:T(8,128)(2,1)} %copy-done.17) | copy-start | bytes 1572868
  133.6 8.8 %copy-start.41 = (bf16[4,128,128]{2,1,0:T(8,128)(2,1)S(1)}, bf16[4,128,128]{2,1,0:T(8,128)(2,1)}, u32[]{:S(2)}) copy-start(bf16[4,128,128]{2,1,0:T(8,128)(2,1)} %copy.43) | copy-start | bytes 393220
  133.6 9.2 %copy-start.50 = (bf16[4,128,128]{2,1,0:T(8,128)(2,1)S(1)}, bf16[4,128,128]{2,1,0:T(8,128)(2,1)}, u32[]{:S(2)}) copy-start(bf16[4,128,128]{2,1,0:T(8,128)(2,1)} %get-tuple-element.122) | copy-start | bytes 393220
  133.6 9.2 %copy-start.52 = (f32[512]{0:T(512)S(1)}, f32[512]{0:T(512)}, u32[]{:S(2)}) copy-start(f32[512]{0:T(512)} %copy-done.51) | copy-start | bytes 6148
  135.1 17.1 %all-to-all-start.5 = ((bf16[16,128,128]{2,1,0:T(8,128)(2,1)}), bf16[16,128,128]{2,1,0:T(8,128)(2,1)}, u32[]{:S(2)}, u32[]{:S(2)}) async-start(bf16[16,128,128]{2,1,0:T(8,128)(2,1)} %bitcast.242), calls=%async_computation.5 | async-start | bytes 1048576 | tf_op jit(solution)/shard_map/all_to_all | solution.py:122
  142.8 1.9 copy-start.12
  142.8 1.9 copy-start.40
  142.8 2.4 copy-start.9
  142.8 2.4 copy-start.38
  144.6 1.4 copy-start.26
  145.2 2.1 copy-start.7
  145.3 2.1 copy-start.47
  146.3 1.0 copy-start.10
  147.3 11.2 %copy-start.23 = (bf16[4,128,128]{2,1,0:T(8,128)(2,1)S(1)}, bf16[4,128,128]{2,1,0:T(8,128)(2,1)}, u32[]{:S(2)}) copy-start(bf16[4,128,128]{2,1,0:T(8,128)(2,1)} %get-tuple-element.124) | copy-start | bytes 393220
  148.9 13.3 %copy-start.20 = (bf16[4,128,128]{2,1,0:T(8,128)(2,1)S(1)}, bf16[4,128,128]{2,1,0:T(8,128)(2,1)}, u32[]{:S(2)}) copy-start(bf16[4,128,128]{2,1,0:T(8,128)(2,1)} %get-tuple-element.123) | copy-start | bytes 393220
  152.3 16.4 %all-to-all-start.6 = ((bf16[16,128,128]{2,1,0:T(8,128)(2,1)}), bf16[16,128,128]{2,1,0:T(8,128)(2,1)S(1)}, u32[]{:S(2)}, u32[]{:S(2)}) async-start(bf16[16,128,128]{2,1,0:T(8,128)(2,1)} %bitcast.78), calls=%async_computation.6 | async-start | bytes 1048576 | tf_op jit(solution)/shard_map/all_to_all | solution.py:123
  158.5 3.7 %copy-start.3 = (f32[512,2048]{1,0:T(8,128)S(1)}, f32[512,2048]{1,0:T(8,128)}, u32[]{:S(2)}) copy-start(f32[512,2048]{1,0:T(8,128)} %fusion.8) | copy-start | bytes 12582916
  168.7 16.2 %all-to-all-start.7 = ((bf16[16,128,128]{1,2,0:T(8,128)(2,1)}), bf16[16,128,128]{1,2,0:T(8,128)(2,1)S(1)}, u32[]{:S(2)}, u32[]{:S(2)}) async-start(bf16[16,128,128]{1,2,0:T(8,128)(2,1)} %copy.62), calls=%async_computation.7 | async-start | bytes 1048576 | tf_op jit(solution)/shard_map/all_to_all | solution.py:124
  185.9 170.3 %copy-start.1 = (bf16[1,128,2048]{2,1,0:T(8,128)(2,1)S(1)}, bf16[1,128,2048]{2,1,0:T(8,128)(2,1)}, u32[]{:S(2)}) copy-start(bf16[1,128,2048]{2,1,0:T(8,128)(2,1)} %param.29) | copy-start | bytes 1572868
Sparse Core Ops, SparseCore 0:
  124.7 229.2 all-reduce.3
where the time goes:
time: 365 us; the launch traced here: 363 us
  waiting for transfers between devices  197 us (54%)
  matrix products  46.5 us (13%)
  starting transfers between devices  46 us (13%)
  local copies, waits for them, and re-layouts  33.7 us (9%)
  between operations  14.8 us (4%)
  blocking collectives  14.4 us (4%)
  other arithmetic  10.8 us (3%)
    psum x1, waiting for transfers between devices, on_device(): summed = lax.psum(product_first(o_tokens, grad_tokens), ('dp', 'seq'))  162 us
    all_to_all x1, blocking collectives, on_device(): lax.all_to_all(o_heads, 'seq', split_axis=0, concat_axis=1, tiled=True)  14.4 us
    unnamed x111, local copies, waits for them, and re-layouts  10.6 us
    dot_general x1, matrix products, product_first(): lax.dot_general(left, right, (((0,), (0,)), ((), ())), preferred_element_...  8.07 us
    dot_general x4, matrix products, on_device(): jnp.einsum('hqk,qhd->khd', probs, d_block, preferred_element_type=jnp.flo...  7.4 us
  transfers between devices with their start and end apart: 8, of which 8 were waited for; matrix products, arithmetic and copies ran while one was open for 10% of the time, Pallas kernels for 0%

commit v1 on v0

v1 whole, which is shorter than its diff:
```python
import math

import jax
import jax.numpy as jnp
from jax import lax
from jax.experimental import pallas as pl
from jax.experimental.pallas import tpu as pltpu
from jax.sharding import PartitionSpec as P

B16 = jnp.bfloat16
F32 = jnp.float32
HEAD = 128
TOK = 128
LENGTH = 2048
WIDTH = 2048
HEADS = 16
BLOCK = 256
BLOCKS = LENGTH // BLOCK
FACTOR = HEAD ** (-0.5)
FACTOR2 = FACTOR * math.log2(math.e)
VMEM_LIMIT = 48 * 1024 * 1024

ZN, XN, CN, YN, HN = 2, 4, 2, 4, 2


def nt(a, b):
    return lax.dot_general(a, b, (((1,), (1,)), ((), ())), preferred_element_type=F32)


def nn(a, b):
    return lax.dot_general(a, b, (((1,), (0,)), ((), ())), preferred_element_type=F32)


def params():
    return pltpu.CompilerParams(vmem_limit_bytes=VMEM_LIMIT)


def cost(flops, nbytes, exps=0):
    return pl.CostEstimate(flops=flops, bytes_accessed=nbytes, transcendentals=exps)


def pack_kernel(q_ref, k_ref, v_ref, g_ref, w_ref, out_ref):
    d = nt(g_ref[...], w_ref[...]).astype(B16)
    for h in range(2):
        cols = slice(h * HEAD, (h + 1) * HEAD)
        out_ref[h, 0] = q_ref[:, cols]
        out_ref[h, 1] = k_ref[:, cols]
        out_ref[h, 2] = v_ref[:, cols]
        out_ref[h, 3] = d[:, cols]


def pack(q, k, v, g, w):
    part = pl.BlockSpec((TOK, 2 * HEAD), lambda i: (0, i))
    return pl.pallas_call(
        pack_kernel,
        grid=(HEADS // 2,),
        in_specs=[
            part,
            part,
            part,
            pl.BlockSpec((TOK, WIDTH), lambda i: (0, 0)),
            pl.BlockSpec((2 * HEAD, WIDTH), lambda i: (i, 0)),
        ],
        out_specs=pl.BlockSpec((2, 4, TOK, HEAD), lambda i: (i, 0, 0, 0)),
        out_shape=jax.ShapeDtypeStruct((HEADS, 4, TOK, HEAD), B16),
        compiler_params=params(),
        cost_estimate=cost(2 * TOK * WIDTH * WIDTH, 12 << 20),
        name="pack",
    )(q, k, v, g, w)


def rows_of(ref, which, first, count):
    return jnp.concatenate(
        [ref[t, which] for t in range(first // TOK, (first + count) // TOK)], axis=0
    )


def mask_of():
    key = lax.broadcasted_iota(jnp.int32, (BLOCK, BLOCK), 0)
    query = lax.broadcasted_iota(jnp.int32, (BLOCK, BLOCK), 1)
    return query >= key


def forward_kernel(pos_ref, x_ref, o_ref, keep_ref, send_ref, stat_ref, vt_ref):
    core = pos_ref[2]
    visible = mask_of()
    for t in range(HEADS):
        vt_ref[:, t * TOK : (t + 1) * TOK] = x_ref[t, 2].T
    for j in range(BLOCKS):
        first = j * BLOCK
        q = rows_of(x_ref, 0, first, BLOCK)
        tiles = []
        for i in range(j + 1):
            s = nt(rows_of(x_ref, 1, i * BLOCK, BLOCK), q) * FACTOR2
            tiles.append(jnp.where(visible, s, -1e30) if i == j else s)
        top = tiles[0]
        for s in tiles[1:]:
            top = jnp.maximum(top, s)
        top = jnp.max(top, axis=0, keepdims=True)
        total = None
        acc = None
        for i, s in enumerate(tiles):
            p = jnp.exp2(s - top)
            total = p if total is None else total + p
            term = nn(vt_ref[:, i * BLOCK : (i + 1) * BLOCK], p.astype(B16))
            acc = term if acc is None else acc + term
        total = jnp.sum(total, axis=0, keepdims=True)
        ot = acc * (1.0 / total)
        ob = ot.astype(B16)
        oc = ot.T.astype(B16)
        o_ref[2 * j] = oc[:TOK]
        o_ref[2 * j + 1] = oc[TOK:]
        keep_ref[j] = jnp.where(core == 0, ob[:, :TOK], ob[:, TOK:])
        send_ref[j] = jnp.where(core == 0, ob[:, TOK:], ob[:, :TOK])
        d = rows_of(x_ref, 3, first, BLOCK)
        delta = jnp.sum(d.T.astype(F32) * ob.astype(F32), axis=0, keepdims=True)
        stat_ref[0:1, first : first + BLOCK] = top + jnp.log2(total)
        stat_ref[1:2, first : first + BLOCK] = delta


def forward(pos, x):
    vmem = pl.BlockSpec(memory_space=pltpu.VMEM)
    return pl.pallas_call(
        forward_kernel,
        in_specs=[pl.BlockSpec(memory_space=pltpu.SMEM), vmem],
        out_specs=[vmem, vmem, vmem, vmem],
        out_shape=[
            jax.ShapeDtypeStruct((HEADS, TOK, HEAD), B16),
            jax.ShapeDtypeStruct((BLOCKS, HEAD, TOK), B16),
            jax.ShapeDtypeStruct((BLOCKS, HEAD, TOK), B16),
            jax.ShapeDtypeStruct((8, LENGTH), F32),
        ],
        scratch_shapes=[pltpu.VMEM((HEAD, LENGTH), B16)],
        compiler_params=params(),
        cost_estimate=cost(4 * LENGTH * LENGTH * HEAD, 4 << 20, LENGTH * LENGTH // 2),
        name="attention_forward",
    )(pos, x)


def backward_kernel(x_ref, stat_ref, out_ref, dqt_ref):
    visible = mask_of()
    dqt_ref[...] = jnp.zeros_like(dqt_ref)
    for i in range(BLOCKS):
        first = i * BLOCK
        k = rows_of(x_ref, 1, first, BLOCK)
        v = rows_of(x_ref, 2, first, BLOCK)
        kt = k.T
        dk = None
        dv = None
        for j in range(i, BLOCKS):
            cols = slice(j * BLOCK, (j + 1) * BLOCK)
            q = rows_of(x_ref, 0, j * BLOCK, BLOCK)
            d = rows_of(x_ref, 3, j * BLOCK, BLOCK)
            s = nt(k, q) * FACTOR2 - stat_ref[0:1, cols]
            if i == j:
                s = jnp.where(visible, s, -1e30)
            p = jnp.exp2(s)
            dp = nt(v, d) - stat_ref[1:2, cols]
            ds = (p * dp).astype(B16)
            term = nn(p.astype(B16), d)
            dv = term if dv is None else dv + term
            term = nn(ds, q)
            dk = term if dk is None else dk + term
            dqt_ref[:, cols] += nn(kt, ds)
        dk = (dk * FACTOR).astype(B16)
        dv = dv.astype(B16)
        for t in range(2):
            rows = slice(t * TOK, (t + 1) * TOK)
            out_ref[2 * i + t, 1] = dk[rows]
            out_ref[2 * i + t, 2] = dv[rows]
    for t in range(HEADS):
        part = dqt_ref[:, t * TOK : (t + 1) * TOK] * FACTOR
        out_ref[t, 0] = part.T.astype(B16)


def backward(x, stat):
    vmem = pl.BlockSpec(memory_space=pltpu.VMEM)
    return pl.pallas_call(
        backward_kernel,
        in_specs=[vmem, vmem],
        out_specs=vmem,
        out_shape=jax.ShapeDtypeStruct((HEADS, 3, TOK, HEAD), B16),
        scratch_shapes=[pltpu.VMEM((HEAD, LENGTH), F32)],
        compiler_params=params(),
        cost_estimate=cost(10 * LENGTH * LENGTH * HEAD, 4 << 20, LENGTH * LENGTH // 2),
        name="attention_backward",
    )(x, stat)


def project_kernel(o_ref, w_ref, out_ref, lhs_ref):
    @pl.when(pl.program_id(0) == 0)
    def _():
        for h in range(HEADS):
            lhs_ref[:, h * HEAD : (h + 1) * HEAD] = o_ref[h]

    out_ref[...] = nn(lhs_ref[...], w_ref[...]).astype(B16)


def project(o, w):
    cols = 256
    return pl.pallas_call(
        project_kernel,
        grid=(WIDTH // cols,),
        in_specs=[
            pl.BlockSpec((HEADS, TOK, HEAD), lambda i: (0, 0, 0)),
            pl.BlockSpec((WIDTH, cols), lambda i: (0, i)),
        ],
        out_specs=pl.BlockSpec((TOK, cols), lambda i: (0, i)),
        out_shape=jax.ShapeDtypeStruct((TOK, WIDTH), B16),
        scratch_shapes=[pltpu.VMEM((TOK, WIDTH), B16)],
        compiler_params=params(),
        cost_estimate=cost(2 * TOK * WIDTH * WIDTH, 9 << 20),
        name="project",
    )(o, w)


def unpack_kernel(x_ref, q_ref, k_ref, v_ref):
    for h in range(4):
        cols = slice(h * HEAD, (h + 1) * HEAD)
        q_ref[:, cols] = x_ref[h, 0]
        k_ref[:, cols] = x_ref[h, 1]
        v_ref[:, cols] = x_ref[h, 2]


def unpack(x):
    shape = jax.ShapeDtypeStruct((TOK, WIDTH), B16)
    spec = pl.BlockSpec((TOK, 4 * HEAD), lambda i: (0, i))
    return pl.pallas_call(
        unpack_kernel,
        grid=(HEADS // 4,),
        in_specs=[pl.BlockSpec((4, 3, TOK, HEAD), lambda i: (i, 0, 0, 0))],
        out_specs=[spec, spec, spec],
        out_shape=[shape, shape, shape],
        compiler_params=params(),
        cost_estimate=cost(0, 3 << 20),
        name="unpack",
    )(x)


def seq_move(x, dz, dx, dc):
    pairs = []
    for z in range(ZN):
        for a in range(XN):
            for c in range(CN):
                source = (z * XN + a) * CN + c
                target = ((z + dz) % ZN * XN + (a + dx) % XN) * CN + (c + dc) % CN
                pairs.append((source, target))
    return lax.ppermute(x, "seq", pairs)


def dp_move(x, dh, dy):
    pairs = []
    for h in range(HN):
        for y in range(YN):
            pairs.append((h * YN + y, (h + dh) % HN * YN + (y + dy) % YN))
    return lax.ppermute(x, "dp", pairs)


def gather_grads(g):
    left = seq_move(g, 0, 1, 0)
    right = seq_move(g, 0, -1, 0)
    over = seq_move(g, 1, 0, 0)
    half = TOK // 2
    far_a = seq_move(left[:half], 0, 1, 0)
    far_b = seq_move(right[half:], 0, -1, 0)
    over_left = seq_move(over, 0, 1, 0)
    over_right = seq_move(over, 0, -1, 0)
    over_far_a = seq_move(far_a, 1, 0, 0)
    over_far_b = seq_move(far_b, 1, 0, 0)
    return [
        (0, 0, 0, g),
        (0, 3, 0, left),
        (0, 1, 0, right),
        (1, 0, 0, over),
        (0, 2, 0, far_a),
        (0, 2, half, far_b),
        (1, 3, 0, over_left),
        (1, 1, 0, over_right),
        (1, 2, 0, over_far_a),
        (1, 2, half, over_far_b),
    ]


def weight_kernel(places, pos_ref, keep_ref, got_ref, *refs):
    parts = refs[: len(places)]
    own_ref, other_ref, lhs_ref = refs[len(places) :]

    @pl.when(pl.program_id(0) == 0)
    def _():
        at = 0
        for dz, dx, first, rows in places:
            z = lax.rem(pos_ref[0] + dz, ZN)
            a = lax.rem(pos_ref[1] + dx, XN)
            index = z * XN + a
            lhs_ref[:HEAD, at : at + rows] = keep_ref[index][:, first : first + rows]
            lhs_ref[HEAD:, at : at + rows] = got_ref[index][:, first : first + rows]
            at += rows

    rhs = jnp.concatenate([part[...] for part in parts], axis=0)
    total = nn(lhs_ref[...], rhs)
    own_ref[...] = total[:HEAD]
    other_ref[...] = total[HEAD:].astype(B16)


def weight_partial(pos, keep, got, blocks):
    cols = 256
    places = [(dz, dx, first, a.shape[0]) for dz, dx, first, a in blocks]
    arrays = [a for _, _, _, a in blocks]

    def body(*refs):
        weight_kernel(places, *refs)

    whole = pl.BlockSpec((BLOCKS, HEAD, TOK), lambda i: (0, 0, 0))
    spec = pl.BlockSpec((HEAD, cols), lambda i: (0, i))
    return pl.pallas_call(
        body,
        grid=(WIDTH // cols,),
        in_specs=[pl.BlockSpec(memory_space=pltpu.SMEM), whole, whole]
        + [pl.BlockSpec((a.shape[0], cols), lambda i: (0, i)) for a in arrays],
        out_specs=[spec, spec],
        out_shape=[
            jax.ShapeDtypeStruct((HEAD, WIDTH), F32),
            jax.ShapeDtypeStruct((HEAD, WIDTH), B16),
        ],
        scratch_shapes=[pltpu.VMEM((2 * HEAD, LENGTH // 2), B16)],
        compiler_params=params(),
        cost_estimate=cost(2 * LENGTH * HEAD * WIDTH, 6 << 20),
        name="weight_partial",
    )(pos, keep, got, *arrays)


SHARE = HEAD // YN


def split_kernel(pos_ref, own_ref, got_ref, mine_ref, one_ref, two_ref, three_ref):
    y = pos_ref[3]
    for r, ref in enumerate((mine_ref, one_ref, two_ref, three_ref)):
        first = pl.multiple_of(lax.rem(y + r, YN) * SHARE, SHARE)
        rows = pl.ds(first, SHARE)
        ref[...] = (own_ref[rows, :] + got_ref[rows, :].astype(F32)).astype(ref.dtype)


def split_shares(pos, own, got):
    vmem = pl.BlockSpec(memory_space=pltpu.VMEM)
    return pl.pallas_call(
        split_kernel,
        in_specs=[pl.BlockSpec(memory_space=pltpu.SMEM), vmem, vmem],
        out_specs=[vmem] * 4,
        out_shape=[jax.ShapeDtypeStruct((SHARE, WIDTH), F32)]
        + [jax.ShapeDtypeStruct((SHARE, WIDTH), B16)] * 3,
        compiler_params=params(),
        cost_estimate=cost(0, 2 << 20),
        name="split_shares",
    )(pos, own, got)


def join_kernel(pos_ref, mine_ref, one_ref, two_ref, three_ref, out_ref):
    y = pos_ref[3]
    for r, ref in enumerate((mine_ref, one_ref, two_ref, three_ref)):
        first = pl.multiple_of(lax.rem(y + YN - r, YN) * SHARE, SHARE)
        out_ref[pl.ds(first, SHARE), :] = ref[...].astype(F32)


def join_shares(pos, shares):
    vmem = pl.BlockSpec(memory_space=pltpu.VMEM)
    return pl.pallas_call(
        join_kernel,
        in_specs=[pl.BlockSpec(memory_space=pltpu.SMEM)] + [vmem] * 4,
        out_specs=vmem,
        out_shape=jax.ShapeDtypeStruct((HEAD, WIDTH), F32),
        compiler_params=params(),
        cost_estimate=cost(0, 2 << 20),
        name="join_shares",
    )(pos, *shares)


def sum_over_dp(pos, own, got):
    mine, one, two, three = split_shares(pos, own, got)
    total = (
        mine
        + dp_move(one, 0, 1).astype(F32)
        + dp_move(two, 0, 2).astype(F32)
        + dp_move(three, 0, 3).astype(F32)
    ).astype(B16)
    share = (total.astype(F32) + dp_move(total, 1, 0).astype(F32)).astype(B16)
    shares = [share] + [dp_move(share, 0, r) for r in range(1, YN)]
    return join_shares(pos, shares)


def to_heads(x):
    return lax.all_to_all(x, "seq", split_axis=0, concat_axis=0, tiled=True)


def on_device(queries, keys, values, out_weight, out_grad):
    s = lax.axis_index("seq")
    y = lax.rem(lax.axis_index("dp"), YN)
    pos = jnp.stack([s // (XN * CN), lax.rem(s // CN, XN), lax.rem(s, CN), y]).astype(jnp.int32)
    q, k, v, g = (a.reshape(TOK, WIDTH) for a in (queries, keys, values, out_grad))
    blocks = gather_grads(g)
    x = to_heads(pack(q, k, v, g, out_weight))
    o, keep, send, stat = forward(pos, x)
    o_tokens = to_heads(o)
    got = seq_move(send, 0, 0, 1)
    own, other = weight_partial(pos, keep, got, blocks)
    grads = backward(x, stat)
    grad_weight = sum_over_dp(pos, own, seq_move(other, 0, 0, 1))
    grad_q, grad_k, grad_v = unpack(to_heads(grads))
    layer_out = project(o_tokens, out_weight)
    shape = (1, TOK, WIDTH)
    return (
        layer_out.reshape(shape),
        grad_q.reshape(shape),
        grad_k.reshape(shape),
        grad_v.reshape(shape),
        grad_weight,
    )


def solution(mesh):
    tokens = P("dp", "seq", None)
    return jax.shard_map(
        on_device,
        mesh=mesh,
        in_specs=(tokens, tokens, tokens, P(), tokens),
        out_specs=(tokens, tokens, tokens, tokens, P("seq", None)),
        check_vma=False,
    )
```

time: 365 us -> 156 us (0.43)
  waiting for transfers between devices: 197 us -> 52.8 us
  matrix products: 46.5 us -> 0 us
  Pallas kernels: 0 us -> 41.8 us
  local copies, waits for them, and re-layouts: 33.7 us -> 15.8 us
  blocking collectives: 14.4 us -> 0 us
  between operations: 14.8 us -> 0.77 us
  other arithmetic: 10.8 us -> 0.17 us
    psum x1 -> x0, waiting for transfers between devices: 162 us -> none  [on_device(): summed = lax.psum(product_first(o_tokens, grad_tokens), ('dp', 'seq'))]
    ppermute x0 -> x18, waiting for transfers between devices: none -> 52.8 us  [the longest x11 40.4 us: seq_move(): return lax.ppermute(x, 'seq', pairs)]
    dot_general x27 -> x0, matrix products: 46.5 us -> none  [the longest x1 8.07 us: product_first(): lax.dot_general(left, right, (((0,), (0,)), ((), ())), preferred_element_...]
    pallas_call x0 -> x8, Pallas kernels: none -> 41.8 us  [the longest x1 8.73 us: pack(): pl.pallas_call(pack_kernel, grid=(HEADS // 2,), in_specs=[part, part, par...]
    all_to_all x7 -> x3, waiting for transfers between devices: 34.6 us -> 0.01 us  [to_heads(): return lax.all_to_all(x, 'seq', split_axis=0, concat_axis=0, tiled=True)]
    all_to_all x7 -> x3, starting transfers between devices: 45.9 us -> 17.7 us  [to_heads(): return lax.all_to_all(x, 'seq', split_axis=0, concat_axis=0, tiled=True)]
    ppermute x0 -> x18, starting transfers between devices: none -> 24.7 us  [the longest x7 14.2 us: dp_move(): return lax.ppermute(x, 'dp', pairs)]
    all_to_all x1 -> x0, blocking collectives: 14.4 us -> none  [on_device(): lax.all_to_all(o_heads, 'seq', split_axis=0, concat_axis=1, tiled=True)]
  transfers between devices with their start and end apart: 8 -> 21, of which waited for: 8 -> 7; matrix products, arithmetic and copies ran while one was open for 10% -> 1% of each run, Pallas kernels for 0% -> 20%
where the time goes in v1:
time: 156 us; the launch traced here: 154 us
  waiting for transfers between devices  52.8 us (34%)
  starting transfers between devices  42.4 us (27%)
  Pallas kernels  41.8 us (27%)
  local copies, waits for them, and re-layouts  15.8 us (10%)
    ppermute x11, waiting for transfers between devices, seq_move(): return lax.ppermute(x, 'seq', pairs)  40.4 us
    all_to_all x3, starting transfers between devices, to_heads(): return lax.all_to_all(x, 'seq', split_axis=0, concat_axis=0, tiled=True)  17.7 us
    unnamed x36, local copies, waits for them, and re-layouts  14.3 us
    ppermute x7, starting transfers between devices, dp_move(): return lax.ppermute(x, 'dp', pairs)  14.2 us
    ppermute x7, waiting for transfers between devices, dp_move(): return lax.ppermute(x, 'dp', pairs)  12.3 us
    ppermute x11, starting transfers between devices, seq_move(): return lax.ppermute(x, 'seq', pairs)  10.4 us
    pallas_call x1, Pallas kernels, pack(): pl.pallas_call(pack_kernel, grid=(HEADS // 2,), in_specs=[part, part, par...  8.73 us
    pallas_call x1, Pallas kernels, backward(): pl.pallas_call(backward_kernel, in_specs=[vmem, vmem], out_specs=vmem, ou...  8.58 us
  transfers between devices with their start and end apart: 21, of which 7 were waited for; matrix products, arithmetic and copies ran while one was open for 1% of the time, Pallas kernels for 20%

profile of v1, /device:TPU:2, one launch (start us, length us, event | category | flops | bytes accessed | tf_op | source)
XLA Modules:
  0.0 153.6 jit_solution(16174825168434892342)
XLA Ops:
  0.6 0.0 copy-start
  0.6 1.0 copy-done
  1.7 1.0 copy-done.8
  2.7 1.0 copy-done.9
  3.8 1.0 copy-done.10
  4.8 8.7 %pack.1 = bf16[16,4,128,128]{3,2,1,0:T(8,128)(2,1)} custom-call(bf16[128,2048]{1,0:T(8,128)(2,1)S(1)} %bitcast.17, bf16[128,2048]{1,0:T(8,128)(2,1)S(1)} %bitcast.18, bf16[128,2048]{1,0:T(8,128)(2,1)S(1)} %bitcast.19, bf16[128,2048]{1,0:T(8,128)(2,1)S(1)} %bitcast.12, bf16[2048,2048]{1,0:T(8,128)(2,1)} %w_ref.3), custom_call_target="tpu_custom_call" | custom-call | flops 1073741824 | bytes 12582912 | tf_op jit(solution)/shard_map/pack/pallas_call | solution.py:54
  13.5 6.3 %all-to-all-start = ((bf16[16,4,128,128]{3,2,1,0:T(8,128)(2,1)}), bf16[16,4,128,128]{3,2,1,0:T(8,128)(2,1)S(1)}, u32[]{:S(2)}, u32[]{:S(2)}) async-start(bf16[16,4,128,128]{3,2,1,0:T(8,128)(2,1)} %pack.1), calls=%async_computation | async-start | bytes 4194304 | tf_op jit(solution)/shard_map/all_to_all | solution.py:391
  19.9 1.5 collective-permute-start.1
  21.4 0.6 collective-permute-start.2
  22.0 1.5 collective-permute-start.3
  23.4 36.3 %collective-permute-done.1.refs_4_ = bf16[128,2048]{1,0:T(8,128)(2,1)S(1)} collective-permute-done((bf16[128,2048]{1,0:T(8,128)(2,1)S(1)}, bf16[128,2048]{1,0:T(8,128)(2,1)S(1)}, u32[]{:S(2)}, u32[]{:S(2)}) %collective-permute-start.1) | collective-permute-done | bytes 524320 | tf_op jit(solution)/shard_map/ppermute | solution.py:248
  59.8 0.7 slice.8
  60.5 0.0 collective-permute-start.4
  60.5 0.0 collective-permute-done.2.refs_5_
  60.5 0.7 slice.9
  61.2 0.8 copy-done.5
  62.0 2.0 %collective-permute-start.5 = (bf16[64,2048]{1,0:T(8,128)(2,1)}, bf16[64,2048]{1,0:T(8,128)(2,1)}, u32[]{:S(2)}, u32[]{:S(2)}) collective-permute-start(bf16[64,2048]{1,0:T(8,128)(2,1)} %slice.9), channel_id=1, source_target_pairs={{0,6},{1,7},{2,0},{3,1},{4,2},{5,3},{6,4},{7,5},{8,14},{9,15},{10,... | collective-permute-start | bytes 786440 | tf_op jit(solution)/shard_map/ppermute | solution.py:248
  64.0 0.0 collective-permute-start.6
  64.0 2.0 %collective-permute-start.7 = (bf16[128,2048]{1,0:T(8,128)(2,1)}, bf16[128,2048]{1,0:T(8,128)(2,1)}, u32[]{:S(2)}, u32[]{:S(2)}) collective-permute-start(bf16[128,2048]{1,0:T(8,128)(2,1)} %collective-permute-done.3.refs_6_), channel_id=1, source_target_pairs={{0,6},{1,7},{2,0},{3,1},{4,2},{5,3},{6,4},{7,5},{8,14},{9,15},{10,... | collective-permute-start | bytes 1572872 | tf_op jit(solution)/shard_map/ppermute | solution.py:248
  66.1 0.1 pad_add_fusion.pos_ref.refs_0_
  66.1 3.7 %collective-permute-done.4.refs_7_ = bf16[64,2048]{1,0:T(8,128)(2,1)S(1)} collective-permute-done((bf16[64,2048]{1,0:T(8,128)(2,1)}, bf16[64,2048]{1,0:T(8,128)(2,1)S(1)}, u32[]{:S(2)}, u32[]{:S(2)}) %collective-permute-start.4) | collective-permute-done | bytes 262176 | tf_op jit(solution)/shard_map/ppermute | solution.py:248
  69.9 1.3 collective-permute-start.8
  71.2 0.3 collective-permute-done.5.refs_8_
  71.5 1.3 collective-permute-start.9
  72.8 0.0 all-to-all-done.x_ref
  72.8 5.8 %attention_forward.1 = (bf16[16,128,128]{2,1,0:T(8,128)(2,1)S(1)}, bf16[8,128,128]{2,1,0:T(8,128)(2,1)S(1)}, bf16[8,128,128]{2,1,0:T(8,128)(2,1)}, f32[8,2048]{1,0:T(8,128)S(1)}) custom-call(s32[4]{0:T(128)S(1)} %pad_add_fusion.pos_ref.refs_0_, bf16[16,4,128,128]{3,2,1,0:T(8,128)(2,1)S(1)} %all-to-all-done.x_ref), custom_call_target="tpu_custom_call" | custom-call | flops 2147483648 | bytes 4194304 | tf_op jit(solution)/shard_map/attention_forward/pallas_call | solution.py:123
  78.6 0.8 copy-done.11
  79.4 0.7 copy-done.14
  80.1 5.6 %all-to-all-start.1 = ((bf16[16,128,128]{2,1,0:T(8,128)(2,1)}), bf16[16,128,128]{2,1,0:T(8,128)(2,1)S(1)}, u32[]{:S(2)}, u32[]{:S(2)}) async-start(bf16[16,128,128]{2,1,0:T(8,128)(2,1)} %copy-done.11), calls=%async_computation.1 | async-start | bytes 1048576 | tf_op jit(solution)/shard_map/all_to_all | solution.py:391
  85.7 0.0 collective-permute-done.6.refs_9_
  85.7 0.0 collective-permute-done.7.refs_10_
  85.7 0.0 collective-permute-done.8.refs_11_
  85.8 0.0 copy-start.16
  85.8 0.7 copy-done.16
  86.5 1.0 copy-done.6
  87.5 0.9 copy-done.15
  88.5 0.9 copy-done.17
  89.4 6.9 %weight_partial.1 = (f32[128,2048]{1,0:T(8,128)}, bf16[128,2048]{1,0:T(8,128)(2,1)}) custom-call(s32[4]{0:T(128)S(1)} %pad_add_fusion.pos_ref.refs_0_, bf16[8,128,128]{2,1,0:T(8,128)(2,1)S(1)} %copy-done.15, bf16[8,128,128]{2,1,0:T(8,128)(2,1)S(1)} %copy-done.17, bf16[128,2048]{1,0:T(8,128)(2,1)S(1)} %bitcast.16, ...), custom_call_target="tpu_custom_call" | custom-call | flops 1073741824 | bytes 6291456 | tf_op jit(solution)/shard_map/weight_partial/pallas_call | solution.py:315
  96.3 0.2 collective-permute-start.10
  96.5 8.6 %attention_backward.1 = bf16[16,3,128,128]{3,2,1,0:T(8,128)(2,1)S(1)} custom-call(bf16[16,4,128,128]{3,2,1,0:T(8,128)(2,1)S(1)} %copy-done.3, f32[8,2048]{1,0:T(8,128)S(1)} %get-tuple-element.19.stat_ref), custom_call_target="tpu_custom_call" | custom-call | flops 5368709120 | bytes 4194304 | tf_op jit(solution)/shard_map/attention_backward/pallas_call | solution.py:178
  105.1 1.2 copy-done.4
  106.3 0.0 all-to-all-done.1.o_ref
  106.3 5.7 %all-to-all-start.2 = ((bf16[16,3,128,128]{3,2,1,0:T(8,128)(2,1)}), bf16[16,3,128,128]{3,2,1,0:T(8,128)(2,1)S(1)}, u32[]{:S(2)}, u32[]{:S(2)}) async-start(bf16[16,3,128,128]{3,2,1,0:T(8,128)(2,1)} %copy-done.4), calls=%async_computation.2 | async-start | bytes 3145728 | tf_op jit(solution)/shard_map/all_to_all | solution.py:391
  112.0 0.0 copy-start.12
  112.0 0.8 copy-done.12
  112.8 1.2 copy-done.7
  114.1 1.0 copy-done.13
  115.1 0.6 split_shares.1
  115.7 3.1 %collective-permute-start.13 = (bf16[32,2048]{1,0:T(8,128)(2,1)S(1)}, bf16[32,2048]{1,0:T(8,128)(2,1)S(1)}, u32[]{:S(2)}, u32[]{:S(2)}) collective-permute-start(bf16[32,2048]{1,0:T(8,128)(2,1)S(1)} %get-tuple-element.30), channel_id=1, source_target_pairs={{0,48},{16,0},{32,16},{48,32},{64,112},{80,64},{96,80},{112,96},{1... | collective-permute-start | bytes 393224 | tf_op jit(solution)/shard_map/ppermute | solution.py:256
  118.8 0.6 collective-permute-start.12
  119.5 1.0 collective-permute-start.11
  120.4 4.3 %collective-permute-done.13 = bf16[32,2048]{1,0:T(8,128)(2,1)S(1)} collective-permute-done((bf16[32,2048]{1,0:T(8,128)(2,1)S(1)}, bf16[32,2048]{1,0:T(8,128)(2,1)S(1)}, u32[]{:S(2)}, u32[]{:S(2)}) %collective-permute-start.13) | collective-permute-done | bytes 131104 | tf_op jit(solution)/shard_map/ppermute | solution.py:256
  124.7 2.0 %collective-permute-done.12 = bf16[32,2048]{1,0:T(8,128)(2,1)S(1)} collective-permute-done((bf16[32,2048]{1,0:T(8,128)(2,1)S(1)}, bf16[32,2048]{1,0:T(8,128)(2,1)S(1)}, u32[]{:S(2)}, u32[]{:S(2)}) %collective-permute-start.12) | collective-permute-done | bytes 131104 | tf_op jit(solution)/shard_map/ppermute | solution.py:256
  126.7 1.7 %collective-permute-done.11 = bf16[32,2048]{1,0:T(8,128)(2,1)S(1)} collective-permute-done((bf16[32,2048]{1,0:T(8,128)(2,1)S(1)}, bf16[32,2048]{1,0:T(8,128)(2,1)S(1)}, u32[]{:S(2)}, u32[]{:S(2)}) %collective-permute-start.11) | collective-permute-done | bytes 131104 | tf_op jit(solution)/shard_map/ppermute | solution.py:256
  128.4 0.1 add_convert_fusion.1
  128.5 3.7 %collective-permute-start.14 = (bf16[32,2048]{1,0:T(8,128)(2,1)S(1)}, bf16[32,2048]{1,0:T(8,128)(2,1)S(1)}, u32[]{:S(2)}, u32[]{:S(2)}) collective-permute-start(bf16[32,2048]{1,0:T(8,128)(2,1)S(1)} %add_convert_fusion.1), channel_id=1, source_target_pairs={{0,64},{16,80},{32,96},{48,112},{64,0},{80,16},{96,32},{112,48},{1... | collective-permute-start | bytes 393224 | tf_op jit(solution)/shard_map/ppermute | solution.py:256
  132.1 4.3 %collective-permute-done.14 = bf16[32,2048]{1,0:T(8,128)(2,1)S(1)} collective-permute-done((bf16[32,2048]{1,0:T(8,128)(2,1)S(1)}, bf16[32,2048]{1,0:T(8,128)(2,1)S(1)}, u32[]{:S(2)}, u32[]{:S(2)}) %collective-permute-start.14) | collective-permute-done | bytes 131104 | tf_op jit(solution)/shard_map/ppermute | solution.py:256
  136.5 1.6 %collective-permute-start.15 = (bf16[32,2048]{1,0:T(8,128)(2,1)S(1)}, bf16[32,2048]{1,0:T(8,128)(2,1)S(1)}, u32[]{:S(2)}, u32[]{:S(2)}) collective-permute-start(bf16[32,2048]{1,0:T(8,128)(2,1)S(1)} %add_convert_fusion.mine_ref), channel_id=1, source_target_pairs={{0,16},{16,32},{32,48},{48,0},{64,80},{80,96},{96,112},{112,64},{1... | collective-permute-start | bytes 393224 | tf_op jit(solution)/shard_map/ppermute | solution.py:256
  138.2 2.9 %collective-permute-start.16 = (bf16[32,2048]{1,0:T(8,128)(2,1)S(1)}, bf16[32,2048]{1,0:T(8,128)(2,1)S(1)}, u32[]{:S(2)}, u32[]{:S(2)}) collective-permute-start(bf16[32,2048]{1,0:T(8,128)(2,1)S(1)} %add_convert_fusion.mine_ref), channel_id=1, source_target_pairs={{0,32},{16,48},{32,0},{48,16},{64,96},{80,112},{96,64},{112,80},{1... | collective-permute-start | bytes 393224 | tf_op jit(solution)/shard_map/ppermute | solution.py:256
  141.1 1.3 collective-permute-start.17
  142.4 7.8 %project.1 = bf16[128,2048]{1,0:T(8,128)(2,1)} custom-call(bf16[16,128,128]{2,1,0:T(8,128)(2,1)S(1)} %all-to-all-done.1.o_ref, bf16[2048,2048]{1,0:T(8,128)(2,1)} %w_ref.3), custom_call_target="tpu_custom_call" | custom-call | flops 1073741824 | bytes 9437184 | tf_op jit(solution)/shard_map/project/pallas_call | solution.py:201
  150.2 0.0 collective-permute-done.15.one_ref
  150.3 1.6 %join_shares.1 = f32[128,2048]{1,0:T(8,128)} custom-call(s32[4]{0:T(128)S(1)} %pad_add_fusion.pos_ref.refs_0_, bf16[32,2048]{1,0:T(8,128)(2,1)S(1)} %add_convert_fusion.mine_ref, bf16[32,2048]{1,0:T(8,128)(2,1)S(1)} %collective-permute-done.15.one_ref, bf16[32,2048]{1,0:T(8,128)(2,1)S(1)} %collective-permute-done.16.two_ref, ...), custom_call_target="tpu_custom_call" | custom-call | bytes 2097152 | tf_op jit(solution)/shard_map/join_shares/pallas_call | solution.py:366
  151.8 1.7 %unpack.1 = (bf16[128,2048]{1,0:T(8,128)(2,1)}, bf16[128,2048]{1,0:T(8,128)(2,1)}, bf16[128,2048]{1,0:T(8,128)(2,1)}) custom-call(bf16[16,3,128,128]{3,2,1,0:T(8,128)(2,1)S(1)} %all-to-all-done.2.x_ref), custom_call_target="tpu_custom_call" | custom-call | bytes 3145728 | tf_op jit(solution)/shard_map/unpack/pallas_call | solution.py:228
  (27 shorter events, 0.1 us)
Async XLA Ops:
  0.6 1.0 copy-start
  1.7 1.0 copy-start.8
  2.7 1.0 copy-start.9
  3.8 1.0 copy-start.10
  13.5 6.3 %copy-start.1 = (bf16[1,128,2048]{2,1,0:T(8,128)(2,1)S(1)}, bf16[1,128,2048]{2,1,0:T(8,128)(2,1)}, u32[]{:S(2)}) copy-start(bf16[1,128,2048]{2,1,0:T(8,128)(2,1)} %param.9) | copy-start | bytes 1572868
  13.5 59.3 %all-to-all-start = ((bf16[16,4,128,128]{3,2,1,0:T(8,128)(2,1)}), bf16[16,4,128,128]{3,2,1,0:T(8,128)(2,1)S(1)}, u32[]{:S(2)}, u32[]{:S(2)}) async-start(bf16[16,4,128,128]{3,2,1,0:T(8,128)(2,1)} %pack.1), calls=%async_computation | async-start | bytes 4194304 | tf_op jit(solution)/shard_map/all_to_all | solution.py:391
  19.9 39.9 %collective-permute-start.1 = (bf16[128,2048]{1,0:T(8,128)(2,1)S(1)}, bf16[128,2048]{1,0:T(8,128)(2,1)S(1)}, u32[]{:S(2)}, u32[]{:S(2)}) collective-permute-start(bf16[128,2048]{1,0:T(8,128)(2,1)S(1)} %bitcast.13), channel_id=1, source_target_pairs={{0,2},{1,3},{2,4},{3,5},{4,6},{5,7},{6,0},{7,1},{8,10},{9,11},{10,... | collective-permute-start | bytes 1572872 | tf_op jit(solution)/shard_map/ppermute | solution.py:248
  21.4 39.1 %collective-permute-start.2 = (bf16[128,2048]{1,0:T(8,128)(2,1)S(1)}, bf16[128,2048]{1,0:T(8,128)(2,1)S(1)}, u32[]{:S(2)}, u32[]{:S(2)}) collective-permute-start(bf16[128,2048]{1,0:T(8,128)(2,1)S(1)} %bitcast.14), channel_id=1, source_target_pairs={{0,6},{1,7},{2,0},{3,1},{4,2},{5,3},{6,4},{7,5},{8,14},{9,15},{10,... | collective-permute-start | bytes 1572872 | tf_op jit(solution)/shard_map/ppermute | solution.py:248
  22.0 42.1 %collective-permute-start.3 = (bf16[128,2048]{1,0:T(8,128)(2,1)S(1)}, bf16[128,2048]{1,0:T(8,128)(2,1)}, u32[]{:S(2)}, u32[]{:S(2)}) collective-permute-start(bf16[128,2048]{1,0:T(8,128)(2,1)S(1)} %bitcast.15), channel_id=1, source_target_pairs={{0,8},{1,9},{2,10},{3,11},{4,12},{5,13},{6,14},{7,15},{8,0},{9,1},... | collective-permute-start | bytes 1572872 | tf_op jit(solution)/shard_map/ppermute | solution.py:248
  60.5 9.4 %collective-permute-start.4 = (bf16[64,2048]{1,0:T(8,128)(2,1)}, bf16[64,2048]{1,0:T(8,128)(2,1)S(1)}, u32[]{:S(2)}, u32[]{:S(2)}) collective-permute-start(bf16[64,2048]{1,0:T(8,128)(2,1)} %slice.8), channel_id=1, source_target_pairs={{0,2},{1,3},{2,4},{3,5},{4,6},{5,7},{6,0},{7,1},{8,10},{9,11},{10,... | collective-permute-start | bytes 786440 | tf_op jit(solution)/shard_map/ppermute | solution.py:248
  61.2 0.8 copy-start.5
  62.0 9.5 %collective-permute-start.5 = (bf16[64,2048]{1,0:T(8,128)(2,1)}, bf16[64,2048]{1,0:T(8,128)(2,1)}, u32[]{:S(2)}, u32[]{:S(2)}) collective-permute-start(bf16[64,2048]{1,0:T(8,128)(2,1)} %slice.9), channel_id=1, source_target_pairs={{0,6},{1,7},{2,0},{3,1},{4,2},{5,3},{6,4},{7,5},{8,14},{9,15},{10,... | collective-permute-start | bytes 786440 | tf_op jit(solution)/shard_map/ppermute | solution.py:248
  64.0 21.7 %collective-permute-start.6 = (bf16[128,2048]{1,0:T(8,128)(2,1)}, bf16[128,2048]{1,0:T(8,128)(2,1)}, u32[]{:S(2)}, u32[]{:S(2)}) collective-permute-start(bf16[128,2048]{1,0:T(8,128)(2,1)} %collective-permute-done.3.refs_6_), channel_id=1, source_target_pairs={{0,2},{1,3},{2,4},{3,5},{4,6},{5,7},{6,0},{7,1},{8,10},{9,11},{10,... | collective-permute-start | bytes 1572872 | tf_op jit(solution)/shard_map/ppermute | solution.py:248
  64.0 21.7 %collective-permute-start.7 = (bf16[128,2048]{1,0:T(8,128)(2,1)}, bf16[128,2048]{1,0:T(8,128)(2,1)}, u32[]{:S(2)}, u32[]{:S(2)}) collective-permute-start(bf16[128,2048]{1,0:T(8,128)(2,1)} %collective-permute-done.3.refs_6_), channel_id=1, source_target_pairs={{0,6},{1,7},{2,0},{3,1},{4,2},{5,3},{6,4},{7,5},{8,14},{9,15},{10,... | collective-permute-start | bytes 1572872 | tf_op jit(solution)/shard_map/ppermute | solution.py:248
  69.9 15.8 %collective-permute-start.8 = (bf16[64,2048]{1,0:T(8,128)(2,1)S(1)}, bf16[64,2048]{1,0:T(8,128)(2,1)}, u32[]{:S(2)}, u32[]{:S(2)}) collective-permute-start(bf16[64,2048]{1,0:T(8,128)(2,1)S(1)} %collective-permute-done.4.refs_7_), channel_id=1, source_target_pairs={{0,8},{1,9},{2,10},{3,11},{4,12},{5,13},{6,14},{7,15},{8,0},{9,1},... | collective-permute-start | bytes 786440 | tf_op jit(solution)/shard_map/ppermute | solution.py:248
  71.5 14.2 %collective-permute-start.9 = (bf16[64,2048]{1,0:T(8,128)(2,1)}, bf16[64,2048]{1,0:T(8,128)(2,1)}, u32[]{:S(2)}, u32[]{:S(2)}) collective-permute-start(bf16[64,2048]{1,0:T(8,128)(2,1)} %collective-permute-done.5.refs_8_), channel_id=1, source_target_pairs={{0,8},{1,9},{2,10},{3,11},{4,12},{5,13},{6,14},{7,15},{8,0},{9,1},... | collective-permute-start | bytes 786440 | tf_op jit(solution)/shard_map/ppermute | solution.py:248
  72.8 5.8 %copy-start.2 = (bf16[16,4,128,128]{3,2,1,0:T(8,128)(2,1)}, bf16[16,4,128,128]{3,2,1,0:T(8,128)(2,1)S(1)}, u32[]{:S(2)}) copy-start(bf16[16,4,128,128]{3,2,1,0:T(8,128)(2,1)S(1)} %all-to-all-done.x_ref) | copy-start | bytes 6291460
  78.6 0.8 copy-start.11
  79.4 0.7 copy-start.14
  80.1 5.6 %collective-permute-start = (bf16[8,128,128]{2,1,0:T(8,128)(2,1)}, bf16[8,128,128]{2,1,0:T(8,128)(2,1)S(1)}, u32[]{:S(2)}, u32[]{:S(2)}) collective-permute-start(bf16[8,128,128]{2,1,0:T(8,128)(2,1)} %get-tuple-element.24), channel_id=1, source_target_pairs={{0,1},{1,0},{2,3},{3,2},{4,5},{5,4},{6,7},{7,6},{8,9},{9,8},{10,11... | collective-permute-start | bytes 786440 | tf_op jit(solution)/shard_map/ppermute | solution.py:248
  80.1 26.2 %all-to-all-start.1 = ((bf16[16,128,128]{2,1,0:T(8,128)(2,1)}), bf16[16,128,128]{2,1,0:T(8,128)(2,1)S(1)}, u32[]{:S(2)}, u32[]{:S(2)}) async-start(bf16[16,128,128]{2,1,0:T(8,128)(2,1)} %copy-done.11), calls=%async_computation.1 | async-start | bytes 1048576 | tf_op jit(solution)/shard_map/all_to_all | solution.py:391
  85.8 0.7 copy-start.16
  86.5 1.0 copy-start.6
  87.5 0.9 copy-start.15
  88.5 0.9 copy-start.17
  89.4 7.1 %copy-start.3 = (bf16[16,4,128,128]{3,2,1,0:T(8,128)(2,1)S(1)}, bf16[16,4,128,128]{3,2,1,0:T(8,128)(2,1)}, u32[]{:S(2)}) copy-start(bf16[16,4,128,128]{3,2,1,0:T(8,128)(2,1)} %copy-done.2) | copy-start | bytes 6291460
  96.3 15.7 %collective-permute-start.10 = (bf16[128,2048]{1,0:T(8,128)(2,1)}, bf16[128,2048]{1,0:T(8,128)(2,1)S(1)}, u32[]{:S(2)}, u32[]{:S(2)}) collective-permute-start(bf16[128,2048]{1,0:T(8,128)(2,1)} %get-tuple-element.26), channel_id=1, source_target_pairs={{0,1},{1,0},{2,3},{3,2},{4,5},{5,4},{6,7},{7,6},{8,9},{9,8},{10,11... | collective-permute-start | bytes 1572872 | tf_op jit(solution)/shard_map/ppermute | solution.py:248
  105.1 1.2 copy-start.4
  106.3 45.6 %all-to-all-start.2 = ((bf16[16,3,128,128]{3,2,1,0:T(8,128)(2,1)}), bf16[16,3,128,128]{3,2,1,0:T(8,128)(2,1)S(1)}, u32[]{:S(2)}, u32[]{:S(2)}) async-start(bf16[16,3,128,128]{3,2,1,0:T(8,128)(2,1)} %copy-done.4), calls=%async_computation.2 | async-start | bytes 3145728 | tf_op jit(solution)/shard_map/all_to_all | solution.py:391
  112.0 0.8 copy-start.12
  112.8 1.2 copy-start.7
  114.1 1.0 copy-start.13
  115.7 9.0 %collective-permute-start.13 = (bf16[32,2048]{1,0:T(8,128)(2,1)S(1)}, bf16[32,2048]{1,0:T(8,128)(2,1)S(1)}, u32[]{:S(2)}, u32[]{:S(2)}) collective-permute-start(bf16[32,2048]{1,0:T(8,128)(2,1)S(1)} %get-tuple-element.30), channel_id=1, source_target_pairs={{0,48},{16,0},{32,16},{48,32},{64,112},{80,64},{96,80},{112,96},{1... | collective-permute-start | bytes 393224 | tf_op jit(solution)/shard_map/ppermute | solution.py:256
  118.8 7.9 %collective-permute-start.12 = (bf16[32,2048]{1,0:T(8,128)(2,1)S(1)}, bf16[32,2048]{1,0:T(8,128)(2,1)S(1)}, u32[]{:S(2)}, u32[]{:S(2)}) collective-permute-start(bf16[32,2048]{1,0:T(8,128)(2,1)S(1)} %get-tuple-element.29), channel_id=1, source_target_pairs={{0,32},{16,48},{32,0},{48,16},{64,96},{80,112},{96,64},{112,80},{1... | collective-permute-start | bytes 393224 | tf_op jit(solution)/shard_map/ppermute | solution.py:256
  119.5 9.0 %collective-permute-start.11 = (bf16[32,2048]{1,0:T(8,128)(2,1)S(1)}, bf16[32,2048]{1,0:T(8,128)(2,1)S(1)}, u32[]{:S(2)}, u32[]{:S(2)}) collective-permute-start(bf16[32,2048]{1,0:T(8,128)(2,1)S(1)} %get-tuple-element.28), channel_id=1, source_target_pairs={{0,16},{16,32},{32,48},{48,0},{64,80},{80,96},{96,112},{112,64},{1... | collective-permute-start | bytes 393224 | tf_op jit(solution)/shard_map/ppermute | solution.py:256
  128.5 8.0 %collective-permute-start.14 = (bf16[32,2048]{1,0:T(8,128)(2,1)S(1)}, bf16[32,2048]{1,0:T(8,128)(2,1)S(1)}, u32[]{:S(2)}, u32[]{:S(2)}) collective-permute-start(bf16[32,2048]{1,0:T(8,128)(2,1)S(1)} %add_convert_fusion.1), channel_id=1, source_target_pairs={{0,64},{16,80},{32,96},{48,112},{64,0},{80,16},{96,32},{112,48},{1... | collective-permute-start | bytes 393224 | tf_op jit(solution)/shard_map/ppermute | solution.py:256
  136.5 13.7 %collective-permute-start.15 = (bf16[32,2048]{1,0:T(8,128)(2,1)S(1)}, bf16[32,2048]{1,0:T(8,128)(2,1)S(1)}, u32[]{:S(2)}, u32[]{:S(2)}) collective-permute-start(bf16[32,2048]{1,0:T(8,128)(2,1)S(1)} %add_convert_fusion.mine_ref), channel_id=1, source_target_pairs={{0,16},{16,32},{32,48},{48,0},{64,80},{80,96},{96,112},{112,64},{1... | collective-permute-start | bytes 393224 | tf_op jit(solution)/shard_map/ppermute | solution.py:256
  138.2 12.1 %collective-permute-start.16 = (bf16[32,2048]{1,0:T(8,128)(2,1)S(1)}, bf16[32,2048]{1,0:T(8,128)(2,1)S(1)}, u32[]{:S(2)}, u32[]{:S(2)}) collective-permute-start(bf16[32,2048]{1,0:T(8,128)(2,1)S(1)} %add_convert_fusion.mine_ref), channel_id=1, source_target_pairs={{0,32},{16,48},{32,0},{48,16},{64,96},{80,112},{96,64},{112,80},{1... | collective-permute-start | bytes 393224 | tf_op jit(solution)/shard_map/ppermute | solution.py:256
  141.1 9.2 %collective-permute-start.17 = (bf16[32,2048]{1,0:T(8,128)(2,1)S(1)}, bf16[32,2048]{1,0:T(8,128)(2,1)S(1)}, u32[]{:S(2)}, u32[]{:S(2)}) collective-permute-start(bf16[32,2048]{1,0:T(8,128)(2,1)S(1)} %add_convert_fusion.mine_ref), channel_id=1, source_target_pairs={{0,48},{16,0},{32,16},{48,32},{64,112},{80,64},{96,80},{112,96},{1... | collective-permute-start | bytes 393224 | tf_op jit(solution)/shard_map/ppermute | solution.py:256

commit v2 on v1

v2 whole, which is shorter than its diff:
```python
import math

import jax
import jax.numpy as jnp
from jax import lax
from jax.experimental import pallas as pl
from jax.experimental.pallas import tpu as pltpu
from jax.sharding import PartitionSpec as P

B16 = jnp.bfloat16
F32 = jnp.float32
HEAD = 128
TOK = 128
LENGTH = 2048
WIDTH = 2048
HEADS = 16
BLOCK = 256
BLOCKS = LENGTH // BLOCK
FACTOR = HEAD ** (-0.5)
FACTOR2 = FACTOR * math.log2(math.e)
BIG = 60 << 20
SMALL = 32 << 20
WIDE = 57 << 20

ZN, XN, CN, YN, HN = 2, 4, 2, 4, 2


def nt(a, b):
    return lax.dot_general(a, b, (((1,), (1,)), ((), ())), preferred_element_type=F32)


def nn(a, b):
    return lax.dot_general(a, b, (((1,), (0,)), ((), ())), preferred_element_type=F32)


def params(limit):
    return pltpu.CompilerParams(vmem_limit_bytes=limit)


def cost(flops, nbytes, exps=0):
    return pl.CostEstimate(flops=flops, bytes_accessed=nbytes, transcendentals=exps)


PACK_HEADS = 8


def pack_kernel(q_ref, k_ref, v_ref, g_ref, *refs):
    out_ref = refs[PACK_HEADS]
    for h in range(PACK_HEADS):
        cols = slice(h * HEAD, (h + 1) * HEAD)
        out_ref[h, 0] = q_ref[:, cols]
        out_ref[h, 1] = k_ref[:, cols]
        out_ref[h, 2] = v_ref[:, cols]
        out_ref[h, 3] = nt(g_ref[...], refs[h][...]).astype(B16)


def pack(q, k, v, g, w):
    part = pl.BlockSpec((TOK, PACK_HEADS * HEAD), lambda i: (0, i))
    return pl.pallas_call(
        pack_kernel,
        grid=(HEADS // PACK_HEADS,),
        in_specs=[part, part, part, pl.BlockSpec((TOK, WIDTH), lambda i: (0, 0))]
        + [
            pl.BlockSpec((HEAD, WIDTH), lambda i, h=h: (PACK_HEADS * i + h, 0))
            for h in range(PACK_HEADS)
        ],
        out_specs=pl.BlockSpec((PACK_HEADS, 4, TOK, HEAD), lambda i: (i, 0, 0, 0)),
        out_shape=jax.ShapeDtypeStruct((HEADS, 4, TOK, HEAD), B16),
        compiler_params=params(WIDE),
        cost_estimate=cost(2 * TOK * WIDTH * WIDTH, 12 << 20),
        name="pack",
    )(q, k, v, g, *[w] * PACK_HEADS)


def rows_of(ref, which, first, count):
    return jnp.concatenate(
        [ref[t, which] for t in range(first // TOK, (first + count) // TOK)], axis=0
    )


def mask_of():
    key = lax.broadcasted_iota(jnp.int32, (BLOCK, BLOCK), 0)
    query = lax.broadcasted_iota(jnp.int32, (BLOCK, BLOCK), 1)
    return query >= key


def forward_kernel(x_ref, o_ref, ot_ref, stat_ref, vt_ref):
    visible = mask_of()
    for t in range(HEADS):
        vt_ref[:, t * TOK : (t + 1) * TOK] = x_ref[t, 2].T
    for j in range(BLOCKS):
        first = j * BLOCK
        q = rows_of(x_ref, 0, first, BLOCK)
        tiles = []
        for i in range(j + 1):
            s = nt(rows_of(x_ref, 1, i * BLOCK, BLOCK), q) * FACTOR2
            tiles.append(jnp.where(visible, s, -1e30) if i == j else s)
        top = tiles[0]
        for s in tiles[1:]:
            top = jnp.maximum(top, s)
        top = jnp.max(top, axis=0, keepdims=True)
        total = None
        acc = None
        for i, s in enumerate(tiles):
            p = jnp.exp2(s - top)
            total = p if total is None else total + p
            term = nn(vt_ref[:, i * BLOCK : (i + 1) * BLOCK], p.astype(B16))
            acc = term if acc is None else acc + term
        total = jnp.sum(total, axis=0, keepdims=True)
        ot = acc * (1.0 / total)
        oc = ot.T.astype(B16)
        ob = ot.astype(B16)
        for t in range(2):
            rows = slice(t * TOK, (t + 1) * TOK)
            o_ref[2 * j + t] = oc[rows]
            ot_ref[2 * j + t] = ob[:, rows]
        stat_ref[0:1, first : first + BLOCK] = top + jnp.log2(total)


def forward(x):
    vmem = pl.BlockSpec(memory_space=pltpu.VMEM)
    return pl.pallas_call(
        forward_kernel,
        in_specs=[vmem],
        out_specs=[vmem, vmem, vmem],
        out_shape=[
            jax.ShapeDtypeStruct((HEADS, TOK, HEAD), B16),
            jax.ShapeDtypeStruct((HEADS, HEAD, TOK), B16),
            jax.ShapeDtypeStruct((8, LENGTH), F32),
        ],
        scratch_shapes=[pltpu.VMEM((HEAD, LENGTH), B16)],
        compiler_params=params(SMALL),
        cost_estimate=cost(0, 0),
        name="attention_forward",
    )(x)


def backward_kernel(x_ref, o_ref, ot_ref, stat_ref, out_ref, dqt_ref, delta_ref):
    visible = mask_of()
    dqt_ref[...] = jnp.zeros_like(dqt_ref)
    for t in range(HEADS):
        product = x_ref[t, 3].T.astype(F32) * ot_ref[t].astype(F32)
        delta_ref[0:1, t * TOK : (t + 1) * TOK] = jnp.sum(product, axis=0, keepdims=True)
    for i in range(BLOCKS):
        first = i * BLOCK
        k = rows_of(x_ref, 1, first, BLOCK)
        v = rows_of(x_ref, 2, first, BLOCK)
        kt = k.T
        dk = None
        dv = None
        for j in range(i, BLOCKS):
            cols = slice(j * BLOCK, (j + 1) * BLOCK)
            q = rows_of(x_ref, 0, j * BLOCK, BLOCK)
            d = rows_of(x_ref, 3, j * BLOCK, BLOCK)
            s = nt(k, q) * FACTOR2 - stat_ref[0:1, cols]
            if i == j:
                s = jnp.where(visible, s, -1e30)
            p = jnp.exp2(s)
            dp = nt(v, d) - delta_ref[0:1, cols]
            ds = (p * dp).astype(B16)
            term = nn(p.astype(B16), d)
            dv = term if dv is None else dv + term
            term = nn(ds, q)
            dk = term if dk is None else dk + term
            dqt_ref[:, cols] += nn(kt, ds)
        dk = (dk * FACTOR).astype(B16)
        dv = dv.astype(B16)
        for t in range(2):
            rows = slice(t * TOK, (t + 1) * TOK)
            out_ref[2 * i + t, 1] = dk[rows]
            out_ref[2 * i + t, 2] = dv[rows]
    for t in range(HEADS):
        part = dqt_ref[:, t * TOK : (t + 1) * TOK] * FACTOR
        out_ref[t, 0] = part.T.astype(B16)
        out_ref[t, 3] = o_ref[t]


def backward(x, o, ot, stat):
    vmem = pl.BlockSpec(memory_space=pltpu.VMEM)
    return pl.pallas_call(
        backward_kernel,
        in_specs=[vmem] * 4,
        out_specs=vmem,
        out_shape=jax.ShapeDtypeStruct((HEADS, 4, TOK, HEAD), B16),
        scratch_shapes=[pltpu.VMEM((HEAD, LENGTH), F32), pltpu.VMEM((8, LENGTH), F32)],
        compiler_params=params(SMALL),
        cost_estimate=cost(0, 0),
        name="attention_backward",
    )(x, o, ot, stat)


WEIGHT_PARTS = 4
FINISH_STEPS = 2


def finish_kernel(x_ref, o_ref, *refs):
    weights = refs[:WEIGHT_PARTS]
    y_ref, q_ref, k_ref, v_ref, lhs_ref = refs[WEIGHT_PARTS:]

    @pl.when(pl.program_id(0) == 0)
    def _():
        for h in range(HEADS):
            lhs_ref[:, h * HEAD : (h + 1) * HEAD] = o_ref[h, 0]

    for h in range(HEADS // FINISH_STEPS):
        cols = slice(h * HEAD, (h + 1) * HEAD)
        q_ref[:, cols] = x_ref[h, 0]
        k_ref[:, cols] = x_ref[h, 1]
        v_ref[:, cols] = x_ref[h, 2]
    w = jnp.concatenate([ref[...] for ref in weights], axis=0)
    y_ref[...] = nn(lhs_ref[...], w).astype(B16)


def finish(x, w):
    rows = WIDTH // WEIGHT_PARTS
    cols = WIDTH // FINISH_STEPS
    shape = jax.ShapeDtypeStruct((TOK, WIDTH), B16)
    spec = pl.BlockSpec((TOK, cols), lambda i: (0, i))
    return pl.pallas_call(
        finish_kernel,
        grid=(FINISH_STEPS,),
        in_specs=[
            pl.BlockSpec((HEADS // FINISH_STEPS, 3, TOK, HEAD), lambda i: (i, 0, 0, 0)),
            pl.BlockSpec((HEADS, 1, TOK, HEAD), lambda i: (0, 3, 0, 0)),
        ]
        + [pl.BlockSpec((rows, cols), lambda i, n=n: (n, i)) for n in range(WEIGHT_PARTS)],
        out_specs=[spec] * 4,
        out_shape=[shape] * 4,
        scratch_shapes=[pltpu.VMEM((TOK, WIDTH), B16)],
        compiler_params=params(WIDE),
        cost_estimate=cost(2 * TOK * WIDTH * WIDTH, 12 << 20),
        name="finish",
    )(x, x, *[w] * WEIGHT_PARTS)


PART = 512
SHARE = HEAD // YN
GROUP = [(0, 0), (0, 1), (1, 0), (1, 1)]


def move(x, dh=0, dy=0, dz=0, dx=0, dc=0):
    pairs = []
    for h in range(HN):
        for y in range(YN):
            for z in range(ZN):
                for a in range(XN):
                    for c in range(CN):
                        source = (((h * YN + y) * ZN + z) * XN + a) * CN + c
                        target = ((h + dh) % HN * YN + (y + dy) % YN) * ZN + (z + dz) % ZN
                        target = (target * XN + (a + dx) % XN) * CN + (c + dc) % CN
                        pairs.append((source, target))
    return lax.ppermute(x, ("dp", "seq"), pairs)


def part_of(pos_ref, dz, dc):
    return lax.rem(pos_ref[0] + dz, ZN) * CN + lax.rem(pos_ref[2] + dc, CN)


def cut_kernel(pos_ref, g_ref, *refs):
    for ref, (dz, dc) in zip(refs, GROUP):
        first = pl.multiple_of(part_of(pos_ref, dz, dc) * PART, PART)
        ref[...] = g_ref[:, pl.ds(first, PART)]


def cut(pos, g):
    vmem = pl.BlockSpec(memory_space=pltpu.VMEM)
    return pl.pallas_call(
        cut_kernel,
        in_specs=[pl.BlockSpec(memory_space=pltpu.SMEM), vmem],
        out_specs=[vmem] * 4,
        out_shape=[jax.ShapeDtypeStruct((TOK, PART), B16)] * 4,
        compiler_params=params(SMALL),
        cost_estimate=cost(0, 1 << 20),
        name="cut",
    )(pos, g)


def join_rows_kernel(a_ref, b_ref, c_ref, d_ref, out_ref):
    for n, ref in enumerate((a_ref, b_ref, c_ref, d_ref)):
        out_ref[n * TOK : (n + 1) * TOK] = ref[...]


def join_rows(parts):
    vmem = pl.BlockSpec(memory_space=pltpu.VMEM)
    return pl.pallas_call(
        join_rows_kernel,
        in_specs=[vmem] * 4,
        out_specs=vmem,
        out_shape=jax.ShapeDtypeStruct((4 * TOK, PART), B16),
        compiler_params=params(SMALL),
        cost_estimate=cost(0, 1 << 20),
        name="join_rows",
    )(*parts)


def stack(parts):
    def body(*refs):
        for n in range(XN):
            refs[XN][n * 4 * TOK : (n + 1) * 4 * TOK] = refs[n][...]

    vmem = pl.BlockSpec(memory_space=pltpu.VMEM)
    return pl.pallas_call(
        body,
        in_specs=[vmem] * XN,
        out_specs=vmem,
        out_shape=jax.ShapeDtypeStruct((LENGTH, PART), B16),
        compiler_params=params(SMALL),
        cost_estimate=cost(0, STACK_COST << 20),
        name="stack",
    )(*parts)


STACK_COST = 100


def weight_kernel(pos_ref, *refs):
    heads, rhs_ref, shares = refs[:4], refs[4], refs[5:9]
    lhs_ref, total_ref = refs[9:]
    for dx in range(XN):
        for n, (dz, dc) in enumerate(GROUP):
            z = lax.rem(pos_ref[0] + dz, ZN)
            x = lax.rem(pos_ref[1] + dx, XN)
            c = lax.rem(pos_ref[2] + dc, CN)
            block = (z * XN + x) * CN + c
            at = (dx * 4 + n) * TOK
            for m, ref in enumerate(heads):
                lhs_ref[m * HEAD : (m + 1) * HEAD, at : at + TOK] = ref[block]
    total_ref[...] = nn(lhs_ref[...], rhs_ref[...])
    y = pos_ref[3]
    for r, ref in enumerate(shares):
        first = lax.rem(y + r, YN) * SHARE
        for m in range(4):
            at = pl.multiple_of(m * HEAD + first, SHARE)
            ref[m] = total_ref[pl.ds(at, SHARE), :].astype(ref.dtype)


def weight_partial(pos, heads, rows):
    vmem = pl.BlockSpec(memory_space=pltpu.VMEM)
    shape = (4, SHARE, PART)
    return pl.pallas_call(
        weight_kernel,
        in_specs=[pl.BlockSpec(memory_space=pltpu.SMEM)] + [vmem] * 5,
        out_specs=[vmem] * 4,
        out_shape=[jax.ShapeDtypeStruct(shape, F32)]
        + [jax.ShapeDtypeStruct(shape, B16)] * 3,
        scratch_shapes=[pltpu.VMEM((4 * HEAD, LENGTH), B16), pltpu.VMEM((4 * HEAD, PART), F32)],
        compiler_params=params(SMALL),
        cost_estimate=cost(2 * LENGTH * HEAD * WIDTH, 5 << 20),
        name="weight_partial",
    )(pos, *heads, rows)


def sum_shares_kernel(mine_ref, a_ref, b_ref, c_ref, *out_refs):
    for m, ref in enumerate(out_refs):
        total = mine_ref[m] + a_ref[m].astype(F32)
        ref[...] = (total + b_ref[m].astype(F32) + c_ref[m].astype(F32)).astype(B16)


def sum_shares(mine, a, b, c):
    vmem = pl.BlockSpec(memory_space=pltpu.VMEM)
    return pl.pallas_call(
        sum_shares_kernel,
        in_specs=[vmem] * 4,
        out_specs=[vmem] * 4,
        out_shape=[jax.ShapeDtypeStruct((SHARE, PART), B16)] * 4,
        compiler_params=params(SMALL),
        cost_estimate=cost(0, 1 << 20),
        name="sum_shares",
    )(mine, a, b, c)


def row_kernel(pos_ref, *refs):
    out_ref = refs[8]
    for n, (dz, dc) in enumerate(GROUP):
        first = pl.multiple_of(part_of(pos_ref, dz, dc) * PART, PART)
        total = refs[n][...].astype(F32) + refs[4 + n][...].astype(F32)
        out_ref[:, pl.ds(first, PART)] = total.astype(B16)


def make_rows(pos, near, far):
    vmem = pl.BlockSpec(memory_space=pltpu.VMEM)
    return pl.pallas_call(
        row_kernel,
        in_specs=[pl.BlockSpec(memory_space=pltpu.SMEM)] + [vmem] * 8,
        out_specs=vmem,
        out_shape=jax.ShapeDtypeStruct((SHARE, WIDTH), B16),
        compiler_params=params(SMALL),
        cost_estimate=cost(0, 1 << 20),
        name="make_rows",
    )(pos, *near, *far)


def join_kernel(pos_ref, mine_ref, one_ref, two_ref, three_ref, out_ref):
    y = pos_ref[3]
    for r, ref in enumerate((mine_ref, one_ref, two_ref, three_ref)):
        first = pl.multiple_of(lax.rem(y + YN - r, YN) * SHARE, SHARE)
        out_ref[pl.ds(first, SHARE), :] = ref[...].astype(F32)


def join_shares(pos, shares):
    vmem = pl.BlockSpec(memory_space=pltpu.VMEM)
    return pl.pallas_call(
        join_kernel,
        in_specs=[pl.BlockSpec(memory_space=pltpu.SMEM)] + [vmem] * 4,
        out_specs=vmem,
        out_shape=jax.ShapeDtypeStruct((HEAD, WIDTH), F32),
        compiler_params=params(SMALL),
        cost_estimate=cost(0, 2 << 20),
        name="join_shares",
    )(pos, *shares)


def share_over_dp(pos, mine, one, two, three):
    totals = sum_shares(mine, move(one, dy=1), move(two, dy=2), move(three, dy=3))
    near, far = [], []
    for (dz, dc), total in zip(GROUP, totals):
        near.append(total if dz + dc == 0 else move(total, dz=dz, dc=dc))
        far.append(move(total, dh=1, dz=dz, dc=dc))
    share = make_rows(pos, near, far)
    return [share] + [move(share, dy=r) for r in range(1, YN)]


def to_heads(x):
    return lax.all_to_all(x, "seq", split_axis=0, concat_axis=0, tiled=True)


def tie(*arrays):
    return lax.optimization_barrier(arrays)


def on_device(queries, keys, values, out_weight, out_grad):
    s = lax.axis_index("seq")
    y = lax.rem(lax.axis_index("dp"), YN)
    pos = jnp.stack([s // (XN * CN), lax.rem(s // CN, XN), lax.rem(s, CN), y]).astype(jnp.int32)
    q, k, v, g = (a.reshape(TOK, WIDTH) for a in (queries, keys, values, out_grad))
    cuts = cut(pos, g)
    parts = [cuts[0]] + [move(cuts[n], dz=GROUP[n][0], dc=GROUP[n][1]) for n in range(1, 4)]
    packed, *parts = tie(pack(q, k, v, g, out_weight), *parts)
    rows = join_rows(parts)
    x = to_heads(packed)
    x, rows = tie(x, rows)
    rows_near, rows_before = move(rows, dx=-1), move(rows, dx=-3)
    rows_far = move(rows, dx=-2)
    o, ot, stat = forward(x)
    beside = move(ot, dc=1)
    over = move(ot, dz=1)
    grads = backward(x, o, ot, stat)
    rows_near, rows_before, rows_far, grads = tie(rows_near, rows_before, rows_far, grads)
    rows = stack([rows, rows_near, rows_far, rows_before])
    over, beside, rows = tie(over, beside, rows)
    heads = [ot, beside, over, move(over, dc=1)]
    shares = weight_partial(pos, heads, rows)
    grads, *shares = tie(grads, *shares)
    share = share_over_dp(pos, *shares)
    results = to_heads(grads)
    layer_out, grad_q, grad_k, grad_v = finish(results, out_weight)
    layer_out, *share = tie(layer_out, *share)
    grad_weight = join_shares(pos, share)
    shape = (1, TOK, WIDTH)
    return (
        layer_out.reshape(shape),
        grad_q.reshape(shape),
        grad_k.reshape(shape),
        grad_v.reshape(shape),
        grad_weight,
    )


def solution(mesh):
    tokens = P("dp", "seq", None)
    return jax.shard_map(
        on_device,
        mesh=mesh,
        in_specs=(tokens, tokens, tokens, P(), tokens),
        out_specs=(tokens, tokens, tokens, tokens, P("seq", None)),
        check_vma=False,
    )
```

time: 156 us -> 127 us (0.81); the launches traced: 154 us -> 127 us
  local copies, waits for them, and re-layouts: 15.8 us -> 2.4 us
  Pallas kernels: 41.8 us -> 32.2 us
  starting transfers between devices: 42.4 us -> 39.8 us
    ppermute x18 -> x22, waiting for transfers between devices: 52.8 us -> 23.3 us  [move(): return lax.ppermute(x, ('dp', 'seq'), pairs)]
    all_to_all x3 -> x2, waiting for transfers between devices: 0.01 us -> 28.6 us  [to_heads(): return lax.all_to_all(x, 'seq', split_axis=0, concat_axis=0, tiled=True)]
    unnamed x36 -> x4, local copies, waits for them, and re-layouts: 14.3 us -> 2.4 us
    pallas_call x7 -> x10, Pallas kernels: 40.2 us -> 30.6 us  [the longest x1 10 us: backward(): pl.pallas_call(backward_kernel, in_specs=[vmem] * 4, out_specs=vmem, out_...]
    all_to_all x3 -> x2, starting transfers between devices: 17.7 us -> 11.6 us  [to_heads(): return lax.all_to_all(x, 'seq', split_axis=0, concat_axis=0, tiled=True)]
    ppermute x18 -> x22, starting transfers between devices: 24.7 us -> 28.2 us  [move(): return lax.ppermute(x, ('dp', 'seq'), pairs)]
  transfers between devices with their start and end apart: 21 -> 24, of which waited for: 7 -> 9; matrix products, arithmetic and copies ran while one was open for 1% -> 0% of each run, Pallas kernels for 20% -> 22%
where the time goes in v2:
time: 127 us
  waiting for transfers between devices  51.9 us (41%)
  starting transfers between devices  39.8 us (31%)
  Pallas kernels  32.2 us (25%)
  local copies, waits for them, and re-layouts  2.4 us (2%)
    all_to_all x2, waiting for transfers between devices, to_heads(): return lax.all_to_all(x, 'seq', split_axis=0, concat_axis=0, tiled=True)  28.6 us
    ppermute x22, starting transfers between devices, move(): return lax.ppermute(x, ('dp', 'seq'), pairs)  28.2 us
    ppermute x22, waiting for transfers between devices, move(): return lax.ppermute(x, ('dp', 'seq'), pairs)  23.3 us
    all_to_all x2, starting transfers between devices, to_heads(): return lax.all_to_all(x, 'seq', split_axis=0, concat_axis=0, tiled=True)  11.6 us
    pallas_call x1, Pallas kernels, backward(): pl.pallas_call(backward_kernel, in_specs=[vmem] * 4, out_specs=vmem, out_...  10 us
    pallas_call x1, Pallas kernels, pack(): pl.pallas_call(pack_kernel, grid=(HEADS // PACK_HEADS,), in_specs=[part,...  7.02 us
    pallas_call x1, Pallas kernels, finish(): pl.pallas_call(finish_kernel, grid=(FINISH_STEPS,), in_specs=[pl.BlockSpe...  5.6 us
    pallas_call x1, Pallas kernels, forward(): pl.pallas_call(forward_kernel, in_specs=[vmem], out_specs=[vmem, vmem, vm...  4.65 us
  transfers between devices with their start and end apart: 24, of which 9 were waited for; matrix products, arithmetic and copies ran while one was open for 0% of the time, Pallas kernels for 22%

profile of v2, /device:TPU:2, one launch (start us, length us, event | category | flops | bytes accessed | tf_op | source)
XLA Modules:
  0.0 127.2 jit_solution(206852353406549080)
XLA Ops:
  0.7 0.1 pad_add_fusion.pos_ref
  0.7 0.0 copy-start
  0.7 1.0 copy-done
  1.8 0.6 cut.1
  2.4 0.1 collective-permute-start
  2.5 2.0 %collective-permute-start.1 = (bf16[128,512]{1,0:T(8,128)(2,1)S(1)}, bf16[128,512]{1,0:T(8,128)(2,1)S(1)}, u32[]{:S(2)}, u32[]{:S(2)}) collective-permute-start(bf16[128,512]{1,0:T(8,128)(2,1)S(1)} %get-tuple-element.50), channel_id=1, source_target_pairs={{0,8},{1,9},{2,10},{3,11},{4,12},{5,13},{6,14},{7,15},{8,0},{9,1},... | collective-permute-start | bytes 393224 | tf_op jit(solution)/shard_map/ppermute | solution.py:252
  4.5 0.1 collective-permute-start.2
  4.5 7.0 %pack.1 = bf16[16,4,128,128]{3,2,1,0:T(8,128)(2,1)} custom-call(bf16[128,2048]{1,0:T(8,128)(2,1)} %bitcast.14, bf16[128,2048]{1,0:T(8,128)(2,1)} %bitcast.15, bf16[128,2048]{1,0:T(8,128)(2,1)} %bitcast.16, bf16[128,2048]{1,0:T(8,128)(2,1)} %bitcast.12, bf16[2048,2048]{1,0:T(8,128)(2,1)} %refs_3_.3, bf16[2048,2048]{1,0:T(8,128)(2,1)} %refs_3_.3, ...), custom_call_target="tpu_custom_call" | custom-call | flops 1073741824 | bytes 12582912 | tf_op jit(solution)/shard_map/pack/pallas_call | solution.py:59
  11.5 0.0 collective-permute-done.b_ref
  11.5 0.0 collective-permute-done.1.c_ref
  11.6 0.0 collective-permute-done.2.d_ref
  11.6 6.0 %all-to-all-start = ((bf16[16,4,128,128]{3,2,1,0:T(8,128)(2,1)}), bf16[16,4,128,128]{3,2,1,0:T(8,128)(2,1)S(1)}, u32[]{:S(2)}, u32[]{:S(2)}) async-start(bf16[16,4,128,128]{3,2,1,0:T(8,128)(2,1)} %pack.1), calls=%async_computation | async-start | bytes 4194304 | tf_op jit(solution)/shard_map/all_to_all | solution.py:424
  17.6 28.6 %all-to-all-done.x_ref = bf16[16,4,128,128]{3,2,1,0:T(8,128)(2,1)S(1)} async-done(((bf16[16,4,128,128]{3,2,1,0:T(8,128)(2,1)}), bf16[16,4,128,128]{3,2,1,0:T(8,128)(2,1)S(1)}, u32[]{:S(2)}, u32[]{:S(2)}) %all-to-all-start) | async-done | bytes 2097184 | tf_op jit(solution)/shard_map/all_to_all | solution.py:424
  46.2 0.0 collective-permute-start.3
  46.2 2.0 %collective-permute-start.4 = (bf16[512,512]{1,0:T(8,128)(2,1)S(1)}, bf16[512,512]{1,0:T(8,128)(2,1)S(1)}, u32[]{:S(2)}, u32[]{:S(2)}) collective-permute-start(bf16[512,512]{1,0:T(8,128)(2,1)S(1)} %join_rows.1.refs_0_), channel_id=1, source_target_pairs={{0,2},{1,3},{2,4},{3,5},{4,6},{5,7},{6,0},{7,1},{8,10},{9,11},{10,... | collective-permute-start | bytes 1572872 | tf_op jit(solution)/shard_map/ppermute | solution.py:252
  48.3 0.4 collective-permute-start.5
  48.6 4.6 %attention_forward.1 = (bf16[16,128,128]{2,1,0:T(8,128)(2,1)S(1)}, bf16[16,128,128]{2,1,0:T(8,128)(2,1)S(1)}, f32[8,2048]{1,0:T(8,128)S(1)}) custom-call(bf16[16,4,128,128]{3,2,1,0:T(8,128)(2,1)S(1)} %all-to-all-done.x_ref), custom_call_target="tpu_custom_call" | custom-call | tf_op jit(solution)/shard_map/attention_forward/pallas_call | solution.py:122
  53.3 1.3 %collective-permute-start.6 = (bf16[16,128,128]{2,1,0:T(8,128)(2,1)S(1)}, bf16[16,128,128]{2,1,0:T(8,128)(2,1)S(1)}, u32[]{:S(2)}, u32[]{:S(2)}) collective-permute-start(bf16[16,128,128]{2,1,0:T(8,128)(2,1)S(1)} %get-tuple-element.60.ot_ref.refs_0_), channel_id=1, source_target_pairs={{0,8},{1,9},{2,10},{3,11},{4,12},{5,13},{6,14},{7,15},{8,0},{9,1},... | collective-permute-start | bytes 1572872 | tf_op jit(solution)/shard_map/ppermute | solution.py:252
  54.6 0.0 collective-permute-start.7
  54.6 10.0 %attention_backward.1 = bf16[16,4,128,128]{3,2,1,0:T(8,128)(2,1)} custom-call(bf16[16,4,128,128]{3,2,1,0:T(8,128)(2,1)S(1)} %all-to-all-done.x_ref, bf16[16,128,128]{2,1,0:T(8,128)(2,1)S(1)} %get-tuple-element.59.o_ref, bf16[16,128,128]{2,1,0:T(8,128)(2,1)S(1)} %get-tuple-element.60.ot_ref.refs_0_, f32[8,2048]{1,0:T(8,128)S(1)} %get-tuple-element.61.stat_ref), custom_call_target="tpu_custom_call" | custom-call | tf_op jit(solution)/shard_map/attention_backward/pallas_call | solution.py:180
  64.7 6.6 %collective-permute-done.3.refs_1_ = bf16[512,512]{1,0:T(8,128)(2,1)S(1)} collective-permute-done((bf16[512,512]{1,0:T(8,128)(2,1)S(1)}, bf16[512,512]{1,0:T(8,128)(2,1)S(1)}, u32[]{:S(2)}, u32[]{:S(2)}) %collective-permute-start.3) | collective-permute-done | bytes 524320 | tf_op jit(solution)/shard_map/ppermute | solution.py:252
  71.2 0.0 collective-permute-done.4.refs_3_
  71.2 0.0 collective-permute-done.5.refs_2_
  71.2 0.1 stack.21.refs_4_
  71.4 0.0 collective-permute-done.6.refs_2_
  71.4 0.0 collective-permute-done.7.refs_1_
  71.4 0.1 collective-permute-start.8
  71.5 1.9 %collective-permute-done.8.refs_3_ = bf16[16,128,128]{2,1,0:T(8,128)(2,1)S(1)} collective-permute-done((bf16[16,128,128]{2,1,0:T(8,128)(2,1)S(1)}, bf16[16,128,128]{2,1,0:T(8,128)(2,1)S(1)}, u32[]{:S(2)}, u32[]{:S(2)}) %collective-permute-start.8) | collective-permute-done | bytes 524320 | tf_op jit(solution)/shard_map/ppermute | solution.py:252
  73.4 1.9 %weight_partial.1 = (f32[4,32,512]{2,1,0:T(8,128)S(1)}, bf16[4,32,512]{2,1,0:T(8,128)(2,1)S(1)}, bf16[4,32,512]{2,1,0:T(8,128)(2,1)S(1)}, bf16[4,32,512]{2,1,0:T(8,128)(2,1)S(1)}) custom-call(s32[4]{0:T(128)S(1)} %pad_add_fusion.pos_ref, bf16[16,128,128]{2,1,0:T(8,128)(2,1)S(1)} %get-tuple-element.60.ot_ref.refs_0_, ...), custom_call_target="tpu_custom_call" | custom-call | flops 1073741824 | bytes 5242880 | tf_op jit(solution)/shard_map/weight_partial/pallas_call | solution.py:340
  75.3 5.6 %all-to-all-start.1 = ((bf16[16,4,128,128]{3,2,1,0:T(8,128)(2,1)}), bf16[16,4,128,128]{3,2,1,0:T(8,128)(2,1)S(1)}, u32[]{:S(2)}, u32[]{:S(2)}) async-start(bf16[16,4,128,128]{3,2,1,0:T(8,128)(2,1)} %attention_backward.1), calls=%async_computation.1 | async-start | bytes 4194304 | tf_op jit(solution)/shard_map/all_to_all | solution.py:424
  80.9 3.2 %collective-permute-start.10 = (bf16[4,32,512]{2,1,0:T(8,128)(2,1)S(1)}, bf16[4,32,512]{2,1,0:T(8,128)(2,1)S(1)}, u32[]{:S(2)}, u32[]{:S(2)}) collective-permute-start(bf16[4,32,512]{2,1,0:T(8,128)(2,1)S(1)} %get-tuple-element.77), channel_id=1, source_target_pairs={{0,32},{1,33},{2,34},{3,35},{4,36},{5,37},{6,38},{7,39},{8,40},{9,... | collective-permute-start | bytes 393224 | tf_op jit(solution)/shard_map/ppermute | solution.py:252
  84.1 1.0 collective-permute-start.11
  85.1 1.0 collective-permute-start.9
  86.1 2.4 %collective-permute-done.10.b_ref = bf16[4,32,512]{2,1,0:T(8,128)(2,1)S(1)} collective-permute-done((bf16[4,32,512]{2,1,0:T(8,128)(2,1)S(1)}, bf16[4,32,512]{2,1,0:T(8,128)(2,1)S(1)}, u32[]{:S(2)}, u32[]{:S(2)}) %collective-permute-start.10) | collective-permute-done | bytes 131104 | tf_op jit(solution)/shard_map/ppermute | solution.py:252
  88.5 2.6 %collective-permute-done.11.c_ref = bf16[4,32,512]{2,1,0:T(8,128)(2,1)S(1)} collective-permute-done((bf16[4,32,512]{2,1,0:T(8,128)(2,1)S(1)}, bf16[4,32,512]{2,1,0:T(8,128)(2,1)S(1)}, u32[]{:S(2)}, u32[]{:S(2)}) %collective-permute-start.11) | collective-permute-done | bytes 131104 | tf_op jit(solution)/shard_map/ppermute | solution.py:252
  91.1 0.2 collective-permute-done.9.a_ref
  91.3 0.1 sum_shares.1
  91.4 0.1 collective-permute-start.12
  91.5 1.6 %collective-permute-start.13 = (bf16[32,512]{1,0:T(8,128)(2,1)S(1)}, bf16[32,512]{1,0:T(8,128)(2,1)S(1)}, u32[]{:S(2)}, u32[]{:S(2)}) collective-permute-start(bf16[32,512]{1,0:T(8,128)(2,1)S(1)} %get-tuple-element.81), channel_id=1, source_target_pairs={{0,8},{1,9},{2,10},{3,11},{4,12},{5,13},{6,14},{7,15},{8,0},{9,1},... | collective-permute-start | bytes 98312 | tf_op jit(solution)/shard_map/ppermute | solution.py:252
  93.1 3.4 %collective-permute-start.16 = (bf16[32,512]{1,0:T(8,128)(2,1)S(1)}, bf16[32,512]{1,0:T(8,128)(2,1)S(1)}, u32[]{:S(2)}, u32[]{:S(2)}) collective-permute-start(bf16[32,512]{1,0:T(8,128)(2,1)S(1)} %get-tuple-element.80), channel_id=1, source_target_pairs={{0,65},{1,64},{2,67},{3,66},{4,69},{5,68},{6,71},{7,70},{8,73},{9,... | collective-permute-start | bytes 98312 | tf_op jit(solution)/shard_map/ppermute | solution.py:252
  96.5 0.0 collective-permute-start.14
  96.5 1.0 collective-permute-start.15
  97.5 0.0 collective-permute-done.12.refs_1_
  97.5 3.7 %collective-permute-start.17 = (bf16[32,512]{1,0:T(8,128)(2,1)S(1)}, bf16[32,512]{1,0:T(8,128)(2,1)S(1)}, u32[]{:S(2)}, u32[]{:S(2)}) collective-permute-start(bf16[32,512]{1,0:T(8,128)(2,1)S(1)} %get-tuple-element.81), channel_id=1, source_target_pairs={{0,72},{1,73},{2,74},{3,75},{4,76},{5,77},{6,78},{7,79},{8,64},{9,... | collective-permute-start | bytes 98312 | tf_op jit(solution)/shard_map/ppermute | solution.py:252
  101.1 6.1 %collective-permute-done.13.refs_2_ = bf16[32,512]{1,0:T(8,128)(2,1)S(1)} collective-permute-done((bf16[32,512]{1,0:T(8,128)(2,1)S(1)}, bf16[32,512]{1,0:T(8,128)(2,1)S(1)}, u32[]{:S(2)}, u32[]{:S(2)}) %collective-permute-start.13) | collective-permute-done | bytes 32800 | tf_op jit(solution)/shard_map/ppermute | solution.py:252
  107.2 1.4 %collective-permute-start.18 = (bf16[32,512]{1,0:T(8,128)(2,1)S(1)}, bf16[32,512]{1,0:T(8,128)(2,1)S(1)}, u32[]{:S(2)}, u32[]{:S(2)}) collective-permute-start(bf16[32,512]{1,0:T(8,128)(2,1)S(1)} %get-tuple-element.82), channel_id=1, source_target_pairs={{0,73},{1,72},{2,75},{3,74},{4,77},{5,76},{6,79},{7,78},{8,65},{9,... | collective-permute-start | bytes 98312 | tf_op jit(solution)/shard_map/ppermute | solution.py:252
  108.6 0.0 collective-permute-done.14.refs_3_
  108.6 2.3 %collective-permute-done.15.refs_4_ = bf16[32,512]{1,0:T(8,128)(2,1)S(1)} collective-permute-done((bf16[32,512]{1,0:T(8,128)(2,1)S(1)}, bf16[32,512]{1,0:T(8,128)(2,1)S(1)}, u32[]{:S(2)}, u32[]{:S(2)}) %collective-permute-start.15) | collective-permute-done | bytes 32800 | tf_op jit(solution)/shard_map/ppermute | solution.py:252
  110.9 0.0 collective-permute-done.16.refs_5_
  110.9 0.0 collective-permute-done.17.refs_6_
  111.0 1.2 collective-permute-done.18.refs_7_
  112.1 0.6 make_rows.1.mine_ref
  112.7 1.7 %collective-permute-start.19 = (bf16[32,2048]{1,0:T(8,128)(2,1)S(1)}, bf16[32,2048]{1,0:T(8,128)(2,1)S(1)}, u32[]{:S(2)}, u32[]{:S(2)}) collective-permute-start(bf16[32,2048]{1,0:T(8,128)(2,1)S(1)} %make_rows.1.mine_ref), channel_id=1, source_target_pairs={{0,16},{1,17},{2,18},{3,19},{4,20},{5,21},{6,22},{7,23},{8,24},{9,... | collective-permute-start | bytes 393224 | tf_op jit(solution)/shard_map/ppermute | solution.py:252
  114.4 2.9 %collective-permute-start.20 = (bf16[32,2048]{1,0:T(8,128)(2,1)S(1)}, bf16[32,2048]{1,0:T(8,128)(2,1)S(1)}, u32[]{:S(2)}, u32[]{:S(2)}) collective-permute-start(bf16[32,2048]{1,0:T(8,128)(2,1)S(1)} %make_rows.1.mine_ref), channel_id=1, source_target_pairs={{0,32},{1,33},{2,34},{3,35},{4,36},{5,37},{6,38},{7,39},{8,40},{9,... | collective-permute-start | bytes 393224 | tf_op jit(solution)/shard_map/ppermute | solution.py:252
  117.2 1.3 %collective-permute-start.21 = (bf16[32,2048]{1,0:T(8,128)(2,1)S(1)}, bf16[32,2048]{1,0:T(8,128)(2,1)S(1)}, u32[]{:S(2)}, u32[]{:S(2)}) collective-permute-start(bf16[32,2048]{1,0:T(8,128)(2,1)S(1)} %make_rows.1.mine_ref), channel_id=1, source_target_pairs={{0,48},{1,49},{2,50},{3,51},{4,52},{5,53},{6,54},{7,55},{8,56},{9,... | collective-permute-start | bytes 393224 | tf_op jit(solution)/shard_map/ppermute | solution.py:252
  118.6 0.0 all-to-all-done.1.x_ref.o_ref
  118.6 0.0 copy-start.1
  118.6 1.4 %copy-done.1 = bf16[16,4,128,128]{3,2,1,0:T(8,128)(2,1)} copy-done((bf16[16,4,128,128]{3,2,1,0:T(8,128)(2,1)}, bf16[16,4,128,128]{3,2,1,0:T(8,128)(2,1)S(1)}, u32[]{:S(2)}) %copy-start.1) | copy-done | bytes 2097176
  120.0 5.6 %finish.1 = (bf16[128,2048]{1,0:T(8,128)(2,1)}, bf16[128,2048]{1,0:T(8,128)(2,1)}, bf16[128,2048]{1,0:T(8,128)(2,1)}, bf16[128,2048]{1,0:T(8,128)(2,1)}) custom-call(bf16[16,4,128,128]{3,2,1,0:T(8,128)(2,1)} %copy-done.1, bf16[16,4,128,128]{3,2,1,0:T(8,128)(2,1)} %copy-done.1, bf16[2048,2048]{1,0:T(8,128)(2,1)} %refs_3_.3, bf16[2048,2048]{1,0:T(8,128)(2,1)} %refs_3_.3, ...), custom_call_target="tpu_custom_call" | custom-call | flops 1073741824 | bytes 12582912 | tf_op jit(solution)/shard_map/finish/pallas_call | solution.py:219
  125.6 0.0 collective-permute-done.19.one_ref
  125.6 0.0 collective-permute-done.20.two_ref
  125.6 0.0 collective-permute-done.21.three_ref
  125.6 1.6 %join_shares.1 = f32[128,2048]{1,0:T(8,128)} custom-call(s32[4]{0:T(128)S(1)} %pad_add_fusion.pos_ref, bf16[32,2048]{1,0:T(8,128)(2,1)S(1)} %make_rows.1.mine_ref, bf16[32,2048]{1,0:T(8,128)(2,1)S(1)} %collective-permute-done.19.one_ref, bf16[32,2048]{1,0:T(8,128)(2,1)S(1)} %collective-permute-done.20.two_ref, ...), custom_call_target="tpu_custom_call" | custom-call | bytes 2097152 | tf_op jit(solution)/shard_map/join_shares/pallas_call | solution.py:402
  (1 shorter events, 0.0 us)
Async XLA Ops:
  0.7 1.0 copy-start
  2.4 9.2 %collective-permute-start = (bf16[128,512]{1,0:T(8,128)(2,1)S(1)}, bf16[128,512]{1,0:T(8,128)(2,1)S(1)}, u32[]{:S(2)}, u32[]{:S(2)}) collective-permute-start(bf16[128,512]{1,0:T(8,128)(2,1)S(1)} %get-tuple-element.49), channel_id=1, source_target_pairs={{0,1},{1,0},{2,3},{3,2},{4,5},{5,4},{6,7},{7,6},{8,9},{9,8},{10,11... | collective-permute-start | bytes 393224 | tf_op jit(solution)/shard_map/ppermute | solution.py:252
  2.5 9.1 %collective-permute-start.1 = (bf16[128,512]{1,0:T(8,128)(2,1)S(1)}, bf16[128,512]{1,0:T(8,128)(2,1)S(1)}, u32[]{:S(2)}, u32[]{:S(2)}) collective-permute-start(bf16[128,512]{1,0:T(8,128)(2,1)S(1)} %get-tuple-element.50), channel_id=1, source_target_pairs={{0,8},{1,9},{2,10},{3,11},{4,12},{5,13},{6,14},{7,15},{8,0},{9,1},... | collective-permute-start | bytes 393224 | tf_op jit(solution)/shard_map/ppermute | solution.py:252
  4.5 7.1 %collective-permute-start.2 = (bf16[128,512]{1,0:T(8,128)(2,1)S(1)}, bf16[128,512]{1,0:T(8,128)(2,1)S(1)}, u32[]{:S(2)}, u32[]{:S(2)}) collective-permute-start(bf16[128,512]{1,0:T(8,128)(2,1)S(1)} %get-tuple-element.51), channel_id=1, source_target_pairs={{0,9},{1,8},{2,11},{3,10},{4,13},{5,12},{6,15},{7,14},{8,1},{9,0},... | collective-permute-start | bytes 393224 | tf_op jit(solution)/shard_map/ppermute | solution.py:252
  11.6 34.7 %all-to-all-start = ((bf16[16,4,128,128]{3,2,1,0:T(8,128)(2,1)}), bf16[16,4,128,128]{3,2,1,0:T(8,128)(2,1)S(1)}, u32[]{:S(2)}, u32[]{:S(2)}) async-start(bf16[16,4,128,128]{3,2,1,0:T(8,128)(2,1)} %pack.1), calls=%async_computation | async-start | bytes 4194304 | tf_op jit(solution)/shard_map/all_to_all | solution.py:424
  46.2 25.0 %collective-permute-start.3 = (bf16[512,512]{1,0:T(8,128)(2,1)S(1)}, bf16[512,512]{1,0:T(8,128)(2,1)S(1)}, u32[]{:S(2)}, u32[]{:S(2)}) collective-permute-start(bf16[512,512]{1,0:T(8,128)(2,1)S(1)} %join_rows.1.refs_0_), channel_id=1, source_target_pairs={{0,6},{1,7},{2,0},{3,1},{4,2},{5,3},{6,4},{7,5},{8,14},{9,15},{10,... | collective-permute-start | bytes 1572872 | tf_op jit(solution)/shard_map/ppermute | solution.py:252
  46.2 25.0 %collective-permute-start.4 = (bf16[512,512]{1,0:T(8,128)(2,1)S(1)}, bf16[512,512]{1,0:T(8,128)(2,1)S(1)}, u32[]{:S(2)}, u32[]{:S(2)}) collective-permute-start(bf16[512,512]{1,0:T(8,128)(2,1)S(1)} %join_rows.1.refs_0_), channel_id=1, source_target_pairs={{0,2},{1,3},{2,4},{3,5},{4,6},{5,7},{6,0},{7,1},{8,10},{9,11},{10,... | collective-permute-start | bytes 1572872 | tf_op jit(solution)/shard_map/ppermute | solution.py:252
  48.3 23.0 %collective-permute-start.5 = (bf16[512,512]{1,0:T(8,128)(2,1)S(1)}, bf16[512,512]{1,0:T(8,128)(2,1)S(1)}, u32[]{:S(2)}, u32[]{:S(2)}) collective-permute-start(bf16[512,512]{1,0:T(8,128)(2,1)S(1)} %join_rows.1.refs_0_), channel_id=1, source_target_pairs={{0,4},{1,5},{2,6},{3,7},{4,0},{5,1},{6,2},{7,3},{8,12},{9,13},{10,... | collective-permute-start | bytes 1572872 | tf_op jit(solution)/shard_map/ppermute | solution.py:252
  53.3 18.1 %collective-permute-start.6 = (bf16[16,128,128]{2,1,0:T(8,128)(2,1)S(1)}, bf16[16,128,128]{2,1,0:T(8,128)(2,1)S(1)}, u32[]{:S(2)}, u32[]{:S(2)}) collective-permute-start(bf16[16,128,128]{2,1,0:T(8,128)(2,1)S(1)} %get-tuple-element.60.ot_ref.refs_0_), channel_id=1, source_target_pairs={{0,8},{1,9},{2,10},{3,11},{4,12},{5,13},{6,14},{7,15},{8,0},{9,1},... | collective-permute-start | bytes 1572872 | tf_op jit(solution)/shard_map/ppermute | solution.py:252
  54.6 16.8 %collective-permute-start.7 = (bf16[16,128,128]{2,1,0:T(8,128)(2,1)S(1)}, bf16[16,128,128]{2,1,0:T(8,128)(2,1)S(1)}, u32[]{:S(2)}, u32[]{:S(2)}) collective-permute-start(bf16[16,128,128]{2,1,0:T(8,128)(2,1)S(1)} %get-tuple-element.60.ot_ref.refs_0_), channel_id=1, source_target_pairs={{0,1},{1,0},{2,3},{3,2},{4,5},{5,4},{6,7},{7,6},{8,9},{9,8},{10,11... | collective-permute-start | bytes 1572872 | tf_op jit(solution)/shard_map/ppermute | solution.py:252
  71.4 2.0 %collective-permute-start.8 = (bf16[16,128,128]{2,1,0:T(8,128)(2,1)S(1)}, bf16[16,128,128]{2,1,0:T(8,128)(2,1)S(1)}, u32[]{:S(2)}, u32[]{:S(2)}) collective-permute-start(bf16[16,128,128]{2,1,0:T(8,128)(2,1)S(1)} %collective-permute-done.6.refs_2_), channel_id=1, source_target_pairs={{0,1},{1,0},{2,3},{3,2},{4,5},{5,4},{6,7},{7,6},{8,9},{9,8},{10,11... | collective-permute-start | bytes 1572872 | tf_op jit(solution)/shard_map/ppermute | solution.py:252
  75.3 43.3 %all-to-all-start.1 = ((bf16[16,4,128,128]{3,2,1,0:T(8,128)(2,1)}), bf16[16,4,128,128]{3,2,1,0:T(8,128)(2,1)S(1)}, u32[]{:S(2)}, u32[]{:S(2)}) async-start(bf16[16,4,128,128]{3,2,1,0:T(8,128)(2,1)} %attention_backward.1), calls=%async_computation.1 | async-start | bytes 4194304 | tf_op jit(solution)/shard_map/all_to_all | solution.py:424
  80.9 7.7 %collective-permute-start.10 = (bf16[4,32,512]{2,1,0:T(8,128)(2,1)S(1)}, bf16[4,32,512]{2,1,0:T(8,128)(2,1)S(1)}, u32[]{:S(2)}, u32[]{:S(2)}) collective-permute-start(bf16[4,32,512]{2,1,0:T(8,128)(2,1)S(1)} %get-tuple-element.77), channel_id=1, source_target_pairs={{0,32},{1,33},{2,34},{3,35},{4,36},{5,37},{6,38},{7,39},{8,40},{9,... | collective-permute-start | bytes 393224 | tf_op jit(solution)/shard_map/ppermute | solution.py:252
  84.1 7.0 %collective-permute-start.11 = (bf16[4,32,512]{2,1,0:T(8,128)(2,1)S(1)}, bf16[4,32,512]{2,1,0:T(8,128)(2,1)S(1)}, u32[]{:S(2)}, u32[]{:S(2)}) collective-permute-start(bf16[4,32,512]{2,1,0:T(8,128)(2,1)S(1)} %get-tuple-element.78), channel_id=1, source_target_pairs={{0,48},{1,49},{2,50},{3,51},{4,52},{5,53},{6,54},{7,55},{8,56},{9,... | collective-permute-start | bytes 393224 | tf_op jit(solution)/shard_map/ppermute | solution.py:252
  85.1 6.2 %collective-permute-start.9 = (bf16[4,32,512]{2,1,0:T(8,128)(2,1)S(1)}, bf16[4,32,512]{2,1,0:T(8,128)(2,1)S(1)}, u32[]{:S(2)}, u32[]{:S(2)}) collective-permute-start(bf16[4,32,512]{2,1,0:T(8,128)(2,1)S(1)} %get-tuple-element.76), channel_id=1, source_target_pairs={{0,16},{1,17},{2,18},{3,19},{4,20},{5,21},{6,22},{7,23},{8,24},{9,... | collective-permute-start | bytes 393224 | tf_op jit(solution)/shard_map/ppermute | solution.py:252
  91.4 6.1 %collective-permute-start.12 = (bf16[32,512]{1,0:T(8,128)(2,1)S(1)}, bf16[32,512]{1,0:T(8,128)(2,1)S(1)}, u32[]{:S(2)}, u32[]{:S(2)}) collective-permute-start(bf16[32,512]{1,0:T(8,128)(2,1)S(1)} %get-tuple-element.80), channel_id=1, source_target_pairs={{0,1},{1,0},{2,3},{3,2},{4,5},{5,4},{6,7},{7,6},{8,9},{9,8},{10,11... | collective-permute-start | bytes 98312 | tf_op jit(solution)/shard_map/ppermute | solution.py:252
  91.5 15.7 %collective-permute-start.13 = (bf16[32,512]{1,0:T(8,128)(2,1)S(1)}, bf16[32,512]{1,0:T(8,128)(2,1)S(1)}, u32[]{:S(2)}, u32[]{:S(2)}) collective-permute-start(bf16[32,512]{1,0:T(8,128)(2,1)S(1)} %get-tuple-element.81), channel_id=1, source_target_pairs={{0,8},{1,9},{2,10},{3,11},{4,12},{5,13},{6,14},{7,15},{8,0},{9,1},... | collective-permute-start | bytes 98312 | tf_op jit(solution)/shard_map/ppermute | solution.py:252
  93.1 17.8 %collective-permute-start.16 = (bf16[32,512]{1,0:T(8,128)(2,1)S(1)}, bf16[32,512]{1,0:T(8,128)(2,1)S(1)}, u32[]{:S(2)}, u32[]{:S(2)}) collective-permute-start(bf16[32,512]{1,0:T(8,128)(2,1)S(1)} %get-tuple-element.80), channel_id=1, source_target_pairs={{0,65},{1,64},{2,67},{3,66},{4,69},{5,68},{6,71},{7,70},{8,73},{9,... | collective-permute-start | bytes 98312 | tf_op jit(solution)/shard_map/ppermute | solution.py:252
  96.5 12.2 %collective-permute-start.14 = (bf16[32,512]{1,0:T(8,128)(2,1)S(1)}, bf16[32,512]{1,0:T(8,128)(2,1)S(1)}, u32[]{:S(2)}, u32[]{:S(2)}) collective-permute-start(bf16[32,512]{1,0:T(8,128)(2,1)S(1)} %get-tuple-element.82), channel_id=1, source_target_pairs={{0,9},{1,8},{2,11},{3,10},{4,13},{5,12},{6,15},{7,14},{8,1},{9,0},... | collective-permute-start | bytes 98312 | tf_op jit(solution)/shard_map/ppermute | solution.py:252
  96.5 14.5 %collective-permute-start.15 = (bf16[32,512]{1,0:T(8,128)(2,1)S(1)}, bf16[32,512]{1,0:T(8,128)(2,1)S(1)}, u32[]{:S(2)}, u32[]{:S(2)}) collective-permute-start(bf16[32,512]{1,0:T(8,128)(2,1)S(1)} %get-tuple-element.79.refs_0_), channel_id=1, source_target_pairs={{0,64},{1,65},{2,66},{3,67},{4,68},{5,69},{6,70},{7,71},{8,72},{9,... | collective-permute-start | bytes 98312 | tf_op jit(solution)/shard_map/ppermute | solution.py:252
  97.5 13.5 %collective-permute-start.17 = (bf16[32,512]{1,0:T(8,128)(2,1)S(1)}, bf16[32,512]{1,0:T(8,128)(2,1)S(1)}, u32[]{:S(2)}, u32[]{:S(2)}) collective-permute-start(bf16[32,512]{1,0:T(8,128)(2,1)S(1)} %get-tuple-element.81), channel_id=1, source_target_pairs={{0,72},{1,73},{2,74},{3,75},{4,76},{5,77},{6,78},{7,79},{8,64},{9,... | collective-permute-start | bytes 98312 | tf_op jit(solution)/shard_map/ppermute | solution.py:252
  107.2 4.9 %collective-permute-start.18 = (bf16[32,512]{1,0:T(8,128)(2,1)S(1)}, bf16[32,512]{1,0:T(8,128)(2,1)S(1)}, u32[]{:S(2)}, u32[]{:S(2)}) collective-permute-start(bf16[32,512]{1,0:T(8,128)(2,1)S(1)} %get-tuple-element.82), channel_id=1, source_target_pairs={{0,73},{1,72},{2,75},{3,74},{4,77},{5,76},{6,79},{7,78},{8,65},{9,... | collective-permute-start | bytes 98312 | tf_op jit(solution)/shard_map/ppermute | solution.py:252
  112.7 12.9 %collective-permute-start.19 = (bf16[32,2048]{1,0:T(8,128)(2,1)S(1)}, bf16[32,2048]{1,0:T(8,128)(2,1)S(1)}, u32[]{:S(2)}, u32[]{:S(2)}) collective-permute-start(bf16[32,2048]{1,0:T(8,128)(2,1)S(1)} %make_rows.1.mine_ref), channel_id=1, source_target_pairs={{0,16},{1,17},{2,18},{3,19},{4,20},{5,21},{6,22},{7,23},{8,24},{9,... | collective-permute-start | bytes 393224 | tf_op jit(solution)/shard_map/ppermute | solution.py:252
  114.4 11.2 %collective-permute-start.20 = (bf16[32,2048]{1,0:T(8,128)(2,1)S(1)}, bf16[32,2048]{1,0:T(8,128)(2,1)S(1)}, u32[]{:S(2)}, u32[]{:S(2)}) collective-permute-start(bf16[32,2048]{1,0:T(8,128)(2,1)S(1)} %make_rows.1.mine_ref), channel_id=1, source_target_pairs={{0,32},{1,33},{2,34},{3,35},{4,36},{5,37},{6,38},{7,39},{8,40},{9,... | collective-permute-start | bytes 393224 | tf_op jit(solution)/shard_map/ppermute | solution.py:252
  117.2 8.3 %collective-permute-start.21 = (bf16[32,2048]{1,0:T(8,128)(2,1)S(1)}, bf16[32,2048]{1,0:T(8,128)(2,1)S(1)}, u32[]{:S(2)}, u32[]{:S(2)}) collective-permute-start(bf16[32,2048]{1,0:T(8,128)(2,1)S(1)} %make_rows.1.mine_ref), channel_id=1, source_target_pairs={{0,48},{1,49},{2,50},{3,51},{4,52},{5,53},{6,54},{7,55},{8,56},{9,... | collective-permute-start | bytes 393224 | tf_op jit(solution)/shard_map/ppermute | solution.py:252
  118.6 1.4 %copy-start.1 = (bf16[16,4,128,128]{3,2,1,0:T(8,128)(2,1)}, bf16[16,4,128,128]{3,2,1,0:T(8,128)(2,1)S(1)}, u32[]{:S(2)}) copy-start(bf16[16,4,128,128]{3,2,1,0:T(8,128)(2,1)S(1)} %all-to-all-done.1.x_ref.o_ref) | copy-start | bytes 6291460

commit v3 on v2

--- a/solution.py
+++ b/solution.py
@@ -227,7 +227,7 @@
         out_specs=[spec] * 4,
         out_shape=[shape] * 4,
         scratch_shapes=[pltpu.VMEM((TOK, WIDTH), B16)],
-        compiler_params=params(WIDE),
+        compiler_params=params(53 << 20),
         cost_estimate=cost(2 * TOK * WIDTH * WIDTH, 12 << 20),
         name="finish",
     )(x, x, *[w] * WEIGHT_PARTS)
@@ -350,10 +350,14 @@
     )(pos, *heads, rows)
 
 
-def sum_shares_kernel(mine_ref, a_ref, b_ref, c_ref, *out_refs):
-    for m, ref in enumerate(out_refs):
+def sum_shares_kernel(mine_ref, a_ref, b_ref, c_ref, here_ref, over_ref):
+    for m in range(4):
         total = mine_ref[m] + a_ref[m].astype(F32)
-        ref[...] = (total + b_ref[m].astype(F32) + c_ref[m].astype(F32)).astype(B16)
+        total = (total + b_ref[m].astype(F32) + c_ref[m].astype(F32)).astype(B16)
+        if m < 2:
+            here_ref[m] = total
+        else:
+            over_ref[m - 2] = total
 
 
 def sum_shares(mine, a, b, c):
@@ -361,33 +365,50 @@
     return pl.pallas_call(
         sum_shares_kernel,
         in_specs=[vmem] * 4,
-        out_specs=[vmem] * 4,
-        out_shape=[jax.ShapeDtypeStruct((SHARE, PART), B16)] * 4,
+        out_specs=[vmem] * 2,
+        out_shape=[jax.ShapeDtypeStruct((2, SHARE, PART), B16)] * 2,
         compiler_params=params(SMALL),
         cost_estimate=cost(0, 1 << 20),
         name="sum_shares",
     )(mine, a, b, c)
 
 
-def row_kernel(pos_ref, *refs):
-    out_ref = refs[8]
-    for n, (dz, dc) in enumerate(GROUP):
+def sum_pairs_kernel(a_ref, a2_ref, b_ref, b2_ref, *out_refs):
+    for m, ref in enumerate(out_refs):
+        ref[0] = (a_ref[m].astype(F32) + a2_ref[m].astype(F32)).astype(B16)
+        ref[1] = (b_ref[m].astype(F32) + b2_ref[m].astype(F32)).astype(B16)
+
+
+def sum_pairs(a, a2, b, b2):
+    vmem = pl.BlockSpec(memory_space=pltpu.VMEM)
+    return pl.pallas_call(
+        sum_pairs_kernel,
+        in_specs=[vmem] * 4,
+        out_specs=[vmem] * 2,
+        out_shape=[jax.ShapeDtypeStruct((2, SHARE, PART), B16)] * 2,
+        compiler_params=params(SMALL),
+        cost_estimate=cost(0, 1 << 20),
+        name="sum_pairs",
+    )(a, a2, b, b2)
+
+
+def row_kernel(pos_ref, mine_ref, got_ref, out_ref):
+    for dz, dc in GROUP:
         first = pl.multiple_of(part_of(pos_ref, dz, dc) * PART, PART)
-        total = refs[n][...].astype(F32) + refs[4 + n][...].astype(F32)
-        out_ref[:, pl.ds(first, PART)] = total.astype(B16)
-
-
-def make_rows(pos, near, far):
+        out_ref[:, pl.ds(first, PART)] = got_ref[dz] if dc else mine_ref[dz]
+
+
+def make_rows(pos, mine, got):
     vmem = pl.BlockSpec(memory_space=pltpu.VMEM)
     return pl.pallas_call(
         row_kernel,
-        in_specs=[pl.BlockSpec(memory_space=pltpu.SMEM)] + [vmem] * 8,
+        in_specs=[pl.BlockSpec(memory_space=pltpu.SMEM)] + [vmem] * 2,
         out_specs=vmem,
         out_shape=jax.ShapeDtypeStruct((SHARE, WIDTH), B16),
         compiler_params=params(SMALL),
         cost_estimate=cost(0, 1 << 20),
         name="make_rows",
-    )(pos, *near, *far)
+    )(pos, mine, got)
 
 
 def join_kernel(pos_ref, mine_ref, one_ref, two_ref, three_ref, out_ref):
@@ -411,12 +432,11 @@
 
 
 def share_over_dp(pos, mine, one, two, three):
-    totals = sum_shares(mine, move(one, dy=1), move(two, dy=2), move(three, dy=3))
-    near, far = [], []
-    for (dz, dc), total in zip(GROUP, totals):
-        near.append(total if dz + dc == 0 else move(total, dz=dz, dc=dc))
-        far.append(move(total, dh=1, dz=dz, dc=dc))
-    share = make_rows(pos, near, far)
+    here, over = sum_shares(mine, move(one, dy=1), move(two, dy=2), move(three, dy=3))
+    own, other = sum_pairs(
+        here, move(here, dh=1), move(over, dz=1), move(over, dh=1, dz=1)
+    )
+    share = make_rows(pos, own, move(other, dc=1))
     return [share] + [move(share, dy=r) for r in range(1, YN)]
 
 

time: 127 us -> 127 us (level)
  starting transfers between devices: 39.8 us -> 33.4 us
  waiting for transfers between devices: 51.9 us -> 57.6 us
    ppermute x22 -> x19, starting transfers between devices: 28.2 us -> 21.7 us  [move(): return lax.ppermute(x, ('dp', 'seq'), pairs)]
    ppermute x22 -> x19, waiting for transfers between devices: 23.3 us -> 29 us  [move(): return lax.ppermute(x, ('dp', 'seq'), pairs)]
  transfers between devices with their start and end apart: 24 -> 21, of which waited for: 9 -> 8; matrix products, arithmetic and copies ran while one was open for 0% -> 0% of each run, Pallas kernels for 22% -> 22%
where the time goes in v3:
time: 127 us; the launch traced here: 126 us
  waiting for transfers between devices  57.6 us (45%)
  starting transfers between devices  33.4 us (26%)
  Pallas kernels  32.2 us (25%)
  local copies, waits for them, and re-layouts  2.4 us (2%)
    ppermute x19, waiting for transfers between devices, move(): return lax.ppermute(x, ('dp', 'seq'), pairs)  29 us
    all_to_all x2, waiting for transfers between devices, to_heads(): return lax.all_to_all(x, 'seq', split_axis=0, concat_axis=0, tiled=True)  28.6 us
    ppermute x19, starting transfers between devices, move(): return lax.ppermute(x, ('dp', 'seq'), pairs)  21.7 us
    all_to_all x2, starting transfers between devices, to_heads(): return lax.all_to_all(x, 'seq', split_axis=0, concat_axis=0, tiled=True)  11.6 us
    pallas_call x1, Pallas kernels, backward(): pl.pallas_call(backward_kernel, in_specs=[vmem] * 4, out_specs=vmem, out_...  10 us
    pallas_call x1, Pallas kernels, pack(): pl.pallas_call(pack_kernel, grid=(HEADS // PACK_HEADS,), in_specs=[part,...  7.02 us
    pallas_call x1, Pallas kernels, finish(): pl.pallas_call(finish_kernel, grid=(FINISH_STEPS,), in_specs=[pl.BlockSpe...  5.6 us
    pallas_call x1, Pallas kernels, forward(): pl.pallas_call(forward_kernel, in_specs=[vmem], out_specs=[vmem, vmem, vm...  4.66 us
  transfers between devices with their start and end apart: 21, of which 8 were waited for; matrix products, arithmetic and copies ran while one was open for 0% of the time, Pallas kernels for 22%

profile of v3, /device:TPU:2, one launch (start us, length us, event | category | flops | bytes accessed | tf_op | source)
XLA Modules:
  0.0 126.5 jit_solution(851129008252576628)
XLA Ops:
  0.7 0.1 pad_add_fusion.pos_ref
  0.7 0.0 copy-start
  0.7 1.0 copy-done
  1.8 0.6 cut.1
  2.4 0.1 collective-permute-start
  2.5 2.0 %collective-permute-start.1 = (bf16[128,512]{1,0:T(8,128)(2,1)S(1)}, bf16[128,512]{1,0:T(8,128)(2,1)S(1)}, u32[]{:S(2)}, u32[]{:S(2)}) collective-permute-start(bf16[128,512]{1,0:T(8,128)(2,1)S(1)} %get-tuple-element.50), channel_id=1, source_target_pairs={{0,8},{1,9},{2,10},{3,11},{4,12},{5,13},{6,14},{7,15},{8,0},{9,1},... | collective-permute-start | bytes 393224 | tf_op jit(solution)/shard_map/ppermute | solution.py:252
  4.5 0.1 collective-permute-start.2
  4.5 7.0 %pack.1 = bf16[16,4,128,128]{3,2,1,0:T(8,128)(2,1)} custom-call(bf16[128,2048]{1,0:T(8,128)(2,1)} %bitcast.14, bf16[128,2048]{1,0:T(8,128)(2,1)} %bitcast.15, bf16[128,2048]{1,0:T(8,128)(2,1)} %bitcast.16, bf16[128,2048]{1,0:T(8,128)(2,1)} %bitcast.12, bf16[2048,2048]{1,0:T(8,128)(2,1)} %refs_3_.3, bf16[2048,2048]{1,0:T(8,128)(2,1)} %refs_3_.3, ...), custom_call_target="tpu_custom_call" | custom-call | flops 1073741824 | bytes 12582912 | tf_op jit(solution)/shard_map/pack/pallas_call | solution.py:59
  11.5 0.0 collective-permute-done.b_ref
  11.5 0.0 collective-permute-done.1.c_ref
  11.6 0.0 collective-permute-done.2.d_ref
  11.6 6.0 %all-to-all-start = ((bf16[16,4,128,128]{3,2,1,0:T(8,128)(2,1)}), bf16[16,4,128,128]{3,2,1,0:T(8,128)(2,1)S(1)}, u32[]{:S(2)}, u32[]{:S(2)}) async-start(bf16[16,4,128,128]{3,2,1,0:T(8,128)(2,1)} %pack.1), calls=%async_computation | async-start | bytes 4194304 | tf_op jit(solution)/shard_map/all_to_all | solution.py:444
  17.6 28.6 %all-to-all-done.x_ref = bf16[16,4,128,128]{3,2,1,0:T(8,128)(2,1)S(1)} async-done(((bf16[16,4,128,128]{3,2,1,0:T(8,128)(2,1)}), bf16[16,4,128,128]{3,2,1,0:T(8,128)(2,1)S(1)}, u32[]{:S(2)}, u32[]{:S(2)}) %all-to-all-start) | async-done | bytes 2097184 | tf_op jit(solution)/shard_map/all_to_all | solution.py:444
  46.2 0.0 collective-permute-start.3
  46.2 2.0 %collective-permute-start.4 = (bf16[512,512]{1,0:T(8,128)(2,1)S(1)}, bf16[512,512]{1,0:T(8,128)(2,1)S(1)}, u32[]{:S(2)}, u32[]{:S(2)}) collective-permute-start(bf16[512,512]{1,0:T(8,128)(2,1)S(1)} %join_rows.1.refs_0_), channel_id=1, source_target_pairs={{0,2},{1,3},{2,4},{3,5},{4,6},{5,7},{6,0},{7,1},{8,10},{9,11},{10,... | collective-permute-start | bytes 1572872 | tf_op jit(solution)/shard_map/ppermute | solution.py:252
  48.3 0.4 collective-permute-start.5
  48.6 4.7 %attention_forward.1 = (bf16[16,128,128]{2,1,0:T(8,128)(2,1)S(1)}, bf16[16,128,128]{2,1,0:T(8,128)(2,1)S(1)}, f32[8,2048]{1,0:T(8,128)S(1)}) custom-call(bf16[16,4,128,128]{3,2,1,0:T(8,128)(2,1)S(1)} %all-to-all-done.x_ref), custom_call_target="tpu_custom_call" | custom-call | tf_op jit(solution)/shard_map/attention_forward/pallas_call | solution.py:122
  53.3 1.3 %collective-permute-start.6 = (bf16[16,128,128]{2,1,0:T(8,128)(2,1)S(1)}, bf16[16,128,128]{2,1,0:T(8,128)(2,1)S(1)}, u32[]{:S(2)}, u32[]{:S(2)}) collective-permute-start(bf16[16,128,128]{2,1,0:T(8,128)(2,1)S(1)} %get-tuple-element.60.ot_ref.refs_0_), channel_id=1, source_target_pairs={{0,8},{1,9},{2,10},{3,11},{4,12},{5,13},{6,14},{7,15},{8,0},{9,1},... | collective-permute-start | bytes 1572872 | tf_op jit(solution)/shard_map/ppermute | solution.py:252
  54.6 0.0 collective-permute-start.7
  54.6 10.0 %attention_backward.1 = bf16[16,4,128,128]{3,2,1,0:T(8,128)(2,1)} custom-call(bf16[16,4,128,128]{3,2,1,0:T(8,128)(2,1)S(1)} %all-to-all-done.x_ref, bf16[16,128,128]{2,1,0:T(8,128)(2,1)S(1)} %get-tuple-element.59.o_ref, bf16[16,128,128]{2,1,0:T(8,128)(2,1)S(1)} %get-tuple-element.60.ot_ref.refs_0_, f32[8,2048]{1,0:T(8,128)S(1)} %get-tuple-element.61.stat_ref), custom_call_target="tpu_custom_call" | custom-call | tf_op jit(solution)/shard_map/attention_backward/pallas_call | solution.py:180
  64.7 6.6 %collective-permute-done.3.refs_1_ = bf16[512,512]{1,0:T(8,128)(2,1)S(1)} collective-permute-done((bf16[512,512]{1,0:T(8,128)(2,1)S(1)}, bf16[512,512]{1,0:T(8,128)(2,1)S(1)}, u32[]{:S(2)}, u32[]{:S(2)}) %collective-permute-start.3) | collective-permute-done | bytes 524320 | tf_op jit(solution)/shard_map/ppermute | solution.py:252
  71.2 0.0 collective-permute-done.4.refs_3_
  71.2 0.0 collective-permute-done.5.refs_2_
  71.2 0.1 stack.21.refs_4_
  71.4 0.0 collective-permute-done.6.refs_2_
  71.4 0.0 collective-permute-done.7.refs_1_
  71.4 0.1 collective-permute-start.8
  71.5 1.9 %collective-permute-done.8.refs_3_ = bf16[16,128,128]{2,1,0:T(8,128)(2,1)S(1)} collective-permute-done((bf16[16,128,128]{2,1,0:T(8,128)(2,1)S(1)}, bf16[16,128,128]{2,1,0:T(8,128)(2,1)S(1)}, u32[]{:S(2)}, u32[]{:S(2)}) %collective-permute-start.8) | collective-permute-done | bytes 524320 | tf_op jit(solution)/shard_map/ppermute | solution.py:252
  73.4 1.9 %weight_partial.1 = (f32[4,32,512]{2,1,0:T(8,128)S(1)}, bf16[4,32,512]{2,1,0:T(8,128)(2,1)S(1)}, bf16[4,32,512]{2,1,0:T(8,128)(2,1)S(1)}, bf16[4,32,512]{2,1,0:T(8,128)(2,1)S(1)}) custom-call(s32[4]{0:T(128)S(1)} %pad_add_fusion.pos_ref, bf16[16,128,128]{2,1,0:T(8,128)(2,1)S(1)} %get-tuple-element.60.ot_ref.refs_0_, ...), custom_call_target="tpu_custom_call" | custom-call | flops 1073741824 | bytes 5242880 | tf_op jit(solution)/shard_map/weight_partial/pallas_call | solution.py:340
  75.3 5.6 %all-to-all-start.1 = ((bf16[16,4,128,128]{3,2,1,0:T(8,128)(2,1)}), bf16[16,4,128,128]{3,2,1,0:T(8,128)(2,1)S(1)}, u32[]{:S(2)}, u32[]{:S(2)}) async-start(bf16[16,4,128,128]{3,2,1,0:T(8,128)(2,1)} %attention_backward.1), calls=%async_computation.1 | async-start | bytes 4194304 | tf_op jit(solution)/shard_map/all_to_all | solution.py:444
  80.9 3.2 %collective-permute-start.10 = (bf16[4,32,512]{2,1,0:T(8,128)(2,1)S(1)}, bf16[4,32,512]{2,1,0:T(8,128)(2,1)S(1)}, u32[]{:S(2)}, u32[]{:S(2)}) collective-permute-start(bf16[4,32,512]{2,1,0:T(8,128)(2,1)S(1)} %get-tuple-element.77), channel_id=1, source_target_pairs={{0,32},{1,33},{2,34},{3,35},{4,36},{5,37},{6,38},{7,39},{8,40},{9,... | collective-permute-start | bytes 393224 | tf_op jit(solution)/shard_map/ppermute | solution.py:252
  84.1 1.0 collective-permute-start.11
  85.2 1.0 collective-permute-start.9
  86.1 2.4 %collective-permute-done.10.b_ref = bf16[4,32,512]{2,1,0:T(8,128)(2,1)S(1)} collective-permute-done((bf16[4,32,512]{2,1,0:T(8,128)(2,1)S(1)}, bf16[4,32,512]{2,1,0:T(8,128)(2,1)S(1)}, u32[]{:S(2)}, u32[]{:S(2)}) %collective-permute-start.10) | collective-permute-done | bytes 131104 | tf_op jit(solution)/shard_map/ppermute | solution.py:252
  88.6 2.5 %collective-permute-done.11.c_ref = bf16[4,32,512]{2,1,0:T(8,128)(2,1)S(1)} collective-permute-done((bf16[4,32,512]{2,1,0:T(8,128)(2,1)S(1)}, bf16[4,32,512]{2,1,0:T(8,128)(2,1)S(1)}, u32[]{:S(2)}, u32[]{:S(2)}) %collective-permute-start.11) | collective-permute-done | bytes 131104 | tf_op jit(solution)/shard_map/ppermute | solution.py:252
  91.1 0.3 collective-permute-done.9.a_ref
  91.4 0.1 sum_shares.1
  91.4 3.7 %collective-permute-start.12 = (bf16[2,32,512]{2,1,0:T(8,128)(2,1)S(1)}, bf16[2,32,512]{2,1,0:T(8,128)(2,1)S(1)}, u32[]{:S(2)}, u32[]{:S(2)}) collective-permute-start(bf16[2,32,512]{2,1,0:T(8,128)(2,1)S(1)} %get-tuple-element.79.a_ref), channel_id=1, source_target_pairs={{0,64},{1,65},{2,66},{3,67},{4,68},{5,69},{6,70},{7,71},{8,72},{9,... | collective-permute-start | bytes 196616 | tf_op jit(solution)/shard_map/ppermute | solution.py:252
  95.1 0.9 collective-permute-start.13
  96.0 0.0 collective-permute-start.14
  96.0 14.0 %collective-permute-done.12.a2_ref = bf16[2,32,512]{2,1,0:T(8,128)(2,1)S(1)} collective-permute-done((bf16[2,32,512]{2,1,0:T(8,128)(2,1)S(1)}, bf16[2,32,512]{2,1,0:T(8,128)(2,1)S(1)}, u32[]{:S(2)}, u32[]{:S(2)}) %collective-permute-start.12) | collective-permute-done | bytes 65568 | tf_op jit(solution)/shard_map/ppermute | solution.py:252
  110.0 0.0 collective-permute-done.13.b_ref
  110.0 0.0 collective-permute-done.14.b2_ref
  110.1 0.1 collective-permute-start.15
  110.2 1.2 collective-permute-done.15.got_ref
  111.4 0.6 make_rows.1.mine_ref
  112.0 1.7 %collective-permute-start.16 = (bf16[32,2048]{1,0:T(8,128)(2,1)S(1)}, bf16[32,2048]{1,0:T(8,128)(2,1)S(1)}, u32[]{:S(2)}, u32[]{:S(2)}) collective-permute-start(bf16[32,2048]{1,0:T(8,128)(2,1)S(1)} %make_rows.1.mine_ref), channel_id=1, source_target_pairs={{0,16},{1,17},{2,18},{3,19},{4,20},{5,21},{6,22},{7,23},{8,24},{9,... | collective-permute-start | bytes 393224 | tf_op jit(solution)/shard_map/ppermute | solution.py:252
  113.6 2.9 %collective-permute-start.17 = (bf16[32,2048]{1,0:T(8,128)(2,1)S(1)}, bf16[32,2048]{1,0:T(8,128)(2,1)S(1)}, u32[]{:S(2)}, u32[]{:S(2)}) collective-permute-start(bf16[32,2048]{1,0:T(8,128)(2,1)S(1)} %make_rows.1.mine_ref), channel_id=1, source_target_pairs={{0,32},{1,33},{2,34},{3,35},{4,36},{5,37},{6,38},{7,39},{8,40},{9,... | collective-permute-start | bytes 393224 | tf_op jit(solution)/shard_map/ppermute | solution.py:252
  116.5 1.3 %collective-permute-start.18 = (bf16[32,2048]{1,0:T(8,128)(2,1)S(1)}, bf16[32,2048]{1,0:T(8,128)(2,1)S(1)}, u32[]{:S(2)}, u32[]{:S(2)}) collective-permute-start(bf16[32,2048]{1,0:T(8,128)(2,1)S(1)} %make_rows.1.mine_ref), channel_id=1, source_target_pairs={{0,48},{1,49},{2,50},{3,51},{4,52},{5,53},{6,54},{7,55},{8,56},{9,... | collective-permute-start | bytes 393224 | tf_op jit(solution)/shard_map/ppermute | solution.py:252
  117.9 0.0 all-to-all-done.1.x_ref.o_ref
  117.9 0.0 copy-start.1
  117.9 1.4 %copy-done.1 = bf16[16,4,128,128]{3,2,1,0:T(8,128)(2,1)} copy-done((bf16[16,4,128,128]{3,2,1,0:T(8,128)(2,1)}, bf16[16,4,128,128]{3,2,1,0:T(8,128)(2,1)S(1)}, u32[]{:S(2)}) %copy-start.1) | copy-done | bytes 2097176
  119.2 5.6 %finish.1 = (bf16[128,2048]{1,0:T(8,128)(2,1)}, bf16[128,2048]{1,0:T(8,128)(2,1)}, bf16[128,2048]{1,0:T(8,128)(2,1)}, bf16[128,2048]{1,0:T(8,128)(2,1)}) custom-call(bf16[16,4,128,128]{3,2,1,0:T(8,128)(2,1)} %copy-done.1, bf16[16,4,128,128]{3,2,1,0:T(8,128)(2,1)} %copy-done.1, bf16[2048,2048]{1,0:T(8,128)(2,1)} %refs_3_.3, bf16[2048,2048]{1,0:T(8,128)(2,1)} %refs_3_.3, ...), custom_call_target="tpu_custom_call" | custom-call | flops 1073741824 | bytes 12582912 | tf_op jit(solution)/shard_map/finish/pallas_call | solution.py:219
  124.8 0.0 collective-permute-done.16.one_ref
  124.8 0.0 collective-permute-done.17.two_ref
  124.9 0.0 collective-permute-done.18.three_ref
  124.9 1.6 %join_shares.1 = f32[128,2048]{1,0:T(8,128)} custom-call(s32[4]{0:T(128)S(1)} %pad_add_fusion.pos_ref, bf16[32,2048]{1,0:T(8,128)(2,1)S(1)} %make_rows.1.mine_ref, bf16[32,2048]{1,0:T(8,128)(2,1)S(1)} %collective-permute-done.16.one_ref, bf16[32,2048]{1,0:T(8,128)(2,1)S(1)} %collective-permute-done.17.two_ref, ...), custom_call_target="tpu_custom_call" | custom-call | bytes 2097152 | tf_op jit(solution)/shard_map/join_shares/pallas_call | solution.py:423
  (2 shorter events, 0.1 us)
Async XLA Ops:
  0.7 1.0 copy-start
  2.4 9.2 %collective-permute-start = (bf16[128,512]{1,0:T(8,128)(2,1)S(1)}, bf16[128,512]{1,0:T(8,128)(2,1)S(1)}, u32[]{:S(2)}, u32[]{:S(2)}) collective-permute-start(bf16[128,512]{1,0:T(8,128)(2,1)S(1)} %get-tuple-element.49), channel_id=1, source_target_pairs={{0,1},{1,0},{2,3},{3,2},{4,5},{5,4},{6,7},{7,6},{8,9},{9,8},{10,11... | collective-permute-start | bytes 393224 | tf_op jit(solution)/shard_map/ppermute | solution.py:252
  2.5 9.1 %collective-permute-start.1 = (bf16[128,512]{1,0:T(8,128)(2,1)S(1)}, bf16[128,512]{1,0:T(8,128)(2,1)S(1)}, u32[]{:S(2)}, u32[]{:S(2)}) collective-permute-start(bf16[128,512]{1,0:T(8,128)(2,1)S(1)} %get-tuple-element.50), channel_id=1, source_target_pairs={{0,8},{1,9},{2,10},{3,11},{4,12},{5,13},{6,14},{7,15},{8,0},{9,1},... | collective-permute-start | bytes 393224 | tf_op jit(solution)/shard_map/ppermute | solution.py:252
  4.5 7.1 %collective-permute-start.2 = (bf16[128,512]{1,0:T(8,128)(2,1)S(1)}, bf16[128,512]{1,0:T(8,128)(2,1)S(1)}, u32[]{:S(2)}, u32[]{:S(2)}) collective-permute-start(bf16[128,512]{1,0:T(8,128)(2,1)S(1)} %get-tuple-element.51), channel_id=1, source_target_pairs={{0,9},{1,8},{2,11},{3,10},{4,13},{5,12},{6,15},{7,14},{8,1},{9,0},... | collective-permute-start | bytes 393224 | tf_op jit(solution)/shard_map/ppermute | solution.py:252
  11.6 34.7 %all-to-all-start = ((bf16[16,4,128,128]{3,2,1,0:T(8,128)(2,1)}), bf16[16,4,128,128]{3,2,1,0:T(8,128)(2,1)S(1)}, u32[]{:S(2)}, u32[]{:S(2)}) async-start(bf16[16,4,128,128]{3,2,1,0:T(8,128)(2,1)} %pack.1), calls=%async_computation | async-start | bytes 4194304 | tf_op jit(solution)/shard_map/all_to_all | solution.py:444
  46.2 25.0 %collective-permute-start.3 = (bf16[512,512]{1,0:T(8,128)(2,1)S(1)}, bf16[512,512]{1,0:T(8,128)(2,1)S(1)}, u32[]{:S(2)}, u32[]{:S(2)}) collective-permute-start(bf16[512,512]{1,0:T(8,128)(2,1)S(1)} %join_rows.1.refs_0_), channel_id=1, source_target_pairs={{0,6},{1,7},{2,0},{3,1},{4,2},{5,3},{6,4},{7,5},{8,14},{9,15},{10,... | collective-permute-start | bytes 1572872 | tf_op jit(solution)/shard_map/ppermute | solution.py:252
  46.2 25.0 %collective-permute-start.4 = (bf16[512,512]{1,0:T(8,128)(2,1)S(1)}, bf16[512,512]{1,0:T(8,128)(2,1)S(1)}, u32[]{:S(2)}, u32[]{:S(2)}) collective-permute-start(bf16[512,512]{1,0:T(8,128)(2,1)S(1)} %join_rows.1.refs_0_), channel_id=1, source_target_pairs={{0,2},{1,3},{2,4},{3,5},{4,6},{5,7},{6,0},{7,1},{8,10},{9,11},{10,... | collective-permute-start | bytes 1572872 | tf_op jit(solution)/shard_map/ppermute | solution.py:252
  48.3 23.0 %collective-permute-start.5 = (bf16[512,512]{1,0:T(8,128)(2,1)S(1)}, bf16[512,512]{1,0:T(8,128)(2,1)S(1)}, u32[]{:S(2)}, u32[]{:S(2)}) collective-permute-start(bf16[512,512]{1,0:T(8,128)(2,1)S(1)} %join_rows.1.refs_0_), channel_id=1, source_target_pairs={{0,4},{1,5},{2,6},{3,7},{4,0},{5,1},{6,2},{7,3},{8,12},{9,13},{10,... | collective-permute-start | bytes 1572872 | tf_op jit(solution)/shard_map/ppermute | solution.py:252
  53.3 18.1 %collective-permute-start.6 = (bf16[16,128,128]{2,1,0:T(8,128)(2,1)S(1)}, bf16[16,128,128]{2,1,0:T(8,128)(2,1)S(1)}, u32[]{:S(2)}, u32[]{:S(2)}) collective-permute-start(bf16[16,128,128]{2,1,0:T(8,128)(2,1)S(1)} %get-tuple-element.60.ot_ref.refs_0_), channel_id=1, source_target_pairs={{0,8},{1,9},{2,10},{3,11},{4,12},{5,13},{6,14},{7,15},{8,0},{9,1},... | collective-permute-start | bytes 1572872 | tf_op jit(solution)/shard_map/ppermute | solution.py:252
  54.6 16.8 %collective-permute-start.7 = (bf16[16,128,128]{2,1,0:T(8,128)(2,1)S(1)}, bf16[16,128,128]{2,1,0:T(8,128)(2,1)S(1)}, u32[]{:S(2)}, u32[]{:S(2)}) collective-permute-start(bf16[16,128,128]{2,1,0:T(8,128)(2,1)S(1)} %get-tuple-element.60.ot_ref.refs_0_), channel_id=1, source_target_pairs={{0,1},{1,0},{2,3},{3,2},{4,5},{5,4},{6,7},{7,6},{8,9},{9,8},{10,11... | collective-permute-start | bytes 1572872 | tf_op jit(solution)/shard_map/ppermute | solution.py:252
  71.4 2.0 %collective-permute-start.8 = (bf16[16,128,128]{2,1,0:T(8,128)(2,1)S(1)}, bf16[16,128,128]{2,1,0:T(8,128)(2,1)S(1)}, u32[]{:S(2)}, u32[]{:S(2)}) collective-permute-start(bf16[16,128,128]{2,1,0:T(8,128)(2,1)S(1)} %collective-permute-done.6.refs_2_), channel_id=1, source_target_pairs={{0,1},{1,0},{2,3},{3,2},{4,5},{5,4},{6,7},{7,6},{8,9},{9,8},{10,11... | collective-permute-start | bytes 1572872 | tf_op jit(solution)/shard_map/ppermute | solution.py:252
  75.3 42.6 %all-to-all-start.1 = ((bf16[16,4,128,128]{3,2,1,0:T(8,128)(2,1)}), bf16[16,4,128,128]{3,2,1,0:T(8,128)(2,1)S(1)}, u32[]{:S(2)}, u32[]{:S(2)}) async-start(bf16[16,4,128,128]{3,2,1,0:T(8,128)(2,1)} %attention_backward.1), calls=%async_computation.1 | async-start | bytes 4194304 | tf_op jit(solution)/shard_map/all_to_all | solution.py:444
  80.9 7.7 %collective-permute-start.10 = (bf16[4,32,512]{2,1,0:T(8,128)(2,1)S(1)}, bf16[4,32,512]{2,1,0:T(8,128)(2,1)S(1)}, u32[]{:S(2)}, u32[]{:S(2)}) collective-permute-start(bf16[4,32,512]{2,1,0:T(8,128)(2,1)S(1)} %get-tuple-element.77), channel_id=1, source_target_pairs={{0,32},{1,33},{2,34},{3,35},{4,36},{5,37},{6,38},{7,39},{8,40},{9,... | collective-permute-start | bytes 393224 | tf_op jit(solution)/shard_map/ppermute | solution.py:252
  84.1 7.0 %collective-permute-start.11 = (bf16[4,32,512]{2,1,0:T(8,128)(2,1)S(1)}, bf16[4,32,512]{2,1,0:T(8,128)(2,1)S(1)}, u32[]{:S(2)}, u32[]{:S(2)}) collective-permute-start(bf16[4,32,512]{2,1,0:T(8,128)(2,1)S(1)} %get-tuple-element.78), channel_id=1, source_target_pairs={{0,48},{1,49},{2,50},{3,51},{4,52},{5,53},{6,54},{7,55},{8,56},{9,... | collective-permute-start | bytes 393224 | tf_op jit(solution)/shard_map/ppermute | solution.py:252
  85.2 6.2 %collective-permute-start.9 = (bf16[4,32,512]{2,1,0:T(8,128)(2,1)S(1)}, bf16[4,32,512]{2,1,0:T(8,128)(2,1)S(1)}, u32[]{:S(2)}, u32[]{:S(2)}) collective-permute-start(bf16[4,32,512]{2,1,0:T(8,128)(2,1)S(1)} %get-tuple-element.76), channel_id=1, source_target_pairs={{0,16},{1,17},{2,18},{3,19},{4,20},{5,21},{6,22},{7,23},{8,24},{9,... | collective-permute-start | bytes 393224 | tf_op jit(solution)/shard_map/ppermute | solution.py:252
  91.4 18.6 %collective-permute-start.12 = (bf16[2,32,512]{2,1,0:T(8,128)(2,1)S(1)}, bf16[2,32,512]{2,1,0:T(8,128)(2,1)S(1)}, u32[]{:S(2)}, u32[]{:S(2)}) collective-permute-start(bf16[2,32,512]{2,1,0:T(8,128)(2,1)S(1)} %get-tuple-element.79.a_ref), channel_id=1, source_target_pairs={{0,64},{1,65},{2,66},{3,67},{4,68},{5,69},{6,70},{7,71},{8,72},{9,... | collective-permute-start | bytes 196616 | tf_op jit(solution)/shard_map/ppermute | solution.py:252
  95.1 14.9 %collective-permute-start.13 = (bf16[2,32,512]{2,1,0:T(8,128)(2,1)S(1)}, bf16[2,32,512]{2,1,0:T(8,128)(2,1)S(1)}, u32[]{:S(2)}, u32[]{:S(2)}) collective-permute-start(bf16[2,32,512]{2,1,0:T(8,128)(2,1)S(1)} %get-tuple-element.80), channel_id=1, source_target_pairs={{0,8},{1,9},{2,10},{3,11},{4,12},{5,13},{6,14},{7,15},{8,0},{9,1},... | collective-permute-start | bytes 196616 | tf_op jit(solution)/shard_map/ppermute | solution.py:252
  96.0 14.0 %collective-permute-start.14 = (bf16[2,32,512]{2,1,0:T(8,128)(2,1)S(1)}, bf16[2,32,512]{2,1,0:T(8,128)(2,1)S(1)}, u32[]{:S(2)}, u32[]{:S(2)}) collective-permute-start(bf16[2,32,512]{2,1,0:T(8,128)(2,1)S(1)} %get-tuple-element.80), channel_id=1, source_target_pairs={{0,72},{1,73},{2,74},{3,75},{4,76},{5,77},{6,78},{7,79},{8,64},{9,... | collective-permute-start | bytes 196616 | tf_op jit(solution)/shard_map/ppermute | solution.py:252
  110.1 1.3 %collective-permute-start.15 = (bf16[2,32,512]{2,1,0:T(8,128)(2,1)S(1)}, bf16[2,32,512]{2,1,0:T(8,128)(2,1)S(1)}, u32[]{:S(2)}, u32[]{:S(2)}) collective-permute-start(bf16[2,32,512]{2,1,0:T(8,128)(2,1)S(1)} %get-tuple-element.82), channel_id=1, source_target_pairs={{0,1},{1,0},{2,3},{3,2},{4,5},{5,4},{6,7},{7,6},{8,9},{9,8},{10,11... | collective-permute-start | bytes 196616 | tf_op jit(solution)/shard_map/ppermute | solution.py:252
  112.0 12.9 %collective-permute-start.16 = (bf16[32,2048]{1,0:T(8,128)(2,1)S(1)}, bf16[32,2048]{1,0:T(8,128)(2,1)S(1)}, u32[]{:S(2)}, u32[]{:S(2)}) collective-permute-start(bf16[32,2048]{1,0:T(8,128)(2,1)S(1)} %make_rows.1.mine_ref), channel_id=1, source_target_pairs={{0,16},{1,17},{2,18},{3,19},{4,20},{5,21},{6,22},{7,23},{8,24},{9,... | collective-permute-start | bytes 393224 | tf_op jit(solution)/shard_map/ppermute | solution.py:252
  113.6 11.2 %collective-permute-start.17 = (bf16[32,2048]{1,0:T(8,128)(2,1)S(1)}, bf16[32,2048]{1,0:T(8,128)(2,1)S(1)}, u32[]{:S(2)}, u32[]{:S(2)}) collective-permute-start(bf16[32,2048]{1,0:T(8,128)(2,1)S(1)} %make_rows.1.mine_ref), channel_id=1, source_target_pairs={{0,32},{1,33},{2,34},{3,35},{4,36},{5,37},{6,38},{7,39},{8,40},{9,... | collective-permute-start | bytes 393224 | tf_op jit(solution)/shard_map/ppermute | solution.py:252
  116.5 8.3 %collective-permute-start.18 = (bf16[32,2048]{1,0:T(8,128)(2,1)S(1)}, bf16[32,2048]{1,0:T(8,128)(2,1)S(1)}, u32[]{:S(2)}, u32[]{:S(2)}) collective-permute-start(bf16[32,2048]{1,0:T(8,128)(2,1)S(1)} %make_rows.1.mine_ref), channel_id=1, source_target_pairs={{0,48},{1,49},{2,50},{3,51},{4,52},{5,53},{6,54},{7,55},{8,56},{9,... | collective-permute-start | bytes 393224 | tf_op jit(solution)/shard_map/ppermute | solution.py:252
  117.9 1.4 %copy-start.1 = (bf16[16,4,128,128]{3,2,1,0:T(8,128)(2,1)}, bf16[16,4,128,128]{3,2,1,0:T(8,128)(2,1)S(1)}, u32[]{:S(2)}) copy-start(bf16[16,4,128,128]{3,2,1,0:T(8,128)(2,1)S(1)} %all-to-all-done.1.x_ref.o_ref) | copy-start | bytes 6291460

commit v4 on v3

--- a/solution.py
+++ b/solution.py
@@ -316,13 +316,13 @@
 def weight_kernel(pos_ref, *refs):
     heads, rhs_ref, shares = refs[:4], refs[4], refs[5:9]
     lhs_ref, total_ref = refs[9:]
-    for dx in range(XN):
+    for place, dx in enumerate((0, 2, 1, 3)):
         for n, (dz, dc) in enumerate(GROUP):
             z = lax.rem(pos_ref[0] + dz, ZN)
             x = lax.rem(pos_ref[1] + dx, XN)
             c = lax.rem(pos_ref[2] + dc, CN)
             block = (z * XN + x) * CN + c
-            at = (dx * 4 + n) * TOK
+            at = (place * 4 + n) * TOK
             for m, ref in enumerate(heads):
                 lhs_ref[m * HEAD : (m + 1) * HEAD, at : at + TOK] = ref[block]
     total_ref[...] = nn(lhs_ref[...], rhs_ref[...])
@@ -459,14 +459,14 @@
     rows = join_rows(parts)
     x = to_heads(packed)
     x, rows = tie(x, rows)
+    rows_far = move(rows, dx=-2)
     rows_near, rows_before = move(rows, dx=-1), move(rows, dx=-3)
-    rows_far = move(rows, dx=-2)
     o, ot, stat = forward(x)
     beside = move(ot, dc=1)
     over = move(ot, dz=1)
     grads = backward(x, o, ot, stat)
-    rows_near, rows_before, rows_far, grads = tie(rows_near, rows_before, rows_far, grads)
-    rows = stack([rows, rows_near, rows_far, rows_before])
+    rows_far, rows_near, rows_before, grads = tie(rows_far, rows_near, rows_before, grads)
+    rows = stack([rows, rows_far, rows_near, rows_before])
     over, beside, rows = tie(over, beside, rows)
     heads = [ot, beside, over, move(over, dc=1)]
     shares = weight_partial(pos, heads, rows)

time: 127 us -> 127 us (level)
  no operation moved by 1% of the time
where the time goes in v4:
time: 127 us
  waiting for transfers between devices  58 us (46%)
  starting transfers between devices  33.2 us (26%)
  Pallas kernels  32.2 us (25%)
  local copies, waits for them, and re-layouts  2.4 us (2%)
    ppermute x19, waiting for transfers between devices, move(): return lax.ppermute(x, ('dp', 'seq'), pairs)  29.4 us
    all_to_all x2, waiting for transfers between devices, to_heads(): return lax.all_to_all(x, 'seq', split_axis=0, concat_axis=0, tiled=True)  28.6 us
    ppermute x19, starting transfers between devices, move(): return lax.ppermute(x, ('dp', 'seq'), pairs)  21.3 us
    all_to_all x2, starting transfers between devices, to_heads(): return lax.all_to_all(x, 'seq', split_axis=0, concat_axis=0, tiled=True)  11.9 us
    pallas_call x1, Pallas kernels, backward(): pl.pallas_call(backward_kernel, in_specs=[vmem] * 4, out_specs=vmem, out_...  10 us
    pallas_call x1, Pallas kernels, pack(): pl.pallas_call(pack_kernel, grid=(HEADS // PACK_HEADS,), in_specs=[part,...  7.02 us
    pallas_call x1, Pallas kernels, finish(): pl.pallas_call(finish_kernel, grid=(FINISH_STEPS,), in_specs=[pl.BlockSpe...  5.6 us
    pallas_call x1, Pallas kernels, forward(): pl.pallas_call(forward_kernel, in_specs=[vmem], out_specs=[vmem, vmem, vm...  4.66 us
  transfers between devices with their start and end apart: 21, of which 8 were waited for; matrix products, arithmetic and copies ran while one was open for 0% of the time, Pallas kernels for 22%

profile of v4, /device:TPU:2, one launch (start us, length us, event | category | flops | bytes accessed | tf_op | source)
XLA Modules:
  0.0 126.8 jit_solution(12138739965134088910)
XLA Ops:
  0.7 0.1 pad_add_fusion.pos_ref
  0.7 0.0 copy-start
  0.7 1.0 copy-done
  1.8 0.6 cut.1
  2.4 0.1 collective-permute-start
  2.5 2.0 %collective-permute-start.1 = (bf16[128,512]{1,0:T(8,128)(2,1)S(1)}, bf16[128,512]{1,0:T(8,128)(2,1)S(1)}, u32[]{:S(2)}, u32[]{:S(2)}) collective-permute-start(bf16[128,512]{1,0:T(8,128)(2,1)S(1)} %get-tuple-element.50), channel_id=1, source_target_pairs={{0,8},{1,9},{2,10},{3,11},{4,12},{5,13},{6,14},{7,15},{8,0},{9,1},... | collective-permute-start | bytes 393224 | tf_op jit(solution)/shard_map/ppermute | solution.py:252
  4.5 0.1 collective-permute-start.2
  4.5 7.0 %pack.1 = bf16[16,4,128,128]{3,2,1,0:T(8,128)(2,1)} custom-call(bf16[128,2048]{1,0:T(8,128)(2,1)} %bitcast.14, bf16[128,2048]{1,0:T(8,128)(2,1)} %bitcast.15, bf16[128,2048]{1,0:T(8,128)(2,1)} %bitcast.16, bf16[128,2048]{1,0:T(8,128)(2,1)} %bitcast.12, bf16[2048,2048]{1,0:T(8,128)(2,1)} %refs_3_.3, bf16[2048,2048]{1,0:T(8,128)(2,1)} %refs_3_.3, ...), custom_call_target="tpu_custom_call" | custom-call | flops 1073741824 | bytes 12582912 | tf_op jit(solution)/shard_map/pack/pallas_call | solution.py:59
  11.5 0.0 collective-permute-done.b_ref
  11.5 0.0 collective-permute-done.1.c_ref
  11.6 0.0 collective-permute-done.2.d_ref
  11.6 6.0 %all-to-all-start = ((bf16[16,4,128,128]{3,2,1,0:T(8,128)(2,1)}), bf16[16,4,128,128]{3,2,1,0:T(8,128)(2,1)S(1)}, u32[]{:S(2)}, u32[]{:S(2)}) async-start(bf16[16,4,128,128]{3,2,1,0:T(8,128)(2,1)} %pack.1), calls=%async_computation | async-start | bytes 4194304 | tf_op jit(solution)/shard_map/all_to_all | solution.py:444
  17.6 28.6 %all-to-all-done.x_ref = bf16[16,4,128,128]{3,2,1,0:T(8,128)(2,1)S(1)} async-done(((bf16[16,4,128,128]{3,2,1,0:T(8,128)(2,1)}), bf16[16,4,128,128]{3,2,1,0:T(8,128)(2,1)S(1)}, u32[]{:S(2)}, u32[]{:S(2)}) %all-to-all-start) | async-done | bytes 2097184 | tf_op jit(solution)/shard_map/all_to_all | solution.py:444
  46.2 0.0 collective-permute-start.3
  46.2 1.6 %collective-permute-start.4 = (bf16[512,512]{1,0:T(8,128)(2,1)S(1)}, bf16[512,512]{1,0:T(8,128)(2,1)S(1)}, u32[]{:S(2)}, u32[]{:S(2)}) collective-permute-start(bf16[512,512]{1,0:T(8,128)(2,1)S(1)} %join_rows.1.refs_0_), channel_id=1, source_target_pairs={{0,6},{1,7},{2,0},{3,1},{4,2},{5,3},{6,4},{7,5},{8,14},{9,15},{10,... | collective-permute-start | bytes 1572872 | tf_op jit(solution)/shard_map/ppermute | solution.py:252
  47.9 0.4 collective-permute-start.5
  48.3 4.7 %attention_forward.1 = (bf16[16,128,128]{2,1,0:T(8,128)(2,1)S(1)}, bf16[16,128,128]{2,1,0:T(8,128)(2,1)S(1)}, f32[8,2048]{1,0:T(8,128)S(1)}) custom-call(bf16[16,4,128,128]{3,2,1,0:T(8,128)(2,1)S(1)} %all-to-all-done.x_ref), custom_call_target="tpu_custom_call" | custom-call | tf_op jit(solution)/shard_map/attention_forward/pallas_call | solution.py:122
  52.9 1.3 %collective-permute-start.6 = (bf16[16,128,128]{2,1,0:T(8,128)(2,1)S(1)}, bf16[16,128,128]{2,1,0:T(8,128)(2,1)S(1)}, u32[]{:S(2)}, u32[]{:S(2)}) collective-permute-start(bf16[16,128,128]{2,1,0:T(8,128)(2,1)S(1)} %get-tuple-element.60.ot_ref.refs_0_), channel_id=1, source_target_pairs={{0,8},{1,9},{2,10},{3,11},{4,12},{5,13},{6,14},{7,15},{8,0},{9,1},... | collective-permute-start | bytes 1572872 | tf_op jit(solution)/shard_map/ppermute | solution.py:252
  54.3 0.0 collective-permute-start.7
  54.3 10.0 %attention_backward.1 = bf16[16,4,128,128]{3,2,1,0:T(8,128)(2,1)} custom-call(bf16[16,4,128,128]{3,2,1,0:T(8,128)(2,1)S(1)} %all-to-all-done.x_ref, bf16[16,128,128]{2,1,0:T(8,128)(2,1)S(1)} %get-tuple-element.59.o_ref, bf16[16,128,128]{2,1,0:T(8,128)(2,1)S(1)} %get-tuple-element.60.ot_ref.refs_0_, f32[8,2048]{1,0:T(8,128)S(1)} %get-tuple-element.61.stat_ref), custom_call_target="tpu_custom_call" | custom-call | tf_op jit(solution)/shard_map/attention_backward/pallas_call | solution.py:180
  64.3 0.0 collective-permute-done.3.refs_1_
  64.3 6.9 %collective-permute-done.4.refs_2_ = bf16[512,512]{1,0:T(8,128)(2,1)S(1)} collective-permute-done((bf16[512,512]{1,0:T(8,128)(2,1)S(1)}, bf16[512,512]{1,0:T(8,128)(2,1)S(1)}, u32[]{:S(2)}, u32[]{:S(2)}) %collective-permute-start.4) | collective-permute-done | bytes 524320 | tf_op jit(solution)/shard_map/ppermute | solution.py:252
  71.2 0.0 collective-permute-done.5.refs_3_
  71.3 0.1 stack.21.refs_4_
  71.4 0.0 collective-permute-done.6.refs_2_
  71.4 0.0 collective-permute-done.7.refs_1_
  71.4 0.1 collective-permute-start.8
  71.5 1.9 %collective-permute-done.8.refs_3_ = bf16[16,128,128]{2,1,0:T(8,128)(2,1)S(1)} collective-permute-done((bf16[16,128,128]{2,1,0:T(8,128)(2,1)S(1)}, bf16[16,128,128]{2,1,0:T(8,128)(2,1)S(1)}, u32[]{:S(2)}, u32[]{:S(2)}) %collective-permute-start.8) | collective-permute-done | bytes 524320 | tf_op jit(solution)/shard_map/ppermute | solution.py:252
  73.4 1.9 %weight_partial.1 = (f32[4,32,512]{2,1,0:T(8,128)S(1)}, bf16[4,32,512]{2,1,0:T(8,128)(2,1)S(1)}, bf16[4,32,512]{2,1,0:T(8,128)(2,1)S(1)}, bf16[4,32,512]{2,1,0:T(8,128)(2,1)S(1)}) custom-call(s32[4]{0:T(128)S(1)} %pad_add_fusion.pos_ref, bf16[16,128,128]{2,1,0:T(8,128)(2,1)S(1)} %get-tuple-element.60.ot_ref.refs_0_, ...), custom_call_target="tpu_custom_call" | custom-call | flops 1073741824 | bytes 5242880 | tf_op jit(solution)/shard_map/weight_partial/pallas_call | solution.py:340
  75.3 5.9 %all-to-all-start.1 = ((bf16[16,4,128,128]{3,2,1,0:T(8,128)(2,1)}), bf16[16,4,128,128]{3,2,1,0:T(8,128)(2,1)S(1)}, u32[]{:S(2)}, u32[]{:S(2)}) async-start(bf16[16,4,128,128]{3,2,1,0:T(8,128)(2,1)} %attention_backward.1), calls=%async_computation.1 | async-start | bytes 4194304 | tf_op jit(solution)/shard_map/all_to_all | solution.py:444
  81.2 3.2 %collective-permute-start.10 = (bf16[4,32,512]{2,1,0:T(8,128)(2,1)S(1)}, bf16[4,32,512]{2,1,0:T(8,128)(2,1)S(1)}, u32[]{:S(2)}, u32[]{:S(2)}) collective-permute-start(bf16[4,32,512]{2,1,0:T(8,128)(2,1)S(1)} %get-tuple-element.77), channel_id=1, source_target_pairs={{0,32},{1,33},{2,34},{3,35},{4,36},{5,37},{6,38},{7,39},{8,40},{9,... | collective-permute-start | bytes 393224 | tf_op jit(solution)/shard_map/ppermute | solution.py:252
  84.4 1.0 collective-permute-start.11
  85.5 1.0 collective-permute-start.9
  86.4 2.5 %collective-permute-done.10.b_ref = bf16[4,32,512]{2,1,0:T(8,128)(2,1)S(1)} collective-permute-done((bf16[4,32,512]{2,1,0:T(8,128)(2,1)S(1)}, bf16[4,32,512]{2,1,0:T(8,128)(2,1)S(1)}, u32[]{:S(2)}, u32[]{:S(2)}) %collective-permute-start.10) | collective-permute-done | bytes 131104 | tf_op jit(solution)/shard_map/ppermute | solution.py:252
  88.9 2.5 %collective-permute-done.11.c_ref = bf16[4,32,512]{2,1,0:T(8,128)(2,1)S(1)} collective-permute-done((bf16[4,32,512]{2,1,0:T(8,128)(2,1)S(1)}, bf16[4,32,512]{2,1,0:T(8,128)(2,1)S(1)}, u32[]{:S(2)}, u32[]{:S(2)}) %collective-permute-start.11) | collective-permute-done | bytes 131104 | tf_op jit(solution)/shard_map/ppermute | solution.py:252
  91.4 0.3 collective-permute-done.9.a_ref
  91.7 0.1 sum_shares.1
  91.7 3.7 %collective-permute-start.12 = (bf16[2,32,512]{2,1,0:T(8,128)(2,1)S(1)}, bf16[2,32,512]{2,1,0:T(8,128)(2,1)S(1)}, u32[]{:S(2)}, u32[]{:S(2)}) collective-permute-start(bf16[2,32,512]{2,1,0:T(8,128)(2,1)S(1)} %get-tuple-element.79.a_ref), channel_id=1, source_target_pairs={{0,64},{1,65},{2,66},{3,67},{4,68},{5,69},{6,70},{7,71},{8,72},{9,... | collective-permute-start | bytes 196616 | tf_op jit(solution)/shard_map/ppermute | solution.py:252
  95.4 0.9 collective-permute-start.13
  96.3 0.0 collective-permute-start.14
  96.3 14.1 %collective-permute-done.12.a2_ref = bf16[2,32,512]{2,1,0:T(8,128)(2,1)S(1)} collective-permute-done((bf16[2,32,512]{2,1,0:T(8,128)(2,1)S(1)}, bf16[2,32,512]{2,1,0:T(8,128)(2,1)S(1)}, u32[]{:S(2)}, u32[]{:S(2)}) %collective-permute-start.12) | collective-permute-done | bytes 65568 | tf_op jit(solution)/shard_map/ppermute | solution.py:252
  110.3 0.0 collective-permute-done.13.b_ref
  110.3 0.0 collective-permute-done.14.b2_ref
  110.4 0.1 collective-permute-start.15
  110.5 1.2 collective-permute-done.15.got_ref
  111.7 0.6 make_rows.1.mine_ref
  112.3 1.6 %collective-permute-start.16 = (bf16[32,2048]{1,0:T(8,128)(2,1)S(1)}, bf16[32,2048]{1,0:T(8,128)(2,1)S(1)}, u32[]{:S(2)}, u32[]{:S(2)}) collective-permute-start(bf16[32,2048]{1,0:T(8,128)(2,1)S(1)} %make_rows.1.mine_ref), channel_id=1, source_target_pairs={{0,16},{1,17},{2,18},{3,19},{4,20},{5,21},{6,22},{7,23},{8,24},{9,... | collective-permute-start | bytes 393224 | tf_op jit(solution)/shard_map/ppermute | solution.py:252
  113.9 2.9 %collective-permute-start.17 = (bf16[32,2048]{1,0:T(8,128)(2,1)S(1)}, bf16[32,2048]{1,0:T(8,128)(2,1)S(1)}, u32[]{:S(2)}, u32[]{:S(2)}) collective-permute-start(bf16[32,2048]{1,0:T(8,128)(2,1)S(1)} %make_rows.1.mine_ref), channel_id=1, source_target_pairs={{0,32},{1,33},{2,34},{3,35},{4,36},{5,37},{6,38},{7,39},{8,40},{9,... | collective-permute-start | bytes 393224 | tf_op jit(solution)/shard_map/ppermute | solution.py:252
  116.8 1.3 %collective-permute-start.18 = (bf16[32,2048]{1,0:T(8,128)(2,1)S(1)}, bf16[32,2048]{1,0:T(8,128)(2,1)S(1)}, u32[]{:S(2)}, u32[]{:S(2)}) collective-permute-start(bf16[32,2048]{1,0:T(8,128)(2,1)S(1)} %make_rows.1.mine_ref), channel_id=1, source_target_pairs={{0,48},{1,49},{2,50},{3,51},{4,52},{5,53},{6,54},{7,55},{8,56},{9,... | collective-permute-start | bytes 393224 | tf_op jit(solution)/shard_map/ppermute | solution.py:252
  118.2 0.0 all-to-all-done.1.x_ref.o_ref
  118.2 0.0 copy-start.1
  118.2 1.4 %copy-done.1 = bf16[16,4,128,128]{3,2,1,0:T(8,128)(2,1)} copy-done((bf16[16,4,128,128]{3,2,1,0:T(8,128)(2,1)}, bf16[16,4,128,128]{3,2,1,0:T(8,128)(2,1)S(1)}, u32[]{:S(2)}) %copy-start.1) | copy-done | bytes 2097176
  119.5 5.6 %finish.1 = (bf16[128,2048]{1,0:T(8,128)(2,1)}, bf16[128,2048]{1,0:T(8,128)(2,1)}, bf16[128,2048]{1,0:T(8,128)(2,1)}, bf16[128,2048]{1,0:T(8,128)(2,1)}) custom-call(bf16[16,4,128,128]{3,2,1,0:T(8,128)(2,1)} %copy-done.1, bf16[16,4,128,128]{3,2,1,0:T(8,128)(2,1)} %copy-done.1, bf16[2048,2048]{1,0:T(8,128)(2,1)} %refs_3_.3, bf16[2048,2048]{1,0:T(8,128)(2,1)} %refs_3_.3, ...), custom_call_target="tpu_custom_call" | custom-call | flops 1073741824 | bytes 12582912 | tf_op jit(solution)/shard_map/finish/pallas_call | solution.py:219
  125.1 0.0 collective-permute-done.16.one_ref
  125.1 0.0 collective-permute-done.17.two_ref
  125.2 0.0 collective-permute-done.18.three_ref
  125.2 1.6 %join_shares.1 = f32[128,2048]{1,0:T(8,128)} custom-call(s32[4]{0:T(128)S(1)} %pad_add_fusion.pos_ref, bf16[32,2048]{1,0:T(8,128)(2,1)S(1)} %make_rows.1.mine_ref, bf16[32,2048]{1,0:T(8,128)(2,1)S(1)} %collective-permute-done.16.one_ref, bf16[32,2048]{1,0:T(8,128)(2,1)S(1)} %collective-permute-done.17.two_ref, ...), custom_call_target="tpu_custom_call" | custom-call | bytes 2097152 | tf_op jit(solution)/shard_map/join_shares/pallas_call | solution.py:423
  (2 shorter events, 0.1 us)
Async XLA Ops:
  0.7 1.0 copy-start
  2.4 9.2 %collective-permute-start = (bf16[128,512]{1,0:T(8,128)(2,1)S(1)}, bf16[128,512]{1,0:T(8,128)(2,1)S(1)}, u32[]{:S(2)}, u32[]{:S(2)}) collective-permute-start(bf16[128,512]{1,0:T(8,128)(2,1)S(1)} %get-tuple-element.49), channel_id=1, source_target_pairs={{0,1},{1,0},{2,3},{3,2},{4,5},{5,4},{6,7},{7,6},{8,9},{9,8},{10,11... | collective-permute-start | bytes 393224 | tf_op jit(solution)/shard_map/ppermute | solution.py:252
  2.5 9.1 %collective-permute-start.1 = (bf16[128,512]{1,0:T(8,128)(2,1)S(1)}, bf16[128,512]{1,0:T(8,128)(2,1)S(1)}, u32[]{:S(2)}, u32[]{:S(2)}) collective-permute-start(bf16[128,512]{1,0:T(8,128)(2,1)S(1)} %get-tuple-element.50), channel_id=1, source_target_pairs={{0,8},{1,9},{2,10},{3,11},{4,12},{5,13},{6,14},{7,15},{8,0},{9,1},... | collective-permute-start | bytes 393224 | tf_op jit(solution)/shard_map/ppermute | solution.py:252
  4.5 7.1 %collective-permute-start.2 = (bf16[128,512]{1,0:T(8,128)(2,1)S(1)}, bf16[128,512]{1,0:T(8,128)(2,1)S(1)}, u32[]{:S(2)}, u32[]{:S(2)}) collective-permute-start(bf16[128,512]{1,0:T(8,128)(2,1)S(1)} %get-tuple-element.51), channel_id=1, source_target_pairs={{0,9},{1,8},{2,11},{3,10},{4,13},{5,12},{6,15},{7,14},{8,1},{9,0},... | collective-permute-start | bytes 393224 | tf_op jit(solution)/shard_map/ppermute | solution.py:252
  11.6 34.7 %all-to-all-start = ((bf16[16,4,128,128]{3,2,1,0:T(8,128)(2,1)}), bf16[16,4,128,128]{3,2,1,0:T(8,128)(2,1)S(1)}, u32[]{:S(2)}, u32[]{:S(2)}) async-start(bf16[16,4,128,128]{3,2,1,0:T(8,128)(2,1)} %pack.1), calls=%async_computation | async-start | bytes 4194304 | tf_op jit(solution)/shard_map/all_to_all | solution.py:444
  46.2 18.1 %collective-permute-start.3 = (bf16[512,512]{1,0:T(8,128)(2,1)S(1)}, bf16[512,512]{1,0:T(8,128)(2,1)S(1)}, u32[]{:S(2)}, u32[]{:S(2)}) collective-permute-start(bf16[512,512]{1,0:T(8,128)(2,1)S(1)} %join_rows.1.refs_0_), channel_id=1, source_target_pairs={{0,4},{1,5},{2,6},{3,7},{4,0},{5,1},{6,2},{7,3},{8,12},{9,13},{10,... | collective-permute-start | bytes 1572872 | tf_op jit(solution)/shard_map/ppermute | solution.py:252
  46.2 25.0 %collective-permute-start.4 = (bf16[512,512]{1,0:T(8,128)(2,1)S(1)}, bf16[512,512]{1,0:T(8,128)(2,1)S(1)}, u32[]{:S(2)}, u32[]{:S(2)}) collective-permute-start(bf16[512,512]{1,0:T(8,128)(2,1)S(1)} %join_rows.1.refs_0_), channel_id=1, source_target_pairs={{0,6},{1,7},{2,0},{3,1},{4,2},{5,3},{6,4},{7,5},{8,14},{9,15},{10,... | collective-permute-start | bytes 1572872 | tf_op jit(solution)/shard_map/ppermute | solution.py:252
  47.9 23.4 %collective-permute-start.5 = (bf16[512,512]{1,0:T(8,128)(2,1)S(1)}, bf16[512,512]{1,0:T(8,128)(2,1)S(1)}, u32[]{:S(2)}, u32[]{:S(2)}) collective-permute-start(bf16[512,512]{1,0:T(8,128)(2,1)S(1)} %join_rows.1.refs_0_), channel_id=1, source_target_pairs={{0,2},{1,3},{2,4},{3,5},{4,6},{5,7},{6,0},{7,1},{8,10},{9,11},{10,... | collective-permute-start | bytes 1572872 | tf_op jit(solution)/shard_map/ppermute | solution.py:252
  52.9 18.5 %collective-permute-start.6 = (bf16[16,128,128]{2,1,0:T(8,128)(2,1)S(1)}, bf16[16,128,128]{2,1,0:T(8,128)(2,1)S(1)}, u32[]{:S(2)}, u32[]{:S(2)}) collective-permute-start(bf16[16,128,128]{2,1,0:T(8,128)(2,1)S(1)} %get-tuple-element.60.ot_ref.refs_0_), channel_id=1, source_target_pairs={{0,8},{1,9},{2,10},{3,11},{4,12},{5,13},{6,14},{7,15},{8,0},{9,1},... | collective-permute-start | bytes 1572872 | tf_op jit(solution)/shard_map/ppermute | solution.py:252
  54.3 17.1 %collective-permute-start.7 = (bf16[16,128,128]{2,1,0:T(8,128)(2,1)S(1)}, bf16[16,128,128]{2,1,0:T(8,128)(2,1)S(1)}, u32[]{:S(2)}, u32[]{:S(2)}) collective-permute-start(bf16[16,128,128]{2,1,0:T(8,128)(2,1)S(1)} %get-tuple-element.60.ot_ref.refs_0_), channel_id=1, source_target_pairs={{0,1},{1,0},{2,3},{3,2},{4,5},{5,4},{6,7},{7,6},{8,9},{9,8},{10,11... | collective-permute-start | bytes 1572872 | tf_op jit(solution)/shard_map/ppermute | solution.py:252
  71.4 2.0 %collective-permute-start.8 = (bf16[16,128,128]{2,1,0:T(8,128)(2,1)S(1)}, bf16[16,128,128]{2,1,0:T(8,128)(2,1)S(1)}, u32[]{:S(2)}, u32[]{:S(2)}) collective-permute-start(bf16[16,128,128]{2,1,0:T(8,128)(2,1)S(1)} %collective-permute-done.6.refs_2_), channel_id=1, source_target_pairs={{0,1},{1,0},{2,3},{3,2},{4,5},{5,4},{6,7},{7,6},{8,9},{9,8},{10,11... | collective-permute-start | bytes 1572872 | tf_op jit(solution)/shard_map/ppermute | solution.py:252
  75.3 42.8 %all-to-all-start.1 = ((bf16[16,4,128,128]{3,2,1,0:T(8,128)(2,1)}), bf16[16,4,128,128]{3,2,1,0:T(8,128)(2,1)S(1)}, u32[]{:S(2)}, u32[]{:S(2)}) async-start(bf16[16,4,128,128]{3,2,1,0:T(8,128)(2,1)} %attention_backward.1), calls=%async_computation.1 | async-start | bytes 4194304 | tf_op jit(solution)/shard_map/all_to_all | solution.py:444
  81.2 7.7 %collective-permute-start.10 = (bf16[4,32,512]{2,1,0:T(8,128)(2,1)S(1)}, bf16[4,32,512]{2,1,0:T(8,128)(2,1)S(1)}, u32[]{:S(2)}, u32[]{:S(2)}) collective-permute-start(bf16[4,32,512]{2,1,0:T(8,128)(2,1)S(1)} %get-tuple-element.77), channel_id=1, source_target_pairs={{0,32},{1,33},{2,34},{3,35},{4,36},{5,37},{6,38},{7,39},{8,40},{9,... | collective-permute-start | bytes 393224 | tf_op jit(solution)/shard_map/ppermute | solution.py:252
  84.4 7.0 %collective-permute-start.11 = (bf16[4,32,512]{2,1,0:T(8,128)(2,1)S(1)}, bf16[4,32,512]{2,1,0:T(8,128)(2,1)S(1)}, u32[]{:S(2)}, u32[]{:S(2)}) collective-permute-start(bf16[4,32,512]{2,1,0:T(8,128)(2,1)S(1)} %get-tuple-element.78), channel_id=1, source_target_pairs={{0,48},{1,49},{2,50},{3,51},{4,52},{5,53},{6,54},{7,55},{8,56},{9,... | collective-permute-start | bytes 393224 | tf_op jit(solution)/shard_map/ppermute | solution.py:252
  85.5 6.2 %collective-permute-start.9 = (bf16[4,32,512]{2,1,0:T(8,128)(2,1)S(1)}, bf16[4,32,512]{2,1,0:T(8,128)(2,1)S(1)}, u32[]{:S(2)}, u32[]{:S(2)}) collective-permute-start(bf16[4,32,512]{2,1,0:T(8,128)(2,1)S(1)} %get-tuple-element.76), channel_id=1, source_target_pairs={{0,16},{1,17},{2,18},{3,19},{4,20},{5,21},{6,22},{7,23},{8,24},{9,... | collective-permute-start | bytes 393224 | tf_op jit(solution)/shard_map/ppermute | solution.py:252
  91.7 18.6 %collective-permute-start.12 = (bf16[2,32,512]{2,1,0:T(8,128)(2,1)S(1)}, bf16[2,32,512]{2,1,0:T(8,128)(2,1)S(1)}, u32[]{:S(2)}, u32[]{:S(2)}) collective-permute-start(bf16[2,32,512]{2,1,0:T(8,128)(2,1)S(1)} %get-tuple-element.79.a_ref), channel_id=1, source_target_pairs={{0,64},{1,65},{2,66},{3,67},{4,68},{5,69},{6,70},{7,71},{8,72},{9,... | collective-permute-start | bytes 196616 | tf_op jit(solution)/shard_map/ppermute | solution.py:252
  95.4 14.9 %collective-permute-start.13 = (bf16[2,32,512]{2,1,0:T(8,128)(2,1)S(1)}, bf16[2,32,512]{2,1,0:T(8,128)(2,1)S(1)}, u32[]{:S(2)}, u32[]{:S(2)}) collective-permute-start(bf16[2,32,512]{2,1,0:T(8,128)(2,1)S(1)} %get-tuple-element.80), channel_id=1, source_target_pairs={{0,8},{1,9},{2,10},{3,11},{4,12},{5,13},{6,14},{7,15},{8,0},{9,1},... | collective-permute-start | bytes 196616 | tf_op jit(solution)/shard_map/ppermute | solution.py:252
  96.3 14.1 %collective-permute-start.14 = (bf16[2,32,512]{2,1,0:T(8,128)(2,1)S(1)}, bf16[2,32,512]{2,1,0:T(8,128)(2,1)S(1)}, u32[]{:S(2)}, u32[]{:S(2)}) collective-permute-start(bf16[2,32,512]{2,1,0:T(8,128)(2,1)S(1)} %get-tuple-element.80), channel_id=1, source_target_pairs={{0,72},{1,73},{2,74},{3,75},{4,76},{5,77},{6,78},{7,79},{8,64},{9,... | collective-permute-start | bytes 196616 | tf_op jit(solution)/shard_map/ppermute | solution.py:252
  110.4 1.3 %collective-permute-start.15 = (bf16[2,32,512]{2,1,0:T(8,128)(2,1)S(1)}, bf16[2,32,512]{2,1,0:T(8,128)(2,1)S(1)}, u32[]{:S(2)}, u32[]{:S(2)}) collective-permute-start(bf16[2,32,512]{2,1,0:T(8,128)(2,1)S(1)} %get-tuple-element.82), channel_id=1, source_target_pairs={{0,1},{1,0},{2,3},{3,2},{4,5},{5,4},{6,7},{7,6},{8,9},{9,8},{10,11... | collective-permute-start | bytes 196616 | tf_op jit(solution)/shard_map/ppermute | solution.py:252
  112.3 12.9 %collective-permute-start.16 = (bf16[32,2048]{1,0:T(8,128)(2,1)S(1)}, bf16[32,2048]{1,0:T(8,128)(2,1)S(1)}, u32[]{:S(2)}, u32[]{:S(2)}) collective-permute-start(bf16[32,2048]{1,0:T(8,128)(2,1)S(1)} %make_rows.1.mine_ref), channel_id=1, source_target_pairs={{0,16},{1,17},{2,18},{3,19},{4,20},{5,21},{6,22},{7,23},{8,24},{9,... | collective-permute-start | bytes 393224 | tf_op jit(solution)/shard_map/ppermute | solution.py:252
  113.9 11.2 %collective-permute-start.17 = (bf16[32,2048]{1,0:T(8,128)(2,1)S(1)}, bf16[32,2048]{1,0:T(8,128)(2,1)S(1)}, u32[]{:S(2)}, u32[]{:S(2)}) collective-permute-start(bf16[32,2048]{1,0:T(8,128)(2,1)S(1)} %make_rows.1.mine_ref), channel_id=1, source_target_pairs={{0,32},{1,33},{2,34},{3,35},{4,36},{5,37},{6,38},{7,39},{8,40},{9,... | collective-permute-start | bytes 393224 | tf_op jit(solution)/shard_map/ppermute | solution.py:252
  116.8 8.3 %collective-permute-start.18 = (bf16[32,2048]{1,0:T(8,128)(2,1)S(1)}, bf16[32,2048]{1,0:T(8,128)(2,1)S(1)}, u32[]{:S(2)}, u32[]{:S(2)}) collective-permute-start(bf16[32,2048]{1,0:T(8,128)(2,1)S(1)} %make_rows.1.mine_ref), channel_id=1, source_target_pairs={{0,48},{1,49},{2,50},{3,51},{4,52},{5,53},{6,54},{7,55},{8,56},{9,... | collective-permute-start | bytes 393224 | tf_op jit(solution)/shard_map/ppermute | solution.py:252
  118.2 1.4 %copy-start.1 = (bf16[16,4,128,128]{3,2,1,0:T(8,128)(2,1)}, bf16[16,4,128,128]{3,2,1,0:T(8,128)(2,1)S(1)}, u32[]{:S(2)}) copy-start(bf16[16,4,128,128]{3,2,1,0:T(8,128)(2,1)S(1)} %all-to-all-done.1.x_ref.o_ref) | copy-start | bytes 6291460
